TPU v7x, 128 devices: a whole 4x4x4 slice. The times are simulated.
128 devices in a mesh: wide: 16 (over x, y), narrow: 8 (over z, core).
Axes of the slice: x: 4, y: 4, z: 4, core: 2. Of those that a mesh axis runs over, the one named last changes fastest.
Arguments:
- incident: bfloat16 [2, 4, 6, 262144], P(None, None, None, ('wide', 'narrow')), may hold values from -6 to 6
- jitter: bfloat16 [2, 262144], P(None, ('wide', 'narrow')), may hold values from -0.079589844 to 0.079589844
- weights: float32 [262144], P(('wide', 'narrow')), may hold values from 0.3 to 3
- cells: int32 [262144], P(('wide', 'narrow')), may hold values from 0 to 8191
- pair_list: int32 [128, 8, 3], P(('wide', 'narrow')), may hold values from 0 to 15, as said below
- pair_count: int32 [128], P(('wide', 'narrow')), may hold values from 1 to 8, as said below
- kernel: float32 [2, 1024, 1024], P(None, None, ('wide', 'narrow')), may hold values from -6 to 6
Outputs:
- coupled: float32 [2, 4, 6, 262144], P(None, None, None, ('wide', 'narrow'))
Inputs may be any that keep to these rules, and one draw needn't show every extreme that they name: `pair_list`: each row names a direction t, an own cluster and a partner cluster, both below 16; the partner device exists on the tile grid, and for t = 0 the two clusters differ. The partner cluster b lies on the partner's side facing the own device: b % 4 == 0 for t = 1, b < 4 for t = 2, b = 3 for t = 3, b = 15 for t = 4. All slots hold such rows. `pair_count`: some device uses all 8 slots. Pillar p of device d lies in grid row d * 8 + cells[p] // 1024 and column cells[p] % 1024.
All inputs are finite; a program needn't handle non-finite values.
Results may differ from a plain program's by a relative error of at most 0.0025.
Values may be sent and summed in bfloat16 or wider, within the bound.
No kernel may reach another device: no remote copies, remote signals or barrier semaphores. Data moves between devices by JAX's collectives and lax.ppermute only.
A program may use at most 128 MiB of HBM per device.

v0:
```python
import math

import jax
import jax.numpy as jnp
import numpy as np
from jax import lax
from jax.sharding import PartitionSpec as P

ANG = 4
PCX = 8
PCY = 16
CCX = 4
CCY = 4
CBX = 8
GY = 1024
PIL = 128


WAVE = 2.0 * math.pi
PITCH = 0.4
STEP_WIDE = (0, 0, 1, 1, -1)
STEP_NARROW = (0, 1, 0, -1, -1)


def padded_2(block, sides, width):
    for axis, dim in sides:
        count = lax.axis_size(axis)
        forward = [(i, i + 1) for i in range(count - 1)]
        backward = [(target, source) for source, target in forward]
        low = lax.ppermute(
            lax.slice_in_dim(block, block.shape[dim] - width, None, axis=dim), axis, forward
        )
        high = lax.ppermute(lax.slice_in_dim(block, 0, width, axis=dim), axis, backward)
        block = jnp.concatenate([low, block, high], axis=dim)
    return block


def coupling_table():
    table = np.zeros((6, 6, 6), np.float32)
    for member in range(6):
        table[0, member, member] = 1.0
    for offset in (0, 3):
        table[1, offset, offset] = 1.0
        table[2, offset, offset + 1] = 1.0
        table[2, offset + 1, offset] = 1.0
        table[3, offset + 1, offset + 1] = 1.0
    table[4, 2, 4] = 1.0
    table[4, 4, 2] = 1.0
    table[4, 1, 5] = -1.0
    table[4, 5, 1] = -1.0
    table[5, 0, 5] = 1.0
    table[5, 5, 0] = 1.0
    table[5, 2, 3] = -1.0
    table[5, 3, 2] = -1.0
    return table


def lattice(wide_pos, narrow_pos, cluster, offsets):
    local_ids = jnp.arange(PIL, dtype=jnp.int32)
    across = ((wide_pos * CCX + cluster // CCY) * PCX + local_ids // PCY).astype(jnp.float32)
    along = ((narrow_pos * CCY + cluster % CCY) * PCY + local_ids % PCY).astype(jnp.float32)
    return (across * PITCH + offsets[0], along * PITCH + offsets[1])


def near_fields(delta_x, delta_y):
    distance = jnp.sqrt(delta_x * delta_x + delta_y * delta_y)
    phase = WAVE * distance
    inverse = 1.0 / phase
    unit_x = delta_x / distance
    unit_y = delta_y / distance
    green_re = jnp.cos(phase) * inverse
    green_im = jnp.sin(phase) * inverse

    def times_green(first, second):
        return (green_re * first - green_im * second, green_re * second + green_im * first)

    term_a = times_green(1.0 - inverse * inverse, inverse)
    term_b = times_green(3.0 * inverse * inverse - 1.0, -3.0 * inverse)
    term_c = times_green(jnp.ones_like(inverse), inverse)

    def stacked(part):
        return jnp.stack(
            [
                term_a[part],
                term_b[part] * unit_x * unit_x,
                term_b[part] * unit_x * unit_y,
                term_b[part] * unit_y * unit_y,
                term_c[part] * unit_x,
                term_c[part] * unit_y,
            ]
        )

    return (stacked(0).astype(jnp.bfloat16), stacked(1).astype(jnp.bfloat16))


def mix_parts(prod_re, prod_im):
    shaped_re = prod_re.reshape(6, 2, ANG, 6, -1)
    shaped_im = prod_im.reshape(6, 2, ANG, 6, -1)
    real_part = shaped_re[:, 0] - shaped_im[:, 1]
    imag_part = shaped_re[:, 1] + shaped_im[:, 0]
    return jnp.stack([real_part, imag_part], 1)


def couple(field_re, field_im, left, right):
    coupling = jnp.asarray(coupling_table(), dtype=jnp.float32)
    high = lax.Precision.HIGHEST
    forward = mix_parts(
        jnp.einsum("fpq,cq->fcp", field_re, right, preferred_element_type=jnp.float32),
        jnp.einsum("fpq,cq->fcp", field_im, right, preferred_element_type=jnp.float32),
    )
    to_left = jnp.einsum("fab,frgbp->rgap", coupling, forward, precision=high).reshape(-1, PIL)
    backward = mix_parts(
        jnp.einsum("fpq,cp->fcq", field_re, left, preferred_element_type=jnp.float32),
        jnp.einsum("fpq,cp->fcq", field_im, left, preferred_element_type=jnp.float32),
    )
    to_right = jnp.einsum("fab,frgaq->rgbq", coupling, backward, precision=high).reshape(-1, PIL)
    return (to_left, to_right)


def twiddle(count):
    index_row = jnp.arange(count, dtype=jnp.int32)
    product = index_row[:, None] * index_row[None, :] % count
    angles = product.astype(jnp.float32) * (2.0 * math.pi / count)
    return (jnp.cos(angles), jnp.sin(angles))


def apply_table(real_part, imag_part, cosine, sine_tab, form, inverse):

    def transform(matrix, vector):
        return jnp.einsum(form, vector, matrix, precision=lax.Precision.HIGHEST)

    if inverse:
        return (
            transform(cosine, real_part) - transform(sine_tab, imag_part),
            transform(cosine, imag_part) + transform(sine_tab, real_part),
        )
    return (
        transform(cosine, real_part) + transform(sine_tab, imag_part),
        transform(cosine, imag_part) - transform(sine_tab, real_part),
    )


def complex_dft(real_part, imag_part, axis, inverse):
    length = real_part.shape[axis]
    outer = math.gcd(length, 32)
    inner = length // outer
    real_part = jnp.moveaxis(real_part, axis, -1)
    imag_part = jnp.moveaxis(imag_part, axis, -1)
    leading = real_part.shape[:-1]
    real_part = real_part.reshape(leading + (inner, outer))
    imag_part = imag_part.reshape(leading + (inner, outer))
    cos_inner, sin_inner = twiddle(inner)
    real_part, imag_part = apply_table(
        real_part, imag_part, cos_inner, sin_inner, "...jn,jk->...kn", inverse
    )
    first_ids = jnp.arange(inner, dtype=jnp.int32)[:, None]
    second_ids = jnp.arange(outer, dtype=jnp.int32)[None, :]
    angles = (first_ids * second_ids % length).astype(jnp.float32) * (2.0 * math.pi / length)
    cos_mid = jnp.cos(angles)
    sin_mid = jnp.sin(angles)
    if inverse:
        real_part, imag_part = (
            real_part * cos_mid - imag_part * sin_mid,
            imag_part * cos_mid + real_part * sin_mid,
        )
    else:
        real_part, imag_part = (
            real_part * cos_mid + imag_part * sin_mid,
            imag_part * cos_mid - real_part * sin_mid,
        )
    cos_outer, sin_outer = twiddle(outer)
    real_part, imag_part = apply_table(
        real_part, imag_part, cos_outer, sin_outer, "...kn,nm->...km", inverse
    )
    real_part = jnp.swapaxes(real_part, -1, -2).reshape(leading + (length,))
    imag_part = jnp.swapaxes(imag_part, -1, -2).reshape(leading + (length,))
    return (jnp.moveaxis(real_part, -1, axis), jnp.moveaxis(imag_part, -1, axis))


def transform_axis(values, axis, inverse):
    half_chan = values.shape[1] // 2
    new_re, new_im = complex_dft(values[:, :half_chan], values[:, half_chan:], axis, inverse)
    return jnp.concatenate([new_re, new_im], axis=1)


def local(incident, jitter, weights, cells, pair_list, pair_count, kernel):
    channels = 12 * ANG
    width_dev = incident.shape[3]
    own_rows = incident.reshape(channels, width_dev)
    packed = jnp.concatenate([own_rows, jitter], axis=0)
    beside_all = padded_2(packed[None, None], (("wide", 0), ("narrow", 1)), 1)
    beside_all = beside_all.reshape(9, channels + 2, width_dev)
    wide_pos = lax.axis_index("wide")
    narrow_pos = lax.axis_index("narrow")
    step_wide = jnp.array(STEP_WIDE, dtype=jnp.int32)
    step_narrow = jnp.array(STEP_NARROW, dtype=jnp.int32)
    used_slots = pair_count[0]

    def one_slot(slot_idx, carry):
        near_sum, returns = carry
        pair_row = pair_list[0, slot_idx]
        direction = pair_row[0]
        own_cluster = pair_row[1]
        far_cluster = pair_row[2]
        move_wide = step_wide[direction]
        move_narrow = step_narrow[direction]
        slot_cell = (1 + move_wide) * 3 + 1 + move_narrow
        partner = lax.dynamic_index_in_dim(beside_all, slot_cell, 0, keepdims=False)
        own_piece = lax.dynamic_slice_in_dim(packed, own_cluster * PIL, PIL, 1)
        far_piece = lax.dynamic_slice_in_dim(partner, far_cluster * PIL, PIL, 1)
        own_x, own_y = lattice(
            wide_pos, narrow_pos, own_cluster, own_piece[channels:].astype(jnp.float32)
        )
        far_x, far_y = lattice(
            wide_pos + move_wide,
            narrow_pos + move_narrow,
            far_cluster,
            far_piece[channels:].astype(jnp.float32),
        )
        field_re, field_im = near_fields(
            own_x[:, None] - far_x[None, :], own_y[:, None] - far_y[None, :]
        )
        to_left, to_right = couple(field_re, field_im, own_piece[:channels], far_piece[:channels])
        active = (slot_idx < used_slots).astype(jnp.float32)
        current = lax.dynamic_slice_in_dim(near_sum, own_cluster * PIL, PIL, 1)
        near_sum = lax.dynamic_update_slice_in_dim(
            near_sum, current + active * to_left, own_cluster * PIL, 1
        )
        starts = (slot_cell, jnp.int32(0), far_cluster * PIL)
        previous = lax.dynamic_slice(returns, starts, (1, channels, PIL))
        returns = lax.dynamic_update_slice(returns, previous + active * to_right[None], starts)
        return (near_sum, returns)

    near_sum = jnp.zeros((channels, width_dev), dtype=jnp.float32)
    returns = jnp.zeros((9, channels, width_dev), dtype=jnp.float32)
    near_sum, returns = lax.fori_loop(0, pair_list.shape[1], one_slot, (near_sum, returns))
    padded = padded_2(
        returns.reshape(3, 3, channels, width_dev).astype(jnp.bfloat16),
        (("wide", 0), ("narrow", 1)),
        1,
    ).astype(jnp.float32)
    near_sum = near_sum + padded[2, 2] + padded[2, 0] + padded[0, 2] + padded[0, 4] + padded[4, 4]
    scaled = own_rows.astype(jnp.float32) * weights[None, :]
    grid = jax.ops.segment_sum(scaled.T, cells, num_segments=CBX * GY)
    grid = grid.reshape(CBX, GY, channels).transpose(0, 2, 1)
    spectrum = transform_axis(grid, 2, False)
    columns_form = lax.all_to_all(
        spectrum, ("wide", "narrow"), split_axis=2, concat_axis=0, tiled=True
    )
    rows_all = columns_form.shape[0]
    spectrum = transform_axis(columns_form, 0, False)
    half_chan = channels // 2
    kernel_re = kernel[0][:, None, :]
    kernel_im = kernel[1][:, None, :]
    spec_re = spectrum[:, :half_chan]
    spec_im = spectrum[:, half_chan:]
    weighted = jnp.concatenate(
        [spec_re * kernel_re - spec_im * kernel_im, spec_re * kernel_im + spec_im * kernel_re],
        axis=1,
    )
    weighted = transform_axis(weighted, 0, True)
    rows_form = lax.all_to_all(
        weighted, ("wide", "narrow"), split_axis=0, concat_axis=2, tiled=True
    )
    far_grid = transform_axis(rows_form, 2, True) * (1.0 / (rows_all * GY))
    far_flat = far_grid.transpose(1, 0, 2).reshape(channels, CBX * GY)
    sampled = jnp.take(far_flat, cells, axis=1) * weights[None, :]
    return (near_sum + sampled).reshape(2, ANG, 6, width_dev)


def solution(mesh):
    in_specs = (
        P(None, None, None, ("wide", "narrow")),
        P(None, ("wide", "narrow")),
        P(("wide", "narrow")),
        P(("wide", "narrow")),
        P(("wide", "narrow"), None, None),
        P(("wide", "narrow")),
        P(None, None, ("wide", "narrow")),
    )
    out_specs = P(None, None, None, ("wide", "narrow"))
    return jax.shard_map(local, mesh=mesh, in_specs=in_specs, out_specs=out_specs, check_vma=False)
```

profile of v0, /device:TPU:1, one launch (start us, length us, event | category | flops | bytes accessed | tf_op | source)
XLA Modules:
  0.0 638.6 jit_solution(5326267404136427946)
XLA Ops:
  3.1 4.7 collective-permute-start
  10.3 13.7 %scatter_custom_fusion = f32[8192,48]{1,0:T(8,128)} fusion(s32[2048]{0:T(1024)S(1)} %copy-done.20, f32[2048,48]{1,0:T(8,128)S(1)} %copy.168, f32[]{:T(128)} %constant.417.clone.1), kind=kCustom, calls=%fused_computation.166 | custom fusion | flops 98304 | bytes 1572868 | tf_op jit(solution)/shard_map/scatter-add | solution.py:244
  30.1 4.5 fusion.163
  34.6 3.5 reshape.1726
  38.1 5.0 fusion.161
  52.1 3.3 add_bitcast_fusion.2
  60.4 4.4 collective-permute-start.2
  66.7 4.6 subtract_bitcast_fusion.2
  73.8 3.8 reshape.1727
  85.9 6.3 reshape.1791
  92.1 11.2 %all-to-all-start = ((f32[128,1,3072]{2,1,0:T(1,128)}), f32[128,1,3072]{2,1,0:T(1,128)S(1)}, u32[]{:S(2)}, u32[]{:S(2)}) async-start(f32[128,1,3072]{2,1,0:T(1,128)} %reshape.1791), calls=%async_computation | async-start | bytes 3145728 | tf_op jit(solution)/shard_map/all_to_all | solution.py:247
  109.2 197.9 %while.19 = (s32[]{:T(128)}, f32[48,2048]{1,0:T(8,128)S(1)}, f32[9,48,2048]{2,1,0:T(8,128)}, s32[1,8,3]{1,0,2:T(1,128)S(1)}, s32[]{:T(128)}, /*index=5*/bf16[9,5...) while((s32[]{:T(128)}, f32[48,2048]{1,0:T(8,128)S(1)}, ...), condition=%wide.region_1.2_spmd.clone, body=%wide.region_0.1_spmd.sunk.clone.sunk | while | flops 46167624 | bytes 4501377 | solution.py:236
  311.8 4.4 collective-permute-start.4
  318.0 6.0 reduce
  324.0 4.9 reshape.1792
  332.1 4.7 fusion.343
  336.7 4.8 copy.246
  341.5 4.5 fusion.151
  346.0 6.0 copy.244
  352.0 5.0 fusion.165
  375.1 15.0 %fusion.122 = f32[32,24,8,32]{3,0,2,1:T(8,128)S(1)} fusion(f32[24,8,32,32]{3,2,1,0:T(8,128)S(1)} %fusion.104, f32[24,8,32,32]{3,2,1,0:T(8,128)S(1)} %fusion.101, f32[8,32,32]{1,2,0:T(8,128)S(1)} %copy.186, f32[8,32,32]{1,2,0:T(8,128)S(1)} %copy.185), kind=kOutput, calls=%fused_computation.197 | convolution fusion | flops 76101632 | bytes 2424832 | tf_op jit(solution)/shard_map/...jn,jk->...kn/dot_general | solution.py:130
  390.1 14.8 %fusion.126 = f32[32,24,8,32]{3,0,2,1:T(8,128)S(1)} fusion(f32[24,8,32,32]{3,2,1,0:T(8,128)S(1)} %fusion.104, f32[24,8,32,32]{3,2,1,0:T(8,128)S(1)} %fusion.101, f32[8,32,32]{1,2,0:T(8,128)S(1)} %copy.186, f32[8,32,32]{1,2,0:T(8,128)S(1)} %copy.185), kind=kOutput, calls=%fused_computation.198 | convolution fusion | flops 76101632 | bytes 2424832 | tf_op jit(solution)/shard_map/...jn,jk->...kn/dot_general | solution.py:130
  404.9 14.7 %convolution_add_fusion.1 = f32[32,24,8,32]{3,0,2,1:T(8,128)S(1)} fusion(f32[32,24,8,32]{3,0,2,1:T(8,128)S(1)} %fusion.122, f32[24,8,32,32]{3,2,1,0:T(8,128)S(1)} %fusion.104, f32[24,8,32,32]{3,2,1,0:T(8,128)S(1)} %fusion.101, f32[8,32,32]{1,2,0:T(8,128)S(1)} %copy.186, f32[8,32,32]{1,2,0:T(8,128)S(1)} %copy.185), kind=kOutput, calls=%fused_computation.173 | convolution fusion | flops 76298240 | bytes 3211264 | tf_op jit(solution)/shard_map/...jn,jk->...kn/dot_general | solution.py:130
  419.6 14.9 %convolution_subtract_fusion.1 = f32[32,24,8,32]{3,0,2,1:T(8,128)S(1)} fusion(f32[32,24,8,32]{3,0,2,1:T(8,128)S(1)} %fusion.126, f32[24,8,32,32]{3,2,1,0:T(8,128)S(1)} %fusion.104, f32[24,8,32,32]{3,2,1,0:T(8,128)S(1)} %fusion.101, f32[8,32,32]{1,2,0:T(8,128)S(1)} %copy.186, f32[8,32,32]{1,2,0:T(8,128)S(1)} %copy.185), kind=kOutput, calls=%fused_computation.174 | convolution fusion | flops 76298240 | bytes 3211264 | tf_op jit(solution)/shard_map/...jn,jk->...kn/dot_general | solution.py:130
  437.6 4.6 fusion.69
  442.2 5.0 subtract_bitcast_fusion.1
  447.2 3.6 copy.195
  450.8 3.7 reshape.1731
  454.5 6.2 add_bitcast_fusion.1
  469.9 6.4 reshape.1793
  476.3 10.1 %all-to-all-start.1 = ((f32[128,1,3072]{2,1,0:T(1,128)}), f32[128,1,3072]{2,1,0:T(1,128)S(1)}, u32[]{:S(2)}, u32[]{:S(2)}) async-start(f32[128,1,3072]{2,1,0:T(1,128)} %reshape.1793), calls=%async_computation.1 | async-start | bytes 3145728 | tf_op jit(solution)/shard_map/all_to_all | solution.py:262
  489.2 3.7 collective-permute-start.6
  497.2 18.5 %collective-permute-done.6 = bf16[5,1,48,2048]{3,2,1,0:T(8,128)(2,1)} collective-permute-done((bf16[5,1,48,2048]{3,2,1,0:T(8,128)(2,1)}, bf16[5,1,48,2048]{3,2,1,0:T(8,128)(2,1)}, u32[]{:S(2)}, u32[]{:S(2)}) %collective-permute-start.6) | collective-permute-done | bytes 983072 | tf_op jit(solution)/shard_map/ppermute | solution.py:30
  516.8 5.1 pad_maximum_fusion
  521.9 13.7 %copy.166 = bf16[5,5,48,2048]{2,3,1,0:T(8,128)(2,1)} copy(bf16[5,5,48,2048]{3,2,1,0:T(8,128)(2,1)} %pad_maximum_fusion) | data formatting | bytes 9830400 | tf_op jit(solution)/shard_map/concatenate | solution.py:34
  535.5 14.2 %convert_element_type.247 = f32[5,5,48,2048]{2,3,1,0:T(8,128)} convert(bf16[5,5,48,2048]{2,3,1,0:T(8,128)(2,1)} %copy.166) | non-fusion elementwise | flops 2457600 | bytes 14745600 | tf_op jit(solution)/shard_map/convert_element_type | solution.py:241
  549.8 4.4 reduce.1
  559.8 4.6 fusion.342
  564.4 4.7 copy.254
  569.1 4.6 fusion.148
  573.7 4.9 copy.252
  583.2 5.1 convolution_add_fusion
  594.5 4.8 fusion.61
  599.3 4.5 subtract_bitcast_fusion
  603.8 3.5 copy.205
  607.3 3.7 reshape.1735
  611.0 6.1 add_bitcast_fusion
  626.1 7.7 %gather_fusion = f32[2048,48]{1,0:T(8,128)S(1)} fusion(f32[48,8192]{0,1:T(8,128)} %bitcast.422, s32[2048]{0:T(1024)S(1)} %fusion.213), kind=kCustom, calls=%fused_computation | custom fusion | bytes 794624 | tf_op jit(solution)/shard_map/jit(_take)/gather | solution.py:267
  (377 shorter events, 225.6 us)
Async XLA Ops:
  0.0 10.3 %copy-start.20 = (s32[2048]{0:T(1024)S(1)}, s32[2048]{0:T(1024)}, u32[]{:S(2)}) copy-start(s32[2048]{0:T(1024)} %param.15) | copy-start | bytes 24580
  3.1 55.1 %collective-permute-start = (bf16[1,1,50,2048]{3,2,1,0:T(8,128)(2,1)}, bf16[1,1,50,2048]{3,2,1,0:T(8,128)(2,1)}, u32[]{:S(2)}, u32[]{:S(2)}) collective-permute-start(bf16[1,1,50,2048]{3,2,1,0:T(8,128)(2,1)} %bitcast.1), channel_id=1, source_target_pairs={{0,8},{8,16},{16,24},{24,32},{32,40},{40,48},{48,56},{56,64},{64,7... | collective-permute-start | bytes 614408 | tf_op jit(solution)/shard_map/ppermute | solution.py:30
  7.9 50.4 %collective-permute-start.1 = (bf16[1,1,50,2048]{3,2,1,0:T(8,128)(2,1)}, bf16[1,1,50,2048]{3,2,1,0:T(8,128)(2,1)}, u32[]{:S(2)}, u32[]{:S(2)}) collective-permute-start(bf16[1,1,50,2048]{3,2,1,0:T(8,128)(2,1)} %bitcast.1), channel_id=1, source_target_pairs={{8,0},{16,8},{24,16},{32,24},{40,32},{48,40},{56,48},{64,56},{72,6... | collective-permute-start | bytes 614408 | tf_op jit(solution)/shard_map/ppermute | solution.py:33
  38.1 5.0 copy-start.6
  38.1 5.0 copy-start.10
  60.4 43.4 %collective-permute-start.2 = (bf16[3,1,50,2048]{3,2,1,0:T(8,128)(2,1)}, bf16[3,1,50,2048]{3,2,1,0:T(8,128)(2,1)}, u32[]{:S(2)}, u32[]{:S(2)}) collective-permute-start(bf16[3,1,50,2048]{3,2,1,0:T(8,128)(2,1)} %pad_maximum_fusion.7), channel_id=1, source_target_pairs={{0,1},{1,2},{2,3},{3,4},{4,5},{5,6},{6,7},{8,9},{9,10},{10,11},{11... | collective-permute-start | bytes 1843208 | tf_op jit(solution)/shard_map/ppermute | solution.py:30
  64.8 39.1 %collective-permute-start.3 = (bf16[3,1,50,2048]{3,2,1,0:T(8,128)(2,1)}, bf16[3,1,50,2048]{3,2,1,0:T(8,128)(2,1)}, u32[]{:S(2)}, u32[]{:S(2)}) collective-permute-start(bf16[3,1,50,2048]{3,2,1,0:T(8,128)(2,1)} %pad_maximum_fusion.7), channel_id=1, source_target_pairs={{1,0},{2,1},{3,2},{4,3},{5,4},{6,5},{7,6},{9,8},{10,9},{11,10},{12... | collective-permute-start | bytes 1843208 | tf_op jit(solution)/shard_map/ppermute | solution.py:33
  73.8 3.8 copy-start.9
  80.0 3.0 copy-start.14
  85.9 17.4 %copy-start.18 = (f32[2,1024,8]{1,2,0:T(8,128)S(1)}, f32[2,1024,8]{1,2,0:T(8,128)}, u32[]{:S(2)}) copy-start(f32[2,1024,8]{1,2,0:T(8,128)} %param.18) | copy-start | bytes 196612
  92.1 225.3 %all-to-all-start = ((f32[128,1,3072]{2,1,0:T(1,128)}), f32[128,1,3072]{2,1,0:T(1,128)S(1)}, u32[]{:S(2)}, u32[]{:S(2)}) async-start(f32[128,1,3072]{2,1,0:T(1,128)} %reshape.1791), calls=%async_computation | async-start | bytes 3145728 | tf_op jit(solution)/shard_map/all_to_all | solution.py:247
  103.7 5.4 copy-start.16
  103.8 5.4 copy-start.17
  103.8 5.4 copy-start.19
  103.8 5.4 copy-start.22
  103.8 5.4 copy-start.23
  307.0 4.7 copy-start.15
  309.5 1.2 copy-start.7
  311.8 174.6 %collective-permute-start.4 = (bf16[1,3,48,2048]{3,2,1,0:T(8,128)(2,1)}, bf16[1,3,48,2048]{3,2,1,0:T(8,128)(2,1)}, u32[]{:S(2)}, u32[]{:S(2)}) collective-permute-start(bf16[1,3,48,2048]{3,2,1,0:T(8,128)(2,1)} %get-tuple-element.453), channel_id=1, source_target_pairs={{0,8},{8,16},{16,24},{24,32},{32,40},{40,48},{48,56},{56,64},{64,7... | collective-permute-start | bytes 1769480 | tf_op jit(solution)/shard_map/ppermute | solution.py:30
  316.2 170.3 %collective-permute-start.5 = (bf16[1,3,48,2048]{3,2,1,0:T(8,128)(2,1)}, bf16[1,3,48,2048]{3,2,1,0:T(8,128)(2,1)}, u32[]{:S(2)}, u32[]{:S(2)}) collective-permute-start(bf16[1,3,48,2048]{3,2,1,0:T(8,128)(2,1)} %get-tuple-element.454), channel_id=1, source_target_pairs={{8,0},{16,8},{24,16},{32,24},{40,32},{48,40},{56,48},{64,56},{72,6... | collective-permute-start | bytes 1769480 | tf_op jit(solution)/shard_map/ppermute | solution.py:33
  352.0 5.0 copy-start.4
  352.0 5.0 copy-start.11
  434.5 7.8 %copy-start = (f32[32,24,8,32]{3,0,2,1:T(8,128)}, f32[32,24,8,32]{3,0,2,1:T(8,128)S(1)}, u32[]{:S(2)}) copy-start(f32[32,24,8,32]{3,0,2,1:T(8,128)S(1)} %convolution_subtract_fusion.1) | copy-start | bytes 2359300
  469.9 16.5 %copy-start.8 = (bf16[9,48,2048]{2,1,0:T(8,128)(2,1)S(1)}, bf16[9,48,2048]{2,1,0:T(8,128)(2,1)}, u32[]{:S(2)}) copy-start(bf16[9,48,2048]{2,1,0:T(8,128)(2,1)} %copy-done.7) | copy-start | bytes 5308420
  476.3 73.5 %all-to-all-start.1 = ((f32[128,1,3072]{2,1,0:T(1,128)}), f32[128,1,3072]{2,1,0:T(1,128)S(1)}, u32[]{:S(2)}, u32[]{:S(2)}) async-start(f32[128,1,3072]{2,1,0:T(1,128)} %reshape.1793), calls=%async_computation.1 | async-start | bytes 3145728 | tf_op jit(solution)/shard_map/all_to_all | solution.py:262
  489.2 26.4 %collective-permute-start.6 = (bf16[5,1,48,2048]{3,2,1,0:T(8,128)(2,1)}, bf16[5,1,48,2048]{3,2,1,0:T(8,128)(2,1)}, u32[]{:S(2)}, u32[]{:S(2)}) collective-permute-start(bf16[5,1,48,2048]{3,2,1,0:T(8,128)(2,1)} %get-tuple-element.451), channel_id=1, source_target_pairs={{0,1},{1,2},{2,3},{3,4},{4,5},{5,6},{6,7},{8,9},{9,10},{10,11},{11... | collective-permute-start | bytes 2949128 | tf_op jit(solution)/shard_map/ppermute | solution.py:30
  492.8 24.0 %collective-permute-start.7 = (bf16[5,1,48,2048]{3,2,1,0:T(8,128)(2,1)}, bf16[5,1,48,2048]{3,2,1,0:T(8,128)(2,1)}, u32[]{:S(2)}, u32[]{:S(2)}) collective-permute-start(bf16[5,1,48,2048]{3,2,1,0:T(8,128)(2,1)} %get-tuple-element.452), channel_id=1, source_target_pairs={{1,0},{2,1},{3,2},{4,3},{5,4},{6,5},{7,6},{9,8},{10,9},{11,10},{12... | collective-permute-start | bytes 2949128 | tf_op jit(solution)/shard_map/ppermute | solution.py:33
  569.1 4.6 copy-start.2
  578.5 1.7 copy-start.5
  580.2 2.9 copy-start.12
  583.2 5.1 copy-start.3
  591.3 8.0 %copy-start.1 = (f32[32,8,24,32]{3,0,2,1:T(8,128)}, f32[32,8,24,32]{3,0,2,1:T(8,128)S(1)}, u32[]{:S(2)}) copy-start(f32[32,8,24,32]{3,0,2,1:T(8,128)S(1)} %convolution_subtract_fusion) | copy-start | bytes 2359300
  626.1 7.7 %copy-start.13 = (f32[48,2048]{0,1:T(8,128)S(1)}, f32[48,2048]{0,1:T(8,128)}, u32[]{:S(2)}) copy-start(f32[48,2048]{0,1:T(8,128)} %copy.167) | copy-start | bytes 1179652
  626.1 7.8 %copy-start.21 = (f32[2048]{0:T(1024)S(1)}, f32[2048]{0:T(1024)}, u32[]{:S(2)}) copy-start(f32[2048]{0:T(1024)} %param.14) | copy-start | bytes 24580
where the time goes:
time: 651 us; the launch traced here: 639 us
  matrix products  203 us (31%)
  local copies, waits for them, and re-layouts  163 us (25%)
  other arithmetic  113 us (17%)
  loops' own time  94.1 us (14%)
  starting transfers between devices  44.8 us (7%)
  waiting for transfers between devices  19.7 us (3%)
    dot_general x32, matrix products, transform(): return jnp.einsum(form, vector, matrix, precision=lax.Precision.HIGHEST)  169 us
    another operation x1, loops' own time, local(): lax.fori_loop(0, pair_list.shape[1], one_slot, (near_sum, returns))  94.1 us
    unnamed x54, local copies, waits for them, and re-layouts  25.4 us
    while x56, other arithmetic  22.6 us
    ppermute x4, waiting for transfers between devices, padded_2(): lax.ppermute(lax.slice_in_dim(block, block.shape[dim] - width, None, axis...  18.5 us
    ppermute x4, starting transfers between devices, padded_2(): lax.ppermute(lax.slice_in_dim(block, block.shape[dim] - width, None, axis...  17.1 us
    convert_element_type x1, other arithmetic, local(): padded = padded_2(returns.reshape(3, 3, channels, width_dev).astype(jnp.b...  14.2 us
    scatter-add x1, other arithmetic, local(): grid = jax.ops.segment_sum(scaled.T, cells, num_segments=CBX * GY)  13.7 us
  transfers between devices with their start and end apart: 10, of which 2 were waited for; matrix products, arithmetic and copies ran while one was open for 60% of the time, Pallas kernels for 0%

commit v1 on v0

v1 whole, which is shorter than its diff:
```python
import math

import jax
import jax.numpy as jnp
import numpy as np
from jax import lax
from jax.experimental import pallas as pl
from jax.experimental.pallas import tpu as pltpu
from jax.sharding import PartitionSpec as P

ANG = 4
PCX = 8
PCY = 16
CCX = 4
CCY = 4
PIL = 128
CHAN = 48
HALF = 24
WIDTH = 2048
PAIRS = 8
N_WIDE = 16
N_NARROW = 8
DEVICES = 128
AXES = ("wide", "narrow")
PITCH = 0.4
BF16 = jnp.bfloat16
F32 = jnp.float32
HALO = 10
MIB = 1 << 20


def split_table(table):
    high = table.astype(BF16)
    low = (table - high.astype(np.float64)).astype(BF16)
    return np.stack([high, low])


def dft_table(sign, scale=1.0):
    ids = np.arange(128)
    angles = (ids[:, None] * ids[None, :] % 128) * (2.0 * math.pi / 128)
    cosine = np.cos(angles) * scale
    sine = np.sin(angles) * scale * sign
    return split_table(np.block([[cosine, -sine], [sine, cosine]]))


def row_twiddle():
    k1 = np.repeat(np.arange(8), 8)
    angles = (k1[:, None] * np.arange(128)[None, :]) * (2.0 * math.pi / 1024)
    return np.stack([np.cos(angles), -np.sin(angles)]).astype(np.float32)


def column_twiddle():
    row = (np.arange(128) // 64)[None, None, :] + 2 * np.arange(4)[:, None, None]
    angles = (row * np.arange(128)[None, :, None]) * (2.0 * math.pi / 1024)
    return np.stack([np.cos(angles), -np.sin(angles)]).reshape(2, 512, 128).astype(np.float32)


def lane_twiddle():
    side = (np.arange(128) // 64)[None, :]
    angles = np.arange(4)[:, None] * side * (2.0 * math.pi / 8)
    table = np.concatenate([np.cos(angles), -np.sin(angles), np.where(side == 0, 1.0, -1.0)])
    return np.concatenate([table, np.zeros((7, 128))]).astype(np.float32)


def mixing_table():
    table = np.zeros((6, 6, 6), np.float32)
    for member in range(6):
        table[0, member, member] = 1.0
    for offset in (0, 3):
        table[1, offset, offset] = 1.0
        table[2, offset, offset + 1] = 1.0
        table[2, offset + 1, offset] = 1.0
        table[3, offset + 1, offset + 1] = 1.0
    table[4, 2, 4] = 1.0
    table[4, 4, 2] = 1.0
    table[4, 1, 5] = -1.0
    table[4, 5, 1] = -1.0
    table[5, 0, 5] = 1.0
    table[5, 5, 0] = 1.0
    table[5, 2, 3] = -1.0
    table[5, 3, 2] = -1.0
    parts = np.zeros((2, 2, 2), np.float32)
    parts[0] = np.eye(2)
    parts[1] = np.array([[0.0, -1.0], [1.0, 0.0]])
    full = np.einsum("fab,rop,gh->frogapb" + "h", table, parts, np.eye(ANG))
    full = full.transpose(0, 1, 2, 3, 4, 5, 7, 6)
    return full.reshape(12 * CHAN, CHAN).astype(BF16)


def dot(left, right, left_dim=1, right_dim=0):
    return lax.dot_general(
        left, right, (((left_dim,), (right_dim,)), ((), ())), preferred_element_type=F32
    )


def halves(value):
    high = value.astype(BF16)
    return high, (value - high.astype(F32)).astype(BF16)


def cadd(left, right):
    return (left[0] + right[0], left[1] + right[1])


def csub(left, right):
    return (left[0] - right[0], left[1] - right[1])


def cmul(left, right):
    return (left[0] * right[0] - left[1] * right[1], left[0] * right[1] + left[1] * right[0])


def cmul_conj(left, right):
    return (left[0] * right[0] + left[1] * right[1], left[1] * right[0] - left[0] * right[1])


def turn(value, sign):
    if sign < 0:
        return (value[1], -value[0])
    return (-value[1], value[0])


def dft4(values, sign):
    even, odd = cadd(values[0], values[2]), csub(values[0], values[2])
    left, right = cadd(values[1], values[3]), turn(csub(values[1], values[3]), sign)
    return [cadd(even, left), cadd(odd, right), csub(even, left), csub(odd, right)]


def dft8(values, sign):
    even = dft4(values[0::2], sign)
    odd = dft4(values[1::2], sign)
    root = math.sqrt(0.5)
    first, third = odd[1], odd[3]
    odd[1] = ((first[0] - sign * first[1]) * root, (first[1] + sign * first[0]) * root)
    odd[2] = turn(odd[2], sign)
    odd[3] = ((-third[0] - sign * third[1]) * root, (-third[1] + sign * third[0]) * root)
    return [cadd(e, o) for e, o in zip(even, odd)] + [csub(e, o) for e, o in zip(even, odd)]


def rows_kernel(x_ref, w_ref, cell_ref, dft_ref, tw_ref, out_ref, xt_ref, hot_ref, g_ref, b_ref):
    cells = cell_ref[...]
    upper = cells >> 8
    weight = w_ref[...]
    high = weight.astype(BF16).astype(F32)
    low = weight - high
    for block in range(16):
        place = lax.broadcasted_iota(jnp.int32, (16, WIDTH), 0) + block * 16
        hit = place == (cells & 255)
        hot_ref[0, block * 16 : block * 16 + 16, :] = jnp.where(hit, high, 0.0).astype(BF16)
        hot_ref[1, block * 16 : block * 16 + 16, :] = jnp.where(hit, low, 0.0).astype(BF16)
    for part in range(32):
        mask = jnp.where(upper == part, 1.0, 0.0).astype(BF16)
        xt_ref[part * CHAN : (part + 1) * CHAN, :] = x_ref[...] * mask
    for chunk in range(2):
        rows = slice(chunk * 768, (chunk + 1) * 768)
        piece = xt_ref[rows, :]
        g_ref[rows, :] = dot(piece, hot_ref[0], 1, 1) + dot(piece, hot_ref[1], 1, 1)

    def one_row(row, carry):
        for t in range(3):
            values = []
            for n1 in range(8):
                start = (row * 4 + n1 // 2) * CHAN + t * 8
                lanes = slice((n1 % 2) * 128, (n1 % 2) * 128 + 128)
                values.append(
                    (
                        g_ref[pl.ds(pl.multiple_of(start, 8), 8), lanes],
                        g_ref[pl.ds(pl.multiple_of(start + HALF, 8), 8), lanes],
                    )
                )
            values = dft8(values, -1.0)
            base = (((row // 2) * 3 + t) * 2 + row % 2) * 64
            for k1 in range(8):
                value = values[k1]
                if k1 > 0:
                    twiddle = (
                        tw_ref[0, k1 * 8 : k1 * 8 + 8, :],
                        tw_ref[1, k1 * 8 : k1 * 8 + 8, :],
                    )
                    value = cmul(value, twiddle)
                rows = pl.ds(pl.multiple_of(base + k1 * 8, 8), 8)
                b_ref[rows, 0:128] = value[0]
                b_ref[rows, 128:256] = value[1]
        return carry

    lax.fori_loop(0, 8, one_row, 0)
    for pair in range(6):
        b_high, b_low = halves(b_ref[pair * 256 : (pair + 1) * 256, :])
        result = (
            dot(dft_ref[0], b_high, 1, 1) + dot(dft_ref[0], b_low, 1, 1) + dot(dft_ref[1], b_high, 1, 1)
        )
        for part in range(2):
            for side in range(2):
                out_ref[pl.ds(part * 12 + pair * 2 + side, 128, 24), :] = result[
                    part * 128 : (part + 1) * 128, side * 128 : (side + 1) * 128
                ]


def columns_kernel(r_ref, kern_ref, fwd_ref, inv_ref, tw_ref, lane_ref, out_ref, v_ref, u_ref):
    for part in range(2):
        for group in range(12):
            v_ref[part * 128 : (part + 1) * 128, group * 128 : (group + 1) * 128] = r_ref[
                pl.ds(part * 12 + group, 128, 24), :
            ]
    for chunk in range(6):
        lanes = slice(chunk * 256, (chunk + 1) * 256)
        v_high, v_low = halves(v_ref[:, lanes])
        u_ref[:, lanes] = dot(fwd_ref[0], v_high) + dot(fwd_ref[0], v_low) + dot(fwd_ref[1], v_high)
    sign = lane_ref[8:9, :]

    def swap(value):
        return tuple(part * sign + pltpu.roll(part, 64, 1) for part in value)

    def one_block(block, carry):
        start = pl.multiple_of(block * 8, 8)
        re_rows = pl.ds(start, 8)
        im_rows = pl.ds(pl.multiple_of(start + 128, 8), 8)
        twiddles, kernels = [], []
        for m in range(4):
            rows = pl.ds(pl.multiple_of(start + m * 128, 8), 8)
            twiddles.append((tw_ref[0, rows, :], tw_ref[1, rows, :]))
            kernels.append((kern_ref[0, rows, :], kern_ref[1, rows, :]))
        for t in range(3):
            values = []
            for m in range(4):
                lanes = slice((m * 3 + t) * 128, (m * 3 + t + 1) * 128)
                values.append(cmul((u_ref[re_rows, lanes], u_ref[im_rows, lanes]), twiddles[m]))
            values = dft4(values, -1.0)
            for a in range(4):
                side = (lane_ref[a : a + 1, :], lane_ref[4 + a : 5 + a, :])
                value = values[a] if a == 0 else cmul(values[a], side)
                value = swap(cmul(swap(value), kernels[a]))
                values[a] = value if a == 0 else cmul_conj(value, side)
            values = dft4(values, 1.0)
            for m in range(4):
                lanes = slice((m * 3 + t) * 128, (m * 3 + t + 1) * 128)
                value = cmul_conj(values[m], twiddles[m])
                v_ref[re_rows, lanes] = value[0]
                v_ref[im_rows, lanes] = value[1]
        return carry

    lax.fori_loop(0, 16, one_block, 0)
    for chunk in range(6):
        lanes = slice(chunk * 256, (chunk + 1) * 256)
        v_high, v_low = halves(v_ref[:, lanes])
        result = dot(inv_ref[0], v_high) + dot(inv_ref[0], v_low) + dot(inv_ref[1], v_high)
        for part in range(2):
            for side in range(2):
                out_ref[pl.ds(part * 12 + chunk * 2 + side, 128, 24), :] = result[
                    part * 128 : (part + 1) * 128, side * 128 : (side + 1) * 128
                ]


def sample_kernel(
    r_ref, w_ref, cell_ref, near_ref, one_ref, two_ref, three_ref, four_ref, dft_ref, tw_ref,
    out_ref, v_ref, g_ref, f_ref,
):
    for part in range(2):
        for group in range(12):
            piece = r_ref[pl.ds(part * 12 + group, 128, 24), :]
            v_ref[group * 128 : (group + 1) * 128, part * 128 : (part + 1) * 128] = piece.T
    for chunk in range(2):
        rows = slice(chunk * 768, (chunk + 1) * 768)
        v_high, v_low = halves(v_ref[rows, :])
        g_ref[rows, :] = (
            dot(v_high, dft_ref[0], 1, 1) + dot(v_low, dft_ref[0], 1, 1) + dot(v_high, dft_ref[1], 1, 1)
        )

    def one_row(row, carry):
        for t in range(3):
            base = (((row // 2) * 3 + t) * 2 + row % 2) * 64
            values = []
            for k1 in range(8):
                rows = pl.ds(pl.multiple_of(base + k1 * 8, 8), 8)
                value = (g_ref[rows, 0:128], g_ref[rows, 128:256])
                if k1 > 0:
                    twiddle = (
                        tw_ref[0, k1 * 8 : k1 * 8 + 8, :],
                        tw_ref[1, k1 * 8 : k1 * 8 + 8, :],
                    )
                    value = cmul_conj(value, twiddle)
                values.append(value)
            values = dft8(values, 1.0)
            for n1 in range(8):
                start = (row * 4 + n1 // 2) * CHAN + t * 8
                lanes = slice((n1 % 2) * 128, (n1 % 2) * 128 + 128)
                v_ref[pl.ds(pl.multiple_of(start, 8), 8), lanes] = values[n1][0]
                v_ref[pl.ds(pl.multiple_of(start + HALF, 8), 8), lanes] = values[n1][1]
        return carry

    lax.fori_loop(0, 8, one_row, 0)
    f_high, f_low = halves(v_ref[...])
    f_ref[0] = f_high
    f_ref[1] = f_low
    place = lax.broadcasted_iota(jnp.int32, (256, 256), 0)
    for chunk in range(8):
        lanes = slice(chunk * 256, (chunk + 1) * 256)
        cells = cell_ref[:, lanes]
        hot = jnp.where(place == (cells & 255), 1.0, 0.0).astype(BF16)
        upper = cells >> 8
        total = jnp.zeros((CHAN, 256), F32)
        for quarter in range(4):
            rows = slice(quarter * 384, (quarter + 1) * 384)
            picked = dot(f_ref[0, rows, :], hot) + dot(f_ref[1, rows, :], hot)
            for part in range(8):
                hit = jnp.broadcast_to(upper == quarter * 8 + part, (CHAN, 256))
                total = total + jnp.where(hit, picked[part * CHAN : (part + 1) * CHAN, :], 0.0)
        out_ref[:, lanes] = total * w_ref[:, lanes] + near_ref[:, lanes]
    for cluster in range(4):
        lanes = slice(cluster * 4 * PIL, (cluster * 4 + 1) * PIL)
        out_ref[:, lanes] += one_ref[:, cluster * PIL : (cluster + 1) * PIL].astype(F32)
        lanes = slice(cluster * PIL, (cluster + 1) * PIL)
        out_ref[:, lanes] += two_ref[:, cluster * PIL : (cluster + 1) * PIL].astype(F32)
    out_ref[:, 3 * PIL : 4 * PIL] += three_ref[...].astype(F32)
    out_ref[:, 15 * PIL : 16 * PIL] += four_ref[...].astype(F32)


def taylor(count, first):
    return [(-1.0) ** n / math.factorial(2 * n + first) for n in range(count)]


def horner(coefficients, square):
    total = jnp.full_like(square, coefficients[-1])
    for coefficient in coefficients[-2::-1]:
        total = total * square + coefficient
    return total


def near_kernel(
    list_ref, own_ref, one_ref, two_ref, three_ref, four_ref, own_pos, one_pos, two_pos, three_pos,
    four_pos, mix_ref, near_ref, back_one, back_two, back_three, back_four, all_ref, pos_ref, sum_ref,
):
    all_ref[:, 0:WIDTH] = own_ref[...]
    pos_ref[0:2, 0:WIDTH] = own_pos[...].astype(F32)
    start = WIDTH
    for data, pos in ((one_ref, one_pos), (two_ref, two_pos), (three_ref, three_pos), (four_ref, four_pos)):
        width = data.shape[1]
        all_ref[:, start : start + width] = data[...]
        pos_ref[0:2, start : start + width] = pos[...].astype(F32)
        start += width
    sum_ref[...] = jnp.zeros_like(sum_ref)
    wide_pos = list_ref[24]
    narrow_pos = list_ref[25]
    used = list_ref[26]
    local = lax.broadcasted_iota(jnp.int32, (1, PIL), 1)

    def place(wide, narrow, cluster, window):
        across = ((wide * CCX + cluster // CCY) * PCX + local // PCY).astype(F32)
        along = ((narrow * CCY + cluster % CCY) * PCY + local % PCY).astype(F32)
        return across * PITCH + pos_ref[0:1, window], along * PITCH + pos_ref[1:2, window]

    def column(vector):
        return jnp.broadcast_to(vector, (PIL, PIL)).T

    def mixed(values):
        return dot(mix_ref[...], values).astype(BF16)

    def one_slot(slot, carry):
        direction = list_ref[slot * 3]
        own = list_ref[slot * 3 + 1]
        far = list_ref[slot * 3 + 2]
        move_wide = jnp.where(direction == 4, -1, jnp.where(direction >= 2, 1, 0))
        move_narrow = jnp.where(direction == 1, 1, jnp.where(direction >= 3, -1, 0))
        index = jnp.where(direction == 1, 16 + far // 4, far)
        index = jnp.where(direction == 2, 20 + far, index)
        index = jnp.where(direction == 3, 24, index)
        index = jnp.where(direction == 4, 25, index)
        own_window = pl.ds(pl.multiple_of(own * PIL, PIL), PIL)
        far_window = pl.ds(pl.multiple_of(index * PIL, PIL), PIL)
        own_x, own_y = place(wide_pos, narrow_pos, own, own_window)
        far_x, far_y = place(wide_pos + move_wide, narrow_pos + move_narrow, far, far_window)
        delta_x = column(own_x) - far_x
        delta_y = column(own_y) - far_y
        square = delta_x * delta_x + delta_y * delta_y
        over = lax.rsqrt(square)
        distance = square * over
        turns = (distance - jnp.round(distance)) * (2.0 * math.pi)
        turns_square = turns * turns
        cosine = horner(taylor(10, 0), turns_square)
        sine = horner(taylor(10, 1), turns_square) * turns
        unit_x = delta_x * over
        unit_y = delta_y * over
        inverse = over * (1.0 / (2.0 * math.pi))
        inverse_square = inverse * inverse
        green = (cosine * inverse, sine * inverse)
        term_a = cmul(green, (1.0 - inverse_square, inverse))
        term_b = cmul(green, (3.0 * inverse_square - 1.0, -3.0 * inverse))
        term_c = (green[0] - green[1] * inverse, green[1] + green[0] * inverse)
        unit_xx = unit_x * unit_x
        unit_xy = unit_x * unit_y
        unit_yy = unit_y * unit_y
        own_mixed = mixed(all_ref[:, own_window])
        far_mixed = mixed(all_ref[:, far_window])
        to_own = jnp.zeros((CHAN, PIL), F32)
        to_far = jnp.zeros((CHAN, PIL), F32)
        for field in range(6):
            for part in range(2):
                value = (
                    term_a[part],
                    term_b[part] * unit_xx,
                    term_b[part] * unit_xy,
                    term_b[part] * unit_yy,
                    term_c[part] * unit_x,
                    term_c[part] * unit_y,
                )[field].astype(BF16)
                rows = slice((field * 2 + part) * CHAN, (field * 2 + part + 1) * CHAN)
                to_own = to_own + dot(far_mixed[rows], value, 1, 1)
                to_far = to_far + dot(own_mixed[rows], value, 1, 0)
        sum_ref[:, own_window] += to_own
        sum_ref[:, far_window] += to_far
        return carry

    lax.fori_loop(0, used, one_slot, 0)
    near_ref[...] = sum_ref[:, 0:WIDTH]
    start = WIDTH
    for back in (back_one, back_two, back_three, back_four):
        width = back.shape[1]
        back[...] = sum_ref[:, start : start + width].astype(BF16)
        start += width


def shape(dims, kind=F32):
    return jax.ShapeDtypeStruct(dims, kind)


def steps(move_wide, move_narrow):
    pairs = []
    for wide in range(N_WIDE):
        for narrow in range(N_NARROW):
            to_wide, to_narrow = wide + move_wide, narrow + move_narrow
            if 0 <= to_wide < N_WIDE and 0 <= to_narrow < N_NARROW:
                pairs.append((wide * N_NARROW + narrow, to_wide * N_NARROW + to_narrow))
    return pairs


MOVES = ((0, 1), (1, 0), (1, -1), (-1, -1))
PARAMS = pltpu.CompilerParams(vmem_limit_bytes=48 * MIB)


def exchange(message):
    code = message * lax.rsqrt(jnp.maximum(jnp.abs(message), 1e-30))
    code = code.reshape(DEVICES, HALF, 128).astype(jnp.float16)
    code = lax.all_to_all(code, AXES, split_axis=0, concat_axis=0, tiled=True)
    code = code.astype(F32)
    return (code * jnp.abs(code)).reshape(DEVICES * HALF, 128)


def local(incident, jitter, weights, cells, pair_list, pair_count, kernel):
    x = incident.reshape(CHAN, WIDTH)
    w = weights.reshape(1, WIDTH)
    cell = cells.reshape(1, WIDTH)

    packed = jnp.concatenate([x, jitter], axis=0)
    pieces = (
        jnp.concatenate([packed[:, c * PIL : (c + 1) * PIL] for c in (0, 4, 8, 12)], axis=1),
        packed[:, 0 : 4 * PIL],
        packed[:, 3 * PIL : 4 * PIL],
        packed[:, 15 * PIL : 16 * PIL],
    )
    halo = [
        lax.ppermute(piece, AXES, steps(-wide, -narrow)) for piece, (wide, narrow) in zip(pieces, MOVES)
    ]

    message = pl.pallas_call(
        rows_kernel,
        out_shape=shape((DEVICES * HALF, 128)),
        scratch_shapes=[
            pltpu.VMEM((1536, WIDTH), BF16),
            pltpu.VMEM((2, 256, WIDTH), BF16),
            pltpu.VMEM((1536, 256), F32),
            pltpu.VMEM((1536, 256), F32),
        ],
        compiler_params=PARAMS,
        cost_estimate=pl.CostEstimate(flops=3_800_000_000, bytes_accessed=4 * MIB, transcendentals=0),
    )(x, w, cell, jnp.asarray(dft_table(-1.0)), jnp.asarray(row_twiddle()))
    columns = exchange(message)

    spots = jnp.concatenate(
        [
            pair_list.reshape(PAIRS * 3),
            lax.axis_index("wide").reshape(1),
            lax.axis_index("narrow").reshape(1),
            pair_count,
        ]
    )
    near, *returns = pl.pallas_call(
        near_kernel,
        in_specs=[pl.BlockSpec(memory_space=pltpu.SMEM)] + [pl.BlockSpec(memory_space=pltpu.VMEM)] * 11,
        out_shape=[
            shape((CHAN, WIDTH)),
            shape((CHAN, 4 * PIL), BF16),
            shape((CHAN, 4 * PIL), BF16),
            shape((CHAN, PIL), BF16),
            shape((CHAN, PIL), BF16),
        ],
        scratch_shapes=[
            pltpu.VMEM((CHAN, WIDTH + HALO * PIL), BF16),
            pltpu.VMEM((8, WIDTH + HALO * PIL), F32),
            pltpu.VMEM((CHAN, WIDTH + HALO * PIL), F32),
        ],
        compiler_params=PARAMS,
        cost_estimate=pl.CostEstimate(flops=8_000_000_000, bytes_accessed=4 * MIB, transcendentals=0),
    )(spots, x, *[h[:CHAN] for h in halo], jitter, *[h[CHAN:] for h in halo], jnp.asarray(mixing_table()))
    back = [
        lax.ppermute(piece, AXES, steps(wide, narrow)) for piece, (wide, narrow) in zip(returns, MOVES)
    ]

    transfer = kernel.reshape(2, 2, 4, 128, 8).transpose(0, 2, 3, 1, 4)
    transfer = jnp.broadcast_to(transfer[..., None], (2, 4, 128, 2, 8, 8)).reshape(2, 512, 128)
    message = pl.pallas_call(
        columns_kernel,
        out_shape=shape((DEVICES * HALF, 128)),
        scratch_shapes=[pltpu.VMEM((256, 1536), F32), pltpu.VMEM((256, 1536), F32)],
        compiler_params=PARAMS,
        cost_estimate=pl.CostEstimate(flops=2_000_000_000, bytes_accessed=6 * MIB, transcendentals=0),
    )(
        columns,
        transfer,
        jnp.asarray(dft_table(-1.0)),
        jnp.asarray(dft_table(1.0, 1.0 / 1048576)),
        jnp.asarray(column_twiddle()),
        jnp.asarray(lane_twiddle()),
    )
    rows = exchange(message)

    coupled = pl.pallas_call(
        sample_kernel,
        out_shape=shape((CHAN, WIDTH)),
        scratch_shapes=[
            pltpu.VMEM((1536, 256), F32),
            pltpu.VMEM((1536, 256), F32),
            pltpu.VMEM((2, 1536, 256), BF16),
        ],
        compiler_params=PARAMS,
        cost_estimate=pl.CostEstimate(flops=3_800_000_000, bytes_accessed=4 * MIB, transcendentals=0),
    )(rows, w, cell, near, *back, jnp.asarray(dft_table(1.0)), jnp.asarray(row_twiddle()))
    return coupled.reshape(2, ANG, 6, WIDTH)


def solution(mesh):
    in_specs = (
        P(None, None, None, AXES),
        P(None, AXES),
        P(AXES),
        P(AXES),
        P(AXES, None, None),
        P(AXES),
        P(None, None, AXES),
    )
    return jax.shard_map(
        local, mesh=mesh, in_specs=in_specs, out_specs=P(None, None, None, AXES), check_vma=False
    )
```

time: 651 us -> 82.7 us (0.13); the launches traced: 639 us -> 82.1 us
  matrix products: 203 us -> 0 us
  local copies, waits for them, and re-layouts: 163 us -> 6.16 us
  other arithmetic: 113 us -> 2.85 us
  loops' own time: 94.1 us -> 0 us
  Pallas kernels: 0 us -> 22 us
  waiting for transfers between devices: 19.7 us -> 9.56 us
    dot_general x80 -> x0, matrix products: 203 us -> none  [the longest x32 169 us: transform(): return jnp.einsum(form, vector, matrix, precision=lax.Precision.HIGHEST)]
    another operation x1 -> x0, loops' own time: 94.1 us -> none  [local(): lax.fori_loop(0, pair_list.shape[1], one_slot, (near_sum, returns))]
    reshape x48 -> x6, local copies, waits for them, and re-layouts: 50.5 us -> 1.61 us  [the longest x2 1.05 us: local(): return coupled.reshape(2, ANG, 6, WIDTH)]
    convert_element_type x18 -> x2, other arithmetic: 28.2 us -> 2.4 us  [exchange(): code = code.reshape(DEVICES, HALF, 128).astype(jnp.float16)]
    while x56 -> x0, other arithmetic: 22.6 us -> none
    pallas_call x0 -> x4, Pallas kernels: none -> 22 us  [the longest x1 6.36 us: local(): pl.pallas_call(near_kernel, in_specs=[pl.BlockSpec(memory_space=pltpu.SME...]
    unnamed x54 -> x35, local copies, waits for them, and re-layouts: 25.4 us -> 4.39 us
    concatenate x4 -> x1, local copies, waits for them, and re-layouts: 20.8 us -> 0.02 us  [local(): packed = jnp.concatenate([x, jitter], axis=0)]
  transfers between devices with their start and end apart: 10 -> 10, of which waited for: 2 -> 2; matrix products, arithmetic and copies ran while one was open for 60% -> 3% of each run, Pallas kernels for 0% -> 14%
where the time goes in v1:
time: 82.7 us; the launch traced here: 82.1 us
  starting transfers between devices  40.3 us (49%)
  Pallas kernels  22 us (27%)
  waiting for transfers between devices  9.56 us (12%)
  local copies, waits for them, and re-layouts  6.16 us (7%)
  other arithmetic  2.85 us (3%)
  between operations  1.23 us (1%)
    all_to_all x2, starting transfers between devices, exchange(): code = lax.all_to_all(code, AXES, split_axis=0, concat_axis=0, tiled=True)  19.6 us
    ppermute x4, starting transfers between devices, local(): lax.ppermute(piece, AXES, steps(-wide, -narrow))  10.9 us
    ppermute x4, starting transfers between devices, local(): lax.ppermute(piece, AXES, steps(wide, narrow))  9.81 us
    pallas_call x1, Pallas kernels, local(): pl.pallas_call(near_kernel, in_specs=[pl.BlockSpec(memory_space=pltpu.SME...  6.36 us
    pallas_call x1, Pallas kernels, local(): pl.pallas_call(sample_kernel, out_shape=shape((CHAN, WIDTH)), scratch_sha...  5.66 us
    ppermute x4, waiting for transfers between devices, local(): lax.ppermute(piece, AXES, steps(wide, narrow))  5.51 us
    pallas_call x1, Pallas kernels, local(): pl.pallas_call(columns_kernel, out_shape=shape((DEVICES * HALF, 128)), sc...  5.13 us
    pallas_call x1, Pallas kernels, local(): pl.pallas_call(rows_kernel, out_shape=shape((DEVICES * HALF, 128)), scrat...  4.85 us
  transfers between devices with their start and end apart: 10, of which 2 were waited for; matrix products, arithmetic and copies ran while one was open for 3% of the time, Pallas kernels for 14%

profile of v1, /device:TPU:1, one launch (start us, length us, event | category | flops | bytes accessed | tf_op | source)
XLA Modules:
  0.0 82.1 jit_solution(15871640996287776428)
XLA Ops:
  0.0 1.0 %copy.21 = bf16[2,4,6,2048]{3,2,1,0:T(8,128)(2,1)S(1)} copy(bf16[2,4,6,2048]{3,1,2,0:T(4,128)(2,1)} %param.16) | data formatting | bytes 393216 | tf_op args[0]
  1.0 0.1 reshape.38.x_ref.own_ref
  1.1 0.0 copy-start.1
  1.1 0.7 copy-done.1
  1.8 0.7 copy-done.3
  2.5 0.9 %copy-done.7 = bf16[2,256,256]{2,1,0:T(8,128)(2,1)S(1)} copy-done((bf16[2,256,256]{2,1,0:T(8,128)(2,1)S(1)}, bf16[2,256,256]{2,1,0:T(8,128)(2,1)}, u32[]{:S(2)}) %copy-start.7) | copy-done | bytes 262168
  3.5 0.8 %copy-done.11 = f32[2,64,128]{2,1,0:T(8,128)S(1)} copy-done((f32[2,64,128]{2,1,0:T(8,128)S(1)}, f32[2,64,128]{2,1,0:T(8,128)}, u32[]{:S(2)}) %copy-start.11) | copy-done | bytes 65560
  4.3 4.9 %shard_map.154 = f32[3072,128]{1,0:T(8,128)S(1)} custom-call(bf16[48,2048]{1,0:T(8,128)(2,1)S(1)} %reshape.38.x_ref.own_ref, f32[1,2048]{1,0:T(1,128)S(1)} %bitcast.15, s32[1,2048]{1,0:T(1,128)S(1)} %bitcast.17, bf16[2,256,256]{2,1,0:T(8,128)(2,1)S(1)} %copy-done.7, f32[2,64,128]{2,1,0:T(8,128)S(1)} %copy-done.11), custom_call_target="tpu_custom_call" | custom-call | flops 3800000000 | bytes 4194304 | tf_op jit(solution)/shard_map/pallas_call | solution.py:464
  9.2 1.2 %multiply_convert_fusion.1 = f16[3072,128]{1,0:T(8,128)(2,1)} fusion(f32[3072,128]{1,0:T(8,128)S(1)} %shard_map.154), kind=kLoop, calls=%fused_computation.3 | loop fusion | flops 1572864 | bytes 2359296 | tf_op jit(solution)/shard_map/convert_element_type | solution.py:442
  10.4 11.5 %all-to-all-start = ((f16[128,24,128]{2,1,0:T(8,128)(2,1)}), f16[128,24,128]{2,1,0:T(8,128)(2,1)S(1)}, u32[]{:S(2)}, u32[]{:S(2)}) async-start(f16[128,24,128]{2,1,0:T(8,128)(2,1)} %bitcast.2), calls=%async_computation | async-start | bytes 1572864 | tf_op jit(solution)/shard_map/all_to_all | solution.py:443
  22.0 0.0 copy-start.15
  22.0 3.0 %collective-permute-start = (bf16[50,512]{1,0:T(8,128)(2,1)S(1)}, bf16[50,512]{1,0:T(8,128)(2,1)S(1)}, u32[]{:S(2)}, u32[]{:S(2)}) collective-permute-start(bf16[50,512]{1,0:T(8,128)(2,1)S(1)} %pad_maximum_fusion), channel_id=1, source_target_pairs={{1,0},{2,1},{3,2},{4,3},{5,4},{6,5},{7,6},{9,8},{10,9},{11,10},{12... | collective-permute-start | bytes 153608 | tf_op jit(solution)/shard_map/ppermute | solution.py:461
  25.0 1.3 %collective-permute-start.1 = (bf16[50,512]{1,0:T(8,128)(2,1)S(1)}, bf16[50,512]{1,0:T(8,128)(2,1)S(1)}, u32[]{:S(2)}, u32[]{:S(2)}) collective-permute-start(bf16[50,512]{1,0:T(8,128)(2,1)S(1)} %slice.65), channel_id=1, source_target_pairs={{8,0},{9,1},{10,2},{11,3},{12,4},{13,5},{14,6},{15,7},{16,8},{17,9... | collective-permute-start | bytes 153608 | tf_op jit(solution)/shard_map/ppermute | solution.py:461
  26.3 1.3 %collective-permute-start.2 = (bf16[50,128]{1,0:T(8,128)(2,1)S(1)}, bf16[50,128]{1,0:T(8,128)(2,1)S(1)}, u32[]{:S(2)}, u32[]{:S(2)}) collective-permute-start(bf16[50,128]{1,0:T(8,128)(2,1)S(1)} %get-tuple-element.16), channel_id=1, source_target_pairs={{8,1},{9,2},{10,3},{11,4},{12,5},{13,6},{14,7},{16,9},{17,10},{18,... | collective-permute-start | bytes 38408 | tf_op jit(solution)/shard_map/ppermute | solution.py:461
  27.6 5.3 %collective-permute-start.3 = (bf16[50,128]{1,0:T(8,128)(2,1)S(1)}, bf16[50,128]{1,0:T(8,128)(2,1)S(1)}, u32[]{:S(2)}, u32[]{:S(2)}) collective-permute-start(bf16[50,128]{1,0:T(8,128)(2,1)S(1)} %get-tuple-element.15), channel_id=1, source_target_pairs={{0,9},{1,10},{2,11},{3,12},{4,13},{5,14},{6,15},{8,17},{9,18},{10,... | collective-permute-start | bytes 38408 | tf_op jit(solution)/shard_map/ppermute | solution.py:461
  32.9 0.1 broadcast_in_dim.2
  33.0 0.2 reshape.43
  33.2 0.0 copy-start.5
  33.3 0.0 copy-start.8
  33.3 0.0 copy-start.9
  33.3 0.0 copy-start.13
  33.3 0.2 copy.23.kern_ref
  34.2 0.1 copy.24
  34.3 0.1 reshape.45
  34.4 4.0 %all-to-all-done = f16[128,24,128]{2,1,0:T(8,128)(2,1)S(1)} async-done(((f16[128,24,128]{2,1,0:T(8,128)(2,1)}), f16[128,24,128]{2,1,0:T(8,128)(2,1)S(1)}, u32[]{:S(2)}, u32[]{:S(2)}) %all-to-all-start) | async-done | bytes 786464 | tf_op jit(solution)/shard_map/all_to_all | solution.py:443
  38.4 0.2 abs_multiply_fusion.1
  38.7 5.1 %shard_map.155 = f32[3072,128]{1,0:T(8,128)S(1)} custom-call(f32[3072,128]{1,0:T(8,128)S(1)} %bitcast.14, f32[2,512,128]{2,1,0:T(8,128)S(1)} %copy.23.kern_ref, bf16[2,256,256]{2,1,0:T(8,128)(2,1)S(1)} %copy-done.8, bf16[2,256,256]{2,1,0:T(8,128)(2,1)S(1)} %copy-done.9, f32[2,512,128]{2,1,0:T(8,128)S(1)} %copy-done.5, f32[16,128]{1,0:T(8,128)S(1)} %copy-done.13), custom_call_target="tpu_custom_call" | custom-call | flops 2000000000 | bytes 6291456 | tf_op jit(solution)/shard_map/pallas_call | solution.py:510
  43.8 0.0 copy-start.10
  43.8 1.2 %multiply_convert_fusion = f16[3072,128]{1,0:T(8,128)(2,1)} fusion(f32[3072,128]{1,0:T(8,128)S(1)} %shard_map.155), kind=kLoop, calls=%fused_computation.2 | loop fusion | flops 1572864 | bytes 2359296 | tf_op jit(solution)/shard_map/convert_element_type | solution.py:442
  45.0 8.1 %all-to-all-start.1 = ((f16[128,24,128]{2,1,0:T(8,128)(2,1)}), f16[128,24,128]{2,1,0:T(8,128)(2,1)S(1)}, u32[]{:S(2)}, u32[]{:S(2)}) async-start(f16[128,24,128]{2,1,0:T(8,128)(2,1)} %bitcast.6), calls=%async_computation.1 | async-start | bytes 1572864 | tf_op jit(solution)/shard_map/all_to_all | solution.py:443
  53.2 0.1 pad_add_fusion.list_ref
  53.3 0.0 collective-permute-done
  53.3 0.0 collective-permute-done.1
  53.4 6.4 %shard_map.156 = (f32[48,2048]{1,0:T(8,128)S(1)}, bf16[48,512]{1,0:T(8,128)(2,1)S(1)}, bf16[48,512]{1,0:T(8,128)(2,1)S(1)}, bf16[48,128]{1,0:T(8,128)(2,1)S(1)}, bf16[48,128]{1,0:T(8,128)(2,1)S(1)}) custom-call(s32[27]{0:T(128)S(1)} %pad_add_fusion.list_ref, bf16[48,2048]{1,0:T(8,128)(2,1)S(1)} %reshape.38.x_ref.own_ref, bf16[48,512]{1,0:T(8,128)(2,1)S(1)} %slice.64.one_ref, ...), custom_call_target="tpu_custom_call" | custom-call | flops 8000000000 | bytes 4194304 | tf_op jit(solution)/shard_map/pallas_call | solution.py:486
  59.7 0.0 copy-start.2
  59.7 0.0 copy-start.4
  59.8 0.0 copy-start.6
  59.8 0.0 copy-start.12
  59.8 2.1 %collective-permute-start.4 = (bf16[48,512]{1,0:T(8,128)(2,1)S(1)}, bf16[48,512]{1,0:T(8,128)(2,1)S(1)}, u32[]{:S(2)}, u32[]{:S(2)}) collective-permute-start(bf16[48,512]{1,0:T(8,128)(2,1)S(1)} %get-tuple-element.11), channel_id=1, source_target_pairs={{0,1},{1,2},{2,3},{3,4},{4,5},{5,6},{6,7},{8,9},{9,10},{10,11},{11... | collective-permute-start | bytes 147464 | tf_op jit(solution)/shard_map/ppermute | solution.py:505
  61.8 1.3 %collective-permute-start.5 = (bf16[48,512]{1,0:T(8,128)(2,1)S(1)}, bf16[48,512]{1,0:T(8,128)(2,1)S(1)}, u32[]{:S(2)}, u32[]{:S(2)}) collective-permute-start(bf16[48,512]{1,0:T(8,128)(2,1)S(1)} %get-tuple-element.12), channel_id=1, source_target_pairs={{0,8},{1,9},{2,10},{3,11},{4,12},{5,13},{6,14},{7,15},{8,16},{9,17... | collective-permute-start | bytes 147464 | tf_op jit(solution)/shard_map/ppermute | solution.py:505
  63.1 5.0 %collective-permute-start.6 = (bf16[48,128]{1,0:T(8,128)(2,1)S(1)}, bf16[48,128]{1,0:T(8,128)(2,1)S(1)}, u32[]{:S(2)}, u32[]{:S(2)}) collective-permute-start(bf16[48,128]{1,0:T(8,128)(2,1)S(1)} %get-tuple-element.13), channel_id=1, source_target_pairs={{1,8},{2,9},{3,10},{4,11},{5,12},{6,13},{7,14},{9,16},{10,17},{11,... | collective-permute-start | bytes 36872 | tf_op jit(solution)/shard_map/ppermute | solution.py:505
  68.1 1.5 %collective-permute-start.7 = (bf16[48,128]{1,0:T(8,128)(2,1)S(1)}, bf16[48,128]{1,0:T(8,128)(2,1)S(1)}, u32[]{:S(2)}, u32[]{:S(2)}) collective-permute-start(bf16[48,128]{1,0:T(8,128)(2,1)S(1)} %get-tuple-element.14), channel_id=1, source_target_pairs={{9,0},{10,1},{11,2},{12,3},{13,4},{14,5},{15,6},{17,8},{18,9},{19,... | collective-permute-start | bytes 36872 | tf_op jit(solution)/shard_map/ppermute | solution.py:505
  69.6 0.2 abs_multiply_fusion
  69.8 0.0 collective-permute-done.6.three_ref
  69.8 5.5 %collective-permute-done.7.four_ref = bf16[48,128]{1,0:T(8,128)(2,1)S(1)} collective-permute-done((bf16[48,128]{1,0:T(8,128)(2,1)S(1)}, bf16[48,128]{1,0:T(8,128)(2,1)S(1)}, u32[]{:S(2)}, u32[]{:S(2)}) %collective-permute-start.7) | collective-permute-done | bytes 12320 | tf_op jit(solution)/shard_map/ppermute | solution.py:505
  75.4 5.7 %shard_map.157 = f32[48,2048]{1,0:T(8,128)S(1)} custom-call(f32[3072,128]{1,0:T(8,128)S(1)} %bitcast.13, f32[1,2048]{1,0:T(1,128)S(1)} %bitcast.16, s32[1,2048]{1,0:T(1,128)S(1)} %bitcast.18, f32[48,2048]{1,0:T(8,128)S(1)} %get-tuple-element.10.near_ref, bf16[48,512]{1,0:T(8,128)(2,1)S(1)} %collective-permute-done.4.one_ref, ...), custom_call_target="tpu_custom_call" | custom-call | flops 3800000000 | bytes 4194304 | tf_op jit(solution)/shard_map/pallas_call | solution.py:526
  81.0 0.1 reshape.48
  81.1 1.0 %copy.25 = f32[2,4,6,2048]{3,1,2,0:T(4,128)} copy(f32[2,4,6,2048]{3,2,1,0:T(8,128)S(1)} %reshape.48) | data formatting | bytes 786432 | tf_op jit(solution)/shard_map/reshape | solution.py:537
  (36 shorter events, 0.2 us)
Async XLA Ops:
  1.1 0.7 copy-start.1
  1.8 0.7 copy-start.3
  2.5 0.9 %copy-start.7 = (bf16[2,256,256]{2,1,0:T(8,128)(2,1)S(1)}, bf16[2,256,256]{2,1,0:T(8,128)(2,1)}, u32[]{:S(2)}) copy-start(bf16[2,256,256]{2,1,0:T(8,128)(2,1)} %constant.25.clone.dft_ref.fwd_ref) | copy-start | bytes 786436
  3.5 0.8 %copy-start.11 = (f32[2,64,128]{2,1,0:T(8,128)S(1)}, f32[2,64,128]{2,1,0:T(8,128)}, u32[]{:S(2)}) copy-start(f32[2,64,128]{2,1,0:T(8,128)} %constant.26.clone.tw_ref) | copy-start | bytes 196612
  10.4 11.5 %copy-start = (bf16[2,2048]{1,0:T(2,128)(2,1)S(1)}, bf16[2,2048]{1,0:T(2,128)(2,1)}, u32[]{:S(2)}) copy-start(bf16[2,2048]{1,0:T(2,128)(2,1)} %own_pos.1) | copy-start | bytes 24580
  10.4 22.5 %copy-start.14 = (f32[2,1024,8]{1,2,0:T(8,128)S(1)}, f32[2,1024,8]{1,2,0:T(8,128)}, u32[]{:S(2)}) copy-start(f32[2,1024,8]{1,2,0:T(8,128)} %param.22) | copy-start | bytes 196612
  10.4 28.1 %all-to-all-start = ((f16[128,24,128]{2,1,0:T(8,128)(2,1)}), f16[128,24,128]{2,1,0:T(8,128)(2,1)S(1)}, u32[]{:S(2)}, u32[]{:S(2)}) async-start(f16[128,24,128]{2,1,0:T(8,128)(2,1)} %bitcast.2), calls=%async_computation | async-start | bytes 1572864 | tf_op jit(solution)/shard_map/all_to_all | solution.py:443
  22.0 12.3 %copy-start.15 = (s32[1,8,3]{1,0,2:T(1,128)S(1)}, s32[1,8,3]{1,0,2:T(1,128)}, u32[]{:S(2)}) copy-start(s32[1,8,3]{1,0,2:T(1,128)} %param.20) | copy-start | bytes 292
  22.0 31.3 %collective-permute-start = (bf16[50,512]{1,0:T(8,128)(2,1)S(1)}, bf16[50,512]{1,0:T(8,128)(2,1)S(1)}, u32[]{:S(2)}, u32[]{:S(2)}) collective-permute-start(bf16[50,512]{1,0:T(8,128)(2,1)S(1)} %pad_maximum_fusion), channel_id=1, source_target_pairs={{1,0},{2,1},{3,2},{4,3},{5,4},{6,5},{7,6},{9,8},{10,9},{11,10},{12... | collective-permute-start | bytes 153608 | tf_op jit(solution)/shard_map/ppermute | solution.py:461
  25.0 28.3 %collective-permute-start.1 = (bf16[50,512]{1,0:T(8,128)(2,1)S(1)}, bf16[50,512]{1,0:T(8,128)(2,1)S(1)}, u32[]{:S(2)}, u32[]{:S(2)}) collective-permute-start(bf16[50,512]{1,0:T(8,128)(2,1)S(1)} %slice.65), channel_id=1, source_target_pairs={{8,0},{9,1},{10,2},{11,3},{12,4},{13,5},{14,6},{15,7},{16,8},{17,9... | collective-permute-start | bytes 153608 | tf_op jit(solution)/shard_map/ppermute | solution.py:461
  26.3 26.9 %collective-permute-start.2 = (bf16[50,128]{1,0:T(8,128)(2,1)S(1)}, bf16[50,128]{1,0:T(8,128)(2,1)S(1)}, u32[]{:S(2)}, u32[]{:S(2)}) collective-permute-start(bf16[50,128]{1,0:T(8,128)(2,1)S(1)} %get-tuple-element.16), channel_id=1, source_target_pairs={{8,1},{9,2},{10,3},{11,4},{12,5},{13,6},{14,7},{16,9},{17,10},{18,... | collective-permute-start | bytes 38408 | tf_op jit(solution)/shard_map/ppermute | solution.py:461
  27.6 25.7 %collective-permute-start.3 = (bf16[50,128]{1,0:T(8,128)(2,1)S(1)}, bf16[50,128]{1,0:T(8,128)(2,1)S(1)}, u32[]{:S(2)}, u32[]{:S(2)}) collective-permute-start(bf16[50,128]{1,0:T(8,128)(2,1)S(1)} %get-tuple-element.15), channel_id=1, source_target_pairs={{0,9},{1,10},{2,11},{3,12},{4,13},{5,14},{6,15},{8,17},{9,18},{10,... | collective-permute-start | bytes 38408 | tf_op jit(solution)/shard_map/ppermute | solution.py:461
  33.2 5.4 %copy-start.5 = (f32[2,512,128]{2,1,0:T(8,128)S(1)}, f32[2,512,128]{2,1,0:T(8,128)}, u32[]{:S(2)}) copy-start(f32[2,512,128]{2,1,0:T(8,128)} %constant.29.clone.tw_ref) | copy-start | bytes 1572868
  33.3 5.4 %copy-start.8 = (bf16[2,256,256]{2,1,0:T(8,128)(2,1)S(1)}, bf16[2,256,256]{2,1,0:T(8,128)(2,1)}, u32[]{:S(2)}) copy-start(bf16[2,256,256]{2,1,0:T(8,128)(2,1)} %constant.25.clone.dft_ref.fwd_ref) | copy-start | bytes 786436
  33.3 5.4 %copy-start.9 = (bf16[2,256,256]{2,1,0:T(8,128)(2,1)S(1)}, bf16[2,256,256]{2,1,0:T(8,128)(2,1)}, u32[]{:S(2)}) copy-start(bf16[2,256,256]{2,1,0:T(8,128)(2,1)} %constant.28.clone.inv_ref) | copy-start | bytes 786436
  33.3 5.4 %copy-start.13 = (f32[16,128]{1,0:T(8,128)S(1)}, f32[16,128]{1,0:T(8,128)}, u32[]{:S(2)}) copy-start(f32[16,128]{1,0:T(8,128)} %constant.30.clone.lane_ref) | copy-start | bytes 24580
  43.8 9.6 %copy-start.10 = (bf16[576,48]{1,0:T(8,128)(2,1)S(1)}, bf16[576,48]{1,0:T(8,128)(2,1)}, u32[]{:S(2)}) copy-start(bf16[576,48]{1,0:T(8,128)(2,1)} %constant.27.clone.mix_ref) | copy-start | bytes 165892
  45.0 24.6 %all-to-all-start.1 = ((f16[128,24,128]{2,1,0:T(8,128)(2,1)}), f16[128,24,128]{2,1,0:T(8,128)(2,1)S(1)}, u32[]{:S(2)}, u32[]{:S(2)}) async-start(f16[128,24,128]{2,1,0:T(8,128)(2,1)} %bitcast.6), calls=%async_computation.1 | async-start | bytes 1572864 | tf_op jit(solution)/shard_map/all_to_all | solution.py:443
  59.7 15.6 %copy-start.2 = (f32[2048]{0:T(1024)S(1)}, f32[2048]{0:T(1024)}, u32[]{:S(2)}) copy-start(f32[2048]{0:T(1024)} %param.18) | copy-start | bytes 24580
  59.7 15.6 %copy-start.4 = (s32[2048]{0:T(1024)S(1)}, s32[2048]{0:T(1024)}, u32[]{:S(2)}) copy-start(s32[2048]{0:T(1024)} %param.19) | copy-start | bytes 24580
  59.8 15.6 %copy-start.6 = (bf16[2,256,256]{2,1,0:T(8,128)(2,1)S(1)}, bf16[2,256,256]{2,1,0:T(8,128)(2,1)}, u32[]{:S(2)}) copy-start(bf16[2,256,256]{2,1,0:T(8,128)(2,1)} %constant.31.clone.dft_ref) | copy-start | bytes 786436
  59.8 15.6 %copy-start.12 = (f32[2,64,128]{2,1,0:T(8,128)S(1)}, f32[2,64,128]{2,1,0:T(8,128)}, u32[]{:S(2)}) copy-start(f32[2,64,128]{2,1,0:T(8,128)} %constant.26.clone.tw_ref) | copy-start | bytes 196612
  59.8 15.6 %collective-permute-start.4 = (bf16[48,512]{1,0:T(8,128)(2,1)S(1)}, bf16[48,512]{1,0:T(8,128)(2,1)S(1)}, u32[]{:S(2)}, u32[]{:S(2)}) collective-permute-start(bf16[48,512]{1,0:T(8,128)(2,1)S(1)} %get-tuple-element.11), channel_id=1, source_target_pairs={{0,1},{1,2},{2,3},{3,4},{4,5},{5,6},{6,7},{8,9},{9,10},{10,11},{11... | collective-permute-start | bytes 147464 | tf_op jit(solution)/shard_map/ppermute | solution.py:505
  61.8 13.5 %collective-permute-start.5 = (bf16[48,512]{1,0:T(8,128)(2,1)S(1)}, bf16[48,512]{1,0:T(8,128)(2,1)S(1)}, u32[]{:S(2)}, u32[]{:S(2)}) collective-permute-start(bf16[48,512]{1,0:T(8,128)(2,1)S(1)} %get-tuple-element.12), channel_id=1, source_target_pairs={{0,8},{1,9},{2,10},{3,11},{4,12},{5,13},{6,14},{7,15},{8,16},{9,17... | collective-permute-start | bytes 147464 | tf_op jit(solution)/shard_map/ppermute | solution.py:505
  63.1 6.7 %collective-permute-start.6 = (bf16[48,128]{1,0:T(8,128)(2,1)S(1)}, bf16[48,128]{1,0:T(8,128)(2,1)S(1)}, u32[]{:S(2)}, u32[]{:S(2)}) collective-permute-start(bf16[48,128]{1,0:T(8,128)(2,1)S(1)} %get-tuple-element.13), channel_id=1, source_target_pairs={{1,8},{2,9},{3,10},{4,11},{5,12},{6,13},{7,14},{9,16},{10,17},{11,... | collective-permute-start | bytes 36872 | tf_op jit(solution)/shard_map/ppermute | solution.py:505
  68.1 7.2 %collective-permute-start.7 = (bf16[48,128]{1,0:T(8,128)(2,1)S(1)}, bf16[48,128]{1,0:T(8,128)(2,1)S(1)}, u32[]{:S(2)}, u32[]{:S(2)}) collective-permute-start(bf16[48,128]{1,0:T(8,128)(2,1)S(1)} %get-tuple-element.14), channel_id=1, source_target_pairs={{9,0},{10,1},{11,2},{12,3},{13,4},{14,5},{15,6},{17,8},{18,9},{19,... | collective-permute-start | bytes 36872 | tf_op jit(solution)/shard_map/ppermute | solution.py:505

commit v2 on v1

--- a/solution.py
+++ b/solution.py
@@ -82,8 +82,7 @@
     parts = np.zeros((2, 2, 2), np.float32)
     parts[0] = np.eye(2)
     parts[1] = np.array([[0.0, -1.0], [1.0, 0.0]])
-    full = np.einsum("fab,rop,gh->frogapb" + "h", table, parts, np.eye(ANG))
-    full = full.transpose(0, 1, 2, 3, 4, 5, 7, 6)
+    full = np.einsum("fab,rop,gh->froagpbh", table, parts, np.eye(ANG))
     return full.reshape(12 * CHAN, CHAN).astype(BF16)
 
 
@@ -137,7 +136,24 @@
     return [cadd(e, o) for e, o in zip(even, odd)] + [csub(e, o) for e, o in zip(even, odd)]
 
 
-def rows_kernel(x_ref, w_ref, cell_ref, dft_ref, tw_ref, out_ref, xt_ref, hot_ref, g_ref, b_ref):
+def pack_kernel(x_ref, jitter_ref, own_ref, one_ref, two_ref, four_ref, pack_ref):
+    for slab in range(12):
+        pack_ref[slab * 4 : slab * 4 + 4, :] = x_ref[slab].astype(F32)
+    pack_ref[CHAN : CHAN + 16, :] = jnp.zeros((16, WIDTH), F32)
+    pack_ref[CHAN : CHAN + 2, :] = jitter_ref[...].astype(F32)
+    own_ref[...] = pack_ref[...].astype(BF16)
+    for cluster in range(4):
+        one_ref[:, cluster * PIL : (cluster + 1) * PIL] = own_ref[:, cluster * 4 * PIL : (cluster * 4 + 1) * PIL]
+    two_ref[...] = own_ref[:, 0 : 4 * PIL]
+    four_ref[...] = own_ref[:, 15 * PIL : 16 * PIL]
+
+
+def rows_kernel(
+    x_ref, w_ref, cell_ref, dft_ref, tw_ref, out_ref, pack_ref, xb_ref, xt_ref, hot_ref, g_ref, b_ref
+):
+    for slab in range(12):
+        pack_ref[slab * 4 : slab * 4 + 4, :] = x_ref[slab].astype(F32)
+    xb_ref[...] = pack_ref[...].astype(BF16)
     cells = cell_ref[...]
     upper = cells >> 8
     weight = w_ref[...]
@@ -150,7 +166,7 @@
         hot_ref[1, block * 16 : block * 16 + 16, :] = jnp.where(hit, low, 0.0).astype(BF16)
     for part in range(32):
         mask = jnp.where(upper == part, 1.0, 0.0).astype(BF16)
-        xt_ref[part * CHAN : (part + 1) * CHAN, :] = x_ref[...] * mask
+        xt_ref[part * CHAN : (part + 1) * CHAN, :] = xb_ref[...] * mask
     for chunk in range(2):
         rows = slice(chunk * 768, (chunk + 1) * 768)
         piece = xt_ref[rows, :]
@@ -252,8 +268,8 @@
 
 
 def sample_kernel(
-    r_ref, w_ref, cell_ref, near_ref, one_ref, two_ref, three_ref, four_ref, dft_ref, tw_ref,
-    out_ref, v_ref, g_ref, f_ref,
+    r_ref, w_ref, cell_ref, near_ref, both_ref, side_ref, four_ref, dft_ref, tw_ref,
+    out_ref, v_ref, g_ref, f_ref, sum_ref,
 ):
     for part in range(2):
         for group in range(12):
@@ -305,14 +321,16 @@
             for part in range(8):
                 hit = jnp.broadcast_to(upper == quarter * 8 + part, (CHAN, 256))
                 total = total + jnp.where(hit, picked[part * CHAN : (part + 1) * CHAN, :], 0.0)
-        out_ref[:, lanes] = total * w_ref[:, lanes] + near_ref[:, lanes]
+        sum_ref[:, lanes] = total * w_ref[:, lanes] + near_ref[:, lanes]
     for cluster in range(4):
         lanes = slice(cluster * 4 * PIL, (cluster * 4 + 1) * PIL)
-        out_ref[:, lanes] += one_ref[:, cluster * PIL : (cluster + 1) * PIL].astype(F32)
+        sum_ref[:, lanes] += both_ref[:, cluster * PIL : (cluster + 1) * PIL].astype(F32)
         lanes = slice(cluster * PIL, (cluster + 1) * PIL)
-        out_ref[:, lanes] += two_ref[:, cluster * PIL : (cluster + 1) * PIL].astype(F32)
-    out_ref[:, 3 * PIL : 4 * PIL] += three_ref[...].astype(F32)
-    out_ref[:, 15 * PIL : 16 * PIL] += four_ref[...].astype(F32)
+        sum_ref[:, lanes] += both_ref[:, (cluster + 4) * PIL : (cluster + 5) * PIL].astype(F32)
+    sum_ref[:, 3 * PIL : 4 * PIL] += side_ref[:, 4 * PIL : 5 * PIL].astype(F32)
+    sum_ref[:, 15 * PIL : 16 * PIL] += four_ref[...].astype(F32)
+    for slab in range(12):
+        out_ref[slab] = sum_ref[slab * 4 : slab * 4 + 4, :]
 
 
 def taylor(count, first):
@@ -327,16 +345,14 @@
 
 
 def near_kernel(
-    list_ref, own_ref, one_ref, two_ref, three_ref, four_ref, own_pos, one_pos, two_pos, three_pos,
-    four_pos, mix_ref, near_ref, back_one, back_two, back_three, back_four, all_ref, pos_ref, sum_ref,
+    list_ref, own_ref, both_ref, side_ref, four_ref, mix_ref,
+    near_ref, back_one, back_side, back_four, all_ref, pos_ref, sum_ref,
 ):
-    all_ref[:, 0:WIDTH] = own_ref[...]
-    pos_ref[0:2, 0:WIDTH] = own_pos[...].astype(F32)
-    start = WIDTH
-    for data, pos in ((one_ref, one_pos), (two_ref, two_pos), (three_ref, three_pos), (four_ref, four_pos)):
+    start = 0
+    for data in (own_ref[...], both_ref[...], side_ref[:, 3 * PIL : 4 * PIL], four_ref[...]):
         width = data.shape[1]
-        all_ref[:, start : start + width] = data[...]
-        pos_ref[0:2, start : start + width] = pos[...].astype(F32)
+        all_ref[:, start : start + width] = data[0:CHAN, :]
+        pos_ref[:, start : start + width] = data[CHAN : CHAN + 16, :].astype(F32)
         start += width
     sum_ref[...] = jnp.zeros_like(sum_ref)
     wide_pos = list_ref[24]
@@ -355,7 +371,7 @@
     def mixed(values):
         return dot(mix_ref[...], values).astype(BF16)
 
-    def one_slot(slot, carry):
+    def one_slot(slot):
         direction = list_ref[slot * 3]
         own = list_ref[slot * 3 + 1]
         far = list_ref[slot * 3 + 2]
@@ -374,10 +390,12 @@
         square = delta_x * delta_x + delta_y * delta_y
         over = lax.rsqrt(square)
         distance = square * over
-        turns = (distance - jnp.round(distance)) * (2.0 * math.pi)
-        turns_square = turns * turns
-        cosine = horner(taylor(10, 0), turns_square)
-        sine = horner(taylor(10, 1), turns_square) * turns
+        half_turns = (distance - jnp.round(distance)) * math.pi
+        half_square = half_turns * half_turns
+        half_sine = horner(taylor(7, 1), half_square) * half_turns
+        half_cosine = horner(taylor(8, 0), half_square)
+        cosine = 1.0 - 2.0 * half_sine * half_sine
+        sine = 2.0 * half_sine * half_cosine
         unit_x = delta_x * over
         unit_y = delta_y * over
         inverse = over * (1.0 / (2.0 * math.pi))
@@ -391,8 +409,7 @@
         unit_yy = unit_y * unit_y
         own_mixed = mixed(all_ref[:, own_window])
         far_mixed = mixed(all_ref[:, far_window])
-        to_own = jnp.zeros((CHAN, PIL), F32)
-        to_far = jnp.zeros((CHAN, PIL), F32)
+        fields = []
         for field in range(6):
             for part in range(2):
                 value = (
@@ -403,17 +420,25 @@
                     term_c[part] * unit_x,
                     term_c[part] * unit_y,
                 )[field].astype(BF16)
-                rows = slice((field * 2 + part) * CHAN, (field * 2 + part + 1) * CHAN)
-                to_own = to_own + dot(far_mixed[rows], value, 1, 1)
-                to_far = to_far + dot(own_mixed[rows], value, 1, 0)
-        sum_ref[:, own_window] += to_own
-        sum_ref[:, far_window] += to_far
+                fields.append(value)
+        far_wide = jnp.concatenate([far_mixed[k * CHAN : (k + 1) * CHAN] for k in range(12)], axis=1)
+        own_wide = jnp.concatenate([own_mixed[k * CHAN : (k + 1) * CHAN] for k in range(12)], axis=1)
+        to_own = dot(far_wide, jnp.concatenate(fields, axis=1), 1, 1)
+        to_far = dot(own_wide, jnp.concatenate(fields, axis=0), 1, 0)
+        active = jnp.where(slot < used, 1.0, 0.0)
+        return own_window, far_window, to_own * active, to_far * active
+
+    def some_slots(step, carry):
+        results = [one_slot(step * 4 + place) for place in range(4)]
+        for own_window, far_window, to_own, to_far in results:
+            sum_ref[:, own_window] += to_own
+            sum_ref[:, far_window] += to_far
         return carry
 
-    lax.fori_loop(0, used, one_slot, 0)
+    lax.fori_loop(0, (used + 3) // 4, some_slots, 0)
     near_ref[...] = sum_ref[:, 0:WIDTH]
     start = WIDTH
-    for back in (back_one, back_two, back_three, back_four):
+    for back in (back_one, back_side, back_four):
         width = back.shape[1]
         back[...] = sum_ref[:, start : start + width].astype(BF16)
         start += width
@@ -423,18 +448,98 @@
     return jax.ShapeDtypeStruct(dims, kind)
 
 
-def steps(move_wide, move_narrow):
+def shift(value, move_wide, move_narrow):
     pairs = []
     for wide in range(N_WIDE):
         for narrow in range(N_NARROW):
-            to_wide, to_narrow = wide + move_wide, narrow + move_narrow
-            if 0 <= to_wide < N_WIDE and 0 <= to_narrow < N_NARROW:
+            to_wide, to_narrow = wide + move_wide, (narrow + move_narrow) % N_NARROW
+            if 0 <= to_wide < N_WIDE:
                 pairs.append((wide * N_NARROW + narrow, to_wide * N_NARROW + to_narrow))
-    return pairs
-
-
-MOVES = ((0, 1), (1, 0), (1, -1), (-1, -1))
+    return lax.ppermute(value, AXES, pairs)
+
+
 PARAMS = pltpu.CompilerParams(vmem_limit_bytes=48 * MIB)
+
+
+def cost(flops, size):
+    return pl.CostEstimate(flops=flops, bytes_accessed=size, transcendentals=0)
+
+
+def pack_call(x, jitter):
+    return pl.pallas_call(
+        pack_kernel,
+        out_shape=[
+            shape((64, WIDTH), BF16),
+            shape((64, 4 * PIL), BF16),
+            shape((64, 4 * PIL), BF16),
+            shape((64, PIL), BF16),
+        ],
+        scratch_shapes=[pltpu.VMEM((64, WIDTH), F32)],
+        compiler_params=PARAMS,
+        cost_estimate=cost(1_000_000, MIB // 2),
+    )(x, jitter)
+
+
+def rows_call(x, w, cell, forward, row_table):
+    return pl.pallas_call(
+        rows_kernel,
+        out_shape=shape((DEVICES * HALF, 128)),
+        scratch_shapes=[
+            pltpu.VMEM((CHAN, WIDTH), F32),
+            pltpu.VMEM((CHAN, WIDTH), BF16),
+            pltpu.VMEM((1536, WIDTH), BF16),
+            pltpu.VMEM((2, 256, WIDTH), BF16),
+            pltpu.VMEM((1536, 256), F32),
+            pltpu.VMEM((1536, 256), F32),
+        ],
+        compiler_params=PARAMS,
+        cost_estimate=cost(3_800_000_000, 4 * MIB),
+    )(x, w, cell, forward, row_table)
+
+
+def near_call(spots, own, both, side, four, mixing):
+    return pl.pallas_call(
+        near_kernel,
+        in_specs=[pl.BlockSpec(memory_space=pltpu.SMEM)] + [pl.BlockSpec(memory_space=pltpu.VMEM)] * 5,
+        out_shape=[
+            shape((CHAN, WIDTH)),
+            shape((CHAN, 4 * PIL), BF16),
+            shape((CHAN, 5 * PIL), BF16),
+            shape((CHAN, PIL), BF16),
+        ],
+        scratch_shapes=[
+            pltpu.VMEM((CHAN, WIDTH + HALO * PIL), BF16),
+            pltpu.VMEM((16, WIDTH + HALO * PIL), F32),
+            pltpu.VMEM((CHAN, WIDTH + HALO * PIL), F32),
+        ],
+        compiler_params=PARAMS,
+        cost_estimate=cost(8_000_000_000, 4 * MIB),
+    )(spots, own, both, side, four, mixing)
+
+
+def columns_call(columns, transfer, forward, backward, column_table, lane_table):
+    return pl.pallas_call(
+        columns_kernel,
+        out_shape=shape((DEVICES * HALF, 128)),
+        scratch_shapes=[pltpu.VMEM((256, 1536), F32), pltpu.VMEM((256, 1536), F32)],
+        compiler_params=PARAMS,
+        cost_estimate=cost(2_000_000_000, 6 * MIB),
+    )(columns, transfer, forward, backward, column_table, lane_table)
+
+
+def sample_call(rows, w, cell, near, both, side, four, backward, row_table):
+    return pl.pallas_call(
+        sample_kernel,
+        out_shape=shape((12, 4, WIDTH)),
+        scratch_shapes=[
+            pltpu.VMEM((1536, 256), F32),
+            pltpu.VMEM((1536, 256), F32),
+            pltpu.VMEM((2, 1536, 256), BF16),
+            pltpu.VMEM((CHAN, WIDTH), F32),
+        ],
+        compiler_params=PARAMS,
+        cost_estimate=cost(3_800_000_000, 4 * MIB),
+    )(rows, w, cell, near, both, side, four, backward, row_table)
 
 
 def exchange(message):
@@ -446,34 +551,30 @@
 
 
 def local(incident, jitter, weights, cells, pair_list, pair_count, kernel):
-    x = incident.reshape(CHAN, WIDTH)
+    x = incident.transpose(0, 2, 1, 3).reshape(12, ANG, WIDTH)
     w = weights.reshape(1, WIDTH)
     cell = cells.reshape(1, WIDTH)
-
-    packed = jnp.concatenate([x, jitter], axis=0)
-    pieces = (
-        jnp.concatenate([packed[:, c * PIL : (c + 1) * PIL] for c in (0, 4, 8, 12)], axis=1),
-        packed[:, 0 : 4 * PIL],
-        packed[:, 3 * PIL : 4 * PIL],
-        packed[:, 15 * PIL : 16 * PIL],
+    forward = jnp.asarray(dft_table(-1.0))
+    row_table = jnp.asarray(row_twiddle())
+
+    message = rows_call(x, w, cell, forward, row_table)
+    columns = exchange(message)
+    own, one, two, four = pack_call(x, jitter)
+    side = shift(two, -1, 1)
+    four = shift(four, 1, 1)
+    both = shift(jnp.concatenate([one, side], axis=1), 0, -1)
+
+    transfer = kernel.reshape(2, 2, 4, 128, 8).transpose(0, 2, 3, 1, 4)
+    transfer = jnp.broadcast_to(transfer[..., None], (2, 4, 128, 2, 8, 8)).reshape(2, 512, 128)
+    message = columns_call(
+        columns,
+        transfer,
+        forward,
+        jnp.asarray(dft_table(1.0, 1.0 / 1048576)),
+        jnp.asarray(column_twiddle()),
+        jnp.asarray(lane_twiddle()),
     )
-    halo = [
-        lax.ppermute(piece, AXES, steps(-wide, -narrow)) for piece, (wide, narrow) in zip(pieces, MOVES)
-    ]
-
-    message = pl.pallas_call(
-        rows_kernel,
-        out_shape=shape((DEVICES * HALF, 128)),
-        scratch_shapes=[
-            pltpu.VMEM((1536, WIDTH), BF16),
-            pltpu.VMEM((2, 256, WIDTH), BF16),
-            pltpu.VMEM((1536, 256), F32),
-            pltpu.VMEM((1536, 256), F32),
-        ],
-        compiler_params=PARAMS,
-        cost_estimate=pl.CostEstimate(flops=3_800_000_000, bytes_accessed=4 * MIB, transcendentals=0),
-    )(x, w, cell, jnp.asarray(dft_table(-1.0)), jnp.asarray(row_twiddle()))
-    columns = exchange(message)
+    rows = exchange(message)
 
     spots = jnp.concatenate(
         [
@@ -483,58 +584,12 @@
             pair_count,
         ]
     )
-    near, *returns = pl.pallas_call(
-        near_kernel,
-        in_specs=[pl.BlockSpec(memory_space=pltpu.SMEM)] + [pl.BlockSpec(memory_space=pltpu.VMEM)] * 11,
-        out_shape=[
-            shape((CHAN, WIDTH)),
-            shape((CHAN, 4 * PIL), BF16),
-            shape((CHAN, 4 * PIL), BF16),
-            shape((CHAN, PIL), BF16),
-            shape((CHAN, PIL), BF16),
-        ],
-        scratch_shapes=[
-            pltpu.VMEM((CHAN, WIDTH + HALO * PIL), BF16),
-            pltpu.VMEM((8, WIDTH + HALO * PIL), F32),
-            pltpu.VMEM((CHAN, WIDTH + HALO * PIL), F32),
-        ],
-        compiler_params=PARAMS,
-        cost_estimate=pl.CostEstimate(flops=8_000_000_000, bytes_accessed=4 * MIB, transcendentals=0),
-    )(spots, x, *[h[:CHAN] for h in halo], jitter, *[h[CHAN:] for h in halo], jnp.asarray(mixing_table()))
-    back = [
-        lax.ppermute(piece, AXES, steps(wide, narrow)) for piece, (wide, narrow) in zip(returns, MOVES)
-    ]
-
-    transfer = kernel.reshape(2, 2, 4, 128, 8).transpose(0, 2, 3, 1, 4)
-    transfer = jnp.broadcast_to(transfer[..., None], (2, 4, 128, 2, 8, 8)).reshape(2, 512, 128)
-    message = pl.pallas_call(
-        columns_kernel,
-        out_shape=shape((DEVICES * HALF, 128)),
-        scratch_shapes=[pltpu.VMEM((256, 1536), F32), pltpu.VMEM((256, 1536), F32)],
-        compiler_params=PARAMS,
-        cost_estimate=pl.CostEstimate(flops=2_000_000_000, bytes_accessed=6 * MIB, transcendentals=0),
-    )(
-        columns,
-        transfer,
-        jnp.asarray(dft_table(-1.0)),
-        jnp.asarray(dft_table(1.0, 1.0 / 1048576)),
-        jnp.asarray(column_twiddle()),
-        jnp.asarray(lane_twiddle()),
-    )
-    rows = exchange(message)
-
-    coupled = pl.pallas_call(
-        sample_kernel,
-        out_shape=shape((CHAN, WIDTH)),
-        scratch_shapes=[
-            pltpu.VMEM((1536, 256), F32),
-            pltpu.VMEM((1536, 256), F32),
-            pltpu.VMEM((2, 1536, 256), BF16),
-        ],
-        compiler_params=PARAMS,
-        cost_estimate=pl.CostEstimate(flops=3_800_000_000, bytes_accessed=4 * MIB, transcendentals=0),
-    )(rows, w, cell, near, *back, jnp.asarray(dft_table(1.0)), jnp.asarray(row_twiddle()))
-    return coupled.reshape(2, ANG, 6, WIDTH)
+    near, one, side, four = near_call(spots, own, both, side, four, jnp.asarray(mixing_table()))
+    side = shift(side, 1, -1)
+    four = shift(four, -1, -1)
+    both = shift(jnp.concatenate([one, side[:, 0 : 4 * PIL]], axis=1), 0, 1)
+    coupled = sample_call(rows, w, cell, near, both, side, four, jnp.asarray(dft_table(1.0)), row_table)
+    return coupled.reshape(2, 6, ANG, WIDTH).transpose(0, 2, 1, 3)
 
 
 def solution(mesh):

time: 82.7 us -> 75.6 us (0.914)
  the two profiles are of different devices: /device:TPU:1 before, /device:TPU:4 now
where the time goes in v2:
time: 75.6 us; the launch traced here: 75.1 us
  starting transfers between devices  34.7 us (46%)
  Pallas kernels  20.4 us (27%)
  waiting for transfers between devices  11.2 us (15%)
  local copies, waits for them, and re-layouts  4.85 us (6%)
  other arithmetic  2.86 us (4%)
  between operations  1.09 us (1%)
    ppermute x6, starting transfers between devices, shift(): return lax.ppermute(value, AXES, pairs)  17.9 us
    all_to_all x2, starting transfers between devices, exchange(): code = lax.all_to_all(code, AXES, split_axis=0, concat_axis=0, tiled=True)  16.8 us
    ppermute x6, waiting for transfers between devices, shift(): return lax.ppermute(value, AXES, pairs)  11 us
    pallas_call x1, Pallas kernels, sample_call(): pl.pallas_call(sample_kernel, out_shape=shape((12, 4, WIDTH)), scratch_sh...  6.45 us
    pallas_call x1, Pallas kernels, columns_call(): pl.pallas_call(columns_kernel, out_shape=shape((DEVICES * HALF, 128)), sc...  5.11 us
    pallas_call x1, Pallas kernels, rows_call(): pl.pallas_call(rows_kernel, out_shape=shape((DEVICES * HALF, 128)), scrat...  4.86 us
    unnamed x37, local copies, waits for them, and re-layouts  4.27 us
    pallas_call x1, Pallas kernels, near_call(): pl.pallas_call(near_kernel, in_specs=[pl.BlockSpec(memory_space=pltpu.SME...  3.9 us
  transfers between devices with their start and end apart: 8, of which 4 were waited for; matrix products, arithmetic and copies ran while one was open for 3% of the time, Pallas kernels for 12%

profile of v2, /device:TPU:4, one launch (start us, length us, event | category | flops | bytes accessed | tf_op | source)
XLA Modules:
  0.0 75.1 jit_solution(5566489459880279301)
XLA Ops:
  0.0 0.9 %copy-done = bf16[2,4,6,2048]{3,1,2,0:T(4,128)(2,1)S(1)} copy-done((bf16[2,4,6,2048]{3,1,2,0:T(4,128)(2,1)S(1)}, bf16[2,4,6,2048]{3,1,2,0:T(4,128)(2,1)}, u32[]{:S(2)}) %copy-start) | copy-done | bytes 196632
  0.9 0.7 copy-done.3
  1.6 0.7 copy-done.5
  2.3 0.9 %copy-done.9 = bf16[2,256,256]{2,1,0:T(8,128)(2,1)S(1)} copy-done((bf16[2,256,256]{2,1,0:T(8,128)(2,1)S(1)}, bf16[2,256,256]{2,1,0:T(8,128)(2,1)}, u32[]{:S(2)}) %copy-start.9) | copy-done | bytes 262168
  3.3 0.8 %copy-done.13 = f32[2,64,128]{2,1,0:T(8,128)S(1)} copy-done((f32[2,64,128]{2,1,0:T(8,128)S(1)}, f32[2,64,128]{2,1,0:T(8,128)}, u32[]{:S(2)}) %copy-start.13) | copy-done | bytes 65560
  4.1 4.9 %shard_map.136 = f32[3072,128]{1,0:T(8,128)S(1)} custom-call(bf16[12,4,2048]{2,1,0:T(4,128)(2,1)S(1)} %bitcast.21, f32[1,2048]{1,0:T(1,128)S(1)} %bitcast.23, s32[1,2048]{1,0:T(1,128)S(1)} %bitcast.25, bf16[2,256,256]{2,1,0:T(8,128)(2,1)S(1)} %copy-done.9, f32[2,64,128]{2,1,0:T(8,128)S(1)} %copy-done.13), custom_call_target="tpu_custom_call" | custom-call | flops 3800000000 | bytes 4194304 | tf_op jit(solution)/shard_map/pallas_call | solution.py:484
  9.0 0.0 copy-start.1
  9.0 0.0 copy-start.2
  9.0 0.0 copy-start.16
  9.0 1.2 %multiply_convert_fusion.1 = f16[3072,128]{1,0:T(8,128)(2,1)} fusion(f32[3072,128]{1,0:T(8,128)S(1)} %shard_map.136), kind=kLoop, calls=%fused_computation.3 | loop fusion | flops 1572864 | bytes 2359296 | tf_op jit(solution)/shard_map/convert_element_type | solution.py:547
  10.2 10.5 %all-to-all-start = ((f16[128,24,128]{2,1,0:T(8,128)(2,1)}), f16[128,24,128]{2,1,0:T(8,128)(2,1)S(1)}, u32[]{:S(2)}, u32[]{:S(2)}) async-start(f16[128,24,128]{2,1,0:T(8,128)(2,1)} %bitcast.4), calls=%async_computation | async-start | bytes 1572864 | tf_op jit(solution)/shard_map/all_to_all | solution.py:548
  20.7 0.0 copy-start.17
  20.8 0.1 shard_map.138
  20.9 4.4 %collective-permute-start = (bf16[64,512]{1,0:T(8,128)(2,1)S(1)}, bf16[64,512]{1,0:T(8,128)(2,1)S(1)}, u32[]{:S(2)}, u32[]{:S(2)}) collective-permute-start(bf16[64,512]{1,0:T(8,128)(2,1)S(1)} %get-tuple-element.15), channel_id=1, source_target_pairs={{8,1},{9,2},{10,3},{11,4},{12,5},{13,6},{14,7},{15,0},{16,9},{17,1... | collective-permute-start | bytes 196616 | tf_op jit(solution)/shard_map/ppermute | solution.py:458
  25.3 2.2 %collective-permute-start.2 = (bf16[64,128]{1,0:T(8,128)(2,1)S(1)}, bf16[64,128]{1,0:T(8,128)(2,1)S(1)}, u32[]{:S(2)}, u32[]{:S(2)}) collective-permute-start(bf16[64,128]{1,0:T(8,128)(2,1)S(1)} %get-tuple-element.16), channel_id=1, source_target_pairs={{0,9},{1,10},{2,11},{3,12},{4,13},{5,14},{6,15},{7,8},{8,17},{9,18... | collective-permute-start | bytes 49160 | tf_op jit(solution)/shard_map/ppermute | solution.py:458
  27.5 0.1 broadcast_in_dim.2
  27.6 0.2 reshape.43
  27.8 0.2 copy.18.kern_ref
  28.0 0.0 copy-start.7
  28.0 0.0 copy-start.10
  28.1 0.0 copy-start.11
  28.1 0.0 copy-start.15
  28.8 0.1 copy.19
  28.9 0.1 reshape.45
  29.0 0.1 pad_add_fusion.list_ref
  29.1 6.1 %collective-permute-done.side_ref = bf16[64,512]{1,0:T(8,128)(2,1)S(1)} collective-permute-done((bf16[64,512]{1,0:T(8,128)(2,1)S(1)}, bf16[64,512]{1,0:T(8,128)(2,1)S(1)}, u32[]{:S(2)}, u32[]{:S(2)}) %collective-permute-start) | collective-permute-done | bytes 65568 | tf_op jit(solution)/shard_map/ppermute | solution.py:458
  35.2 0.3 collective-permute-start.1
  35.5 0.1 all-to-all-done
  35.6 0.2 abs_multiply_fusion.1
  35.9 5.1 %shard_map.137 = f32[3072,128]{1,0:T(8,128)S(1)} custom-call(f32[3072,128]{1,0:T(8,128)S(1)} %bitcast.20, f32[2,512,128]{2,1,0:T(8,128)S(1)} %copy.18.kern_ref, bf16[2,256,256]{2,1,0:T(8,128)(2,1)S(1)} %copy-done.10, bf16[2,256,256]{2,1,0:T(8,128)(2,1)S(1)} %copy-done.11, f32[2,512,128]{2,1,0:T(8,128)S(1)} %copy-done.7, f32[16,128]{1,0:T(8,128)S(1)} %copy-done.15), custom_call_target="tpu_custom_call" | custom-call | flops 2000000000 | bytes 6291456 | tf_op jit(solution)/shard_map/pallas_call | solution.py:521
  41.0 0.0 copy-start.12
  41.0 1.2 %multiply_convert_fusion = f16[3072,128]{1,0:T(8,128)(2,1)} fusion(f32[3072,128]{1,0:T(8,128)S(1)} %shard_map.137), kind=kLoop, calls=%fused_computation.2 | loop fusion | flops 1572864 | bytes 2359296 | tf_op jit(solution)/shard_map/convert_element_type | solution.py:547
  42.2 6.3 %all-to-all-start.1 = ((f16[128,24,128]{2,1,0:T(8,128)(2,1)}), f16[128,24,128]{2,1,0:T(8,128)(2,1)S(1)}, u32[]{:S(2)}, u32[]{:S(2)}) async-start(f16[128,24,128]{2,1,0:T(8,128)(2,1)} %bitcast.8), calls=%async_computation.1 | async-start | bytes 1572864 | tf_op jit(solution)/shard_map/all_to_all | solution.py:548
  48.6 0.0 collective-permute-done.1.both_ref
  48.6 3.9 %shard_map.139 = (f32[48,2048]{1,0:T(8,128)S(1)}, bf16[48,512]{1,0:T(8,128)(2,1)S(1)}, bf16[48,640]{1,0:T(8,128)(2,1)S(1)}, bf16[48,128]{1,0:T(8,128)(2,1)S(1)}) custom-call(s32[27]{0:T(128)S(1)} %pad_add_fusion.list_ref, bf16[64,2048]{1,0:T(8,128)(2,1)S(1)} %get-tuple-element.13.own_ref, bf16[64,1024]{1,0:T(8,128)(2,1)S(1)} %collective-permute-done.1.both_ref, ...), custom_call_target="tpu_custom_call" | custom-call | flops 8000000000 | bytes 4194304 | tf_op jit(solution)/shard_map/pallas_call | solution.py:501
  52.5 0.0 copy-start.4
  52.5 0.0 copy-start.6
  52.5 0.0 copy-start.8
  52.5 0.0 copy-start.14
  52.5 4.5 %collective-permute-start.3 = (bf16[48,640]{1,0:T(8,128)(2,1)S(1)}, bf16[48,640]{1,0:T(8,128)(2,1)S(1)}, u32[]{:S(2)}, u32[]{:S(2)}) collective-permute-start(bf16[48,640]{1,0:T(8,128)(2,1)S(1)} %get-tuple-element.19), channel_id=1, source_target_pairs={{0,15},{1,8},{2,9},{3,10},{4,11},{5,12},{6,13},{7,14},{8,23},{9,16... | collective-permute-start | bytes 184328 | tf_op jit(solution)/shard_map/ppermute | solution.py:458
  57.1 6.3 %collective-permute-start.5 = (bf16[48,128]{1,0:T(8,128)(2,1)S(1)}, bf16[48,128]{1,0:T(8,128)(2,1)S(1)}, u32[]{:S(2)}, u32[]{:S(2)}) collective-permute-start(bf16[48,128]{1,0:T(8,128)(2,1)S(1)} %get-tuple-element.20), channel_id=1, source_target_pairs={{8,7},{9,0},{10,1},{11,2},{12,3},{13,4},{14,5},{15,6},{16,15},{17,... | collective-permute-start | bytes 36872 | tf_op jit(solution)/shard_map/ppermute | solution.py:458
  63.3 0.0 collective-permute-done.3.side_ref
  63.4 0.2 collective-permute-start.4
  63.5 0.0 all-to-all-done.1
  63.5 0.2 abs_multiply_fusion
  63.7 0.8 %collective-permute-done.5.four_ref = bf16[48,128]{1,0:T(8,128)(2,1)S(1)} collective-permute-done((bf16[48,128]{1,0:T(8,128)(2,1)S(1)}, bf16[48,128]{1,0:T(8,128)(2,1)S(1)}, u32[]{:S(2)}, u32[]{:S(2)}) %collective-permute-start.5) | collective-permute-done | bytes 12320 | tf_op jit(solution)/shard_map/ppermute | solution.py:458
  64.5 4.1 %collective-permute-done.4.both_ref = bf16[48,1024]{1,0:T(8,128)(2,1)S(1)} collective-permute-done((bf16[48,1024]{1,0:T(8,128)(2,1)S(1)}, bf16[48,1024]{1,0:T(8,128)(2,1)S(1)}, u32[]{:S(2)}, u32[]{:S(2)}) %collective-permute-start.4) | collective-permute-done | bytes 98336 | tf_op jit(solution)/shard_map/ppermute | solution.py:458
  68.7 6.5 %shard_map.140 = f32[12,4,2048]{2,1,0:T(4,128)} custom-call(f32[3072,128]{1,0:T(8,128)S(1)} %bitcast.19, f32[1,2048]{1,0:T(1,128)S(1)} %bitcast.24, s32[1,2048]{1,0:T(1,128)S(1)} %bitcast.26, f32[48,2048]{1,0:T(8,128)S(1)} %get-tuple-element.17.near_ref, bf16[48,1024]{1,0:T(8,128)(2,1)S(1)} %collective-permute-done.4.both_ref, ...), custom_call_target="tpu_custom_call" | custom-call | flops 3800000000 | bytes 4194304 | tf_op jit(solution)/shard_map/pallas_call | solution.py:531
  (23 shorter events, 0.1 us)
Async XLA Ops:
  0.0 0.9 %copy-start = (bf16[2,4,6,2048]{3,1,2,0:T(4,128)(2,1)S(1)}, bf16[2,4,6,2048]{3,1,2,0:T(4,128)(2,1)}, u32[]{:S(2)}) copy-start(bf16[2,4,6,2048]{3,1,2,0:T(4,128)(2,1)} %param.14) | copy-start | bytes 589828
  0.9 0.7 copy-start.3
  1.6 0.7 copy-start.5
  2.3 0.9 %copy-start.9 = (bf16[2,256,256]{2,1,0:T(8,128)(2,1)S(1)}, bf16[2,256,256]{2,1,0:T(8,128)(2,1)}, u32[]{:S(2)}) copy-start(bf16[2,256,256]{2,1,0:T(8,128)(2,1)} %constant.25.clone.dft_ref.fwd_ref) | copy-start | bytes 786436
  3.3 0.8 %copy-start.13 = (f32[2,64,128]{2,1,0:T(8,128)S(1)}, f32[2,64,128]{2,1,0:T(8,128)}, u32[]{:S(2)}) copy-start(f32[2,64,128]{2,1,0:T(8,128)} %constant.26.clone.tw_ref) | copy-start | bytes 196612
  9.0 11.7 %copy-start.1 = (bf16[2,4,6,2048]{3,1,2,0:T(4,128)(2,1)S(1)}, bf16[2,4,6,2048]{3,1,2,0:T(4,128)(2,1)}, u32[]{:S(2)}) copy-start(bf16[2,4,6,2048]{3,1,2,0:T(4,128)(2,1)} %param.14) | copy-start | bytes 589828
  9.0 11.7 %copy-start.2 = (bf16[2,2048]{1,0:T(2,128)(2,1)S(1)}, bf16[2,2048]{1,0:T(2,128)(2,1)}, u32[]{:S(2)}) copy-start(bf16[2,2048]{1,0:T(2,128)(2,1)} %jitter_ref.1) | copy-start | bytes 24580
  9.0 18.5 %copy-start.16 = (f32[2,1024,8]{1,2,0:T(8,128)S(1)}, f32[2,1024,8]{1,2,0:T(8,128)}, u32[]{:S(2)}) copy-start(f32[2,1024,8]{1,2,0:T(8,128)} %param.20) | copy-start | bytes 196612
  10.2 25.4 %all-to-all-start = ((f16[128,24,128]{2,1,0:T(8,128)(2,1)}), f16[128,24,128]{2,1,0:T(8,128)(2,1)S(1)}, u32[]{:S(2)}, u32[]{:S(2)}) async-start(f16[128,24,128]{2,1,0:T(8,128)(2,1)} %bitcast.4), calls=%async_computation | async-start | bytes 1572864 | tf_op jit(solution)/shard_map/all_to_all | solution.py:548
  20.7 8.1 %copy-start.17 = (s32[1,8,3]{1,0,2:T(1,128)S(1)}, s32[1,8,3]{1,0,2:T(1,128)}, u32[]{:S(2)}) copy-start(s32[1,8,3]{1,0,2:T(1,128)} %param.18) | copy-start | bytes 292
  20.9 14.3 %collective-permute-start = (bf16[64,512]{1,0:T(8,128)(2,1)S(1)}, bf16[64,512]{1,0:T(8,128)(2,1)S(1)}, u32[]{:S(2)}, u32[]{:S(2)}) collective-permute-start(bf16[64,512]{1,0:T(8,128)(2,1)S(1)} %get-tuple-element.15), channel_id=1, source_target_pairs={{8,1},{9,2},{10,3},{11,4},{12,5},{13,6},{14,7},{15,0},{16,9},{17,1... | collective-permute-start | bytes 196616 | tf_op jit(solution)/shard_map/ppermute | solution.py:458
  25.3 23.3 %collective-permute-start.2 = (bf16[64,128]{1,0:T(8,128)(2,1)S(1)}, bf16[64,128]{1,0:T(8,128)(2,1)S(1)}, u32[]{:S(2)}, u32[]{:S(2)}) collective-permute-start(bf16[64,128]{1,0:T(8,128)(2,1)S(1)} %get-tuple-element.16), channel_id=1, source_target_pairs={{0,9},{1,10},{2,11},{3,12},{4,13},{5,14},{6,15},{7,8},{8,17},{9,18... | collective-permute-start | bytes 49160 | tf_op jit(solution)/shard_map/ppermute | solution.py:458
  28.0 7.8 %copy-start.7 = (f32[2,512,128]{2,1,0:T(8,128)S(1)}, f32[2,512,128]{2,1,0:T(8,128)}, u32[]{:S(2)}) copy-start(f32[2,512,128]{2,1,0:T(8,128)} %constant.28.clone.tw_ref) | copy-start | bytes 1572868
  28.0 7.8 %copy-start.10 = (bf16[2,256,256]{2,1,0:T(8,128)(2,1)S(1)}, bf16[2,256,256]{2,1,0:T(8,128)(2,1)}, u32[]{:S(2)}) copy-start(bf16[2,256,256]{2,1,0:T(8,128)(2,1)} %constant.25.clone.dft_ref.fwd_ref) | copy-start | bytes 786436
  28.1 7.8 %copy-start.11 = (bf16[2,256,256]{2,1,0:T(8,128)(2,1)S(1)}, bf16[2,256,256]{2,1,0:T(8,128)(2,1)}, u32[]{:S(2)}) copy-start(bf16[2,256,256]{2,1,0:T(8,128)(2,1)} %constant.27.clone.inv_ref) | copy-start | bytes 786436
  28.1 7.8 %copy-start.15 = (f32[16,128]{1,0:T(8,128)S(1)}, f32[16,128]{1,0:T(8,128)}, u32[]{:S(2)}) copy-start(f32[16,128]{1,0:T(8,128)} %constant.29.clone.lane_ref) | copy-start | bytes 24580
  35.2 13.4 %collective-permute-start.1 = (bf16[64,1024]{1,0:T(8,128)(2,1)S(1)}, bf16[64,1024]{1,0:T(8,128)(2,1)S(1)}, u32[]{:S(2)}, u32[]{:S(2)}) collective-permute-start(bf16[64,1024]{1,0:T(8,128)(2,1)S(1)} %pad_maximum_fusion), channel_id=1, source_target_pairs={{0,7},{1,0},{2,1},{3,2},{4,3},{5,4},{6,5},{7,6},{8,15},{9,8},{10,9... | collective-permute-start | bytes 393224 | tf_op jit(solution)/shard_map/ppermute | solution.py:458
  41.0 7.6 %copy-start.12 = (bf16[576,48]{1,0:T(8,128)(2,1)S(1)}, bf16[576,48]{1,0:T(8,128)(2,1)}, u32[]{:S(2)}) copy-start(bf16[576,48]{1,0:T(8,128)(2,1)} %constant.30.clone.mix_ref) | copy-start | bytes 165892
  42.2 21.3 %all-to-all-start.1 = ((f16[128,24,128]{2,1,0:T(8,128)(2,1)}), f16[128,24,128]{2,1,0:T(8,128)(2,1)S(1)}, u32[]{:S(2)}, u32[]{:S(2)}) async-start(f16[128,24,128]{2,1,0:T(8,128)(2,1)} %bitcast.8), calls=%async_computation.1 | async-start | bytes 1572864 | tf_op jit(solution)/shard_map/all_to_all | solution.py:548
  52.5 16.2 %copy-start.4 = (f32[2048]{0:T(1024)S(1)}, f32[2048]{0:T(1024)}, u32[]{:S(2)}) copy-start(f32[2048]{0:T(1024)} %param.16) | copy-start | bytes 24580
  52.5 16.2 %copy-start.6 = (s32[2048]{0:T(1024)S(1)}, s32[2048]{0:T(1024)}, u32[]{:S(2)}) copy-start(s32[2048]{0:T(1024)} %param.17) | copy-start | bytes 24580
  52.5 16.1 %copy-start.8 = (bf16[2,256,256]{2,1,0:T(8,128)(2,1)S(1)}, bf16[2,256,256]{2,1,0:T(8,128)(2,1)}, u32[]{:S(2)}) copy-start(bf16[2,256,256]{2,1,0:T(8,128)(2,1)} %constant.31.clone.dft_ref) | copy-start | bytes 786436
  52.5 16.1 %copy-start.14 = (f32[2,64,128]{2,1,0:T(8,128)S(1)}, f32[2,64,128]{2,1,0:T(8,128)}, u32[]{:S(2)}) copy-start(f32[2,64,128]{2,1,0:T(8,128)} %constant.26.clone.tw_ref) | copy-start | bytes 196612
  52.5 10.8 %collective-permute-start.3 = (bf16[48,640]{1,0:T(8,128)(2,1)S(1)}, bf16[48,640]{1,0:T(8,128)(2,1)S(1)}, u32[]{:S(2)}, u32[]{:S(2)}) collective-permute-start(bf16[48,640]{1,0:T(8,128)(2,1)S(1)} %get-tuple-element.19), channel_id=1, source_target_pairs={{0,15},{1,8},{2,9},{3,10},{4,11},{5,12},{6,13},{7,14},{8,23},{9,16... | collective-permute-start | bytes 184328 | tf_op jit(solution)/shard_map/ppermute | solution.py:458
  57.1 7.5 %collective-permute-start.5 = (bf16[48,128]{1,0:T(8,128)(2,1)S(1)}, bf16[48,128]{1,0:T(8,128)(2,1)S(1)}, u32[]{:S(2)}, u32[]{:S(2)}) collective-permute-start(bf16[48,128]{1,0:T(8,128)(2,1)S(1)} %get-tuple-element.20), channel_id=1, source_target_pairs={{8,7},{9,0},{10,1},{11,2},{12,3},{13,4},{14,5},{15,6},{16,15},{17,... | collective-permute-start | bytes 36872 | tf_op jit(solution)/shard_map/ppermute | solution.py:458
  63.4 5.3 %collective-permute-start.4 = (bf16[48,1024]{1,0:T(8,128)(2,1)S(1)}, bf16[48,1024]{1,0:T(8,128)(2,1)S(1)}, u32[]{:S(2)}, u32[]{:S(2)}) collective-permute-start(bf16[48,1024]{1,0:T(8,128)(2,1)S(1)} %pad_maximum_fusion.1), channel_id=1, source_target_pairs={{0,1},{1,2},{2,3},{3,4},{4,5},{5,6},{6,7},{7,0},{8,9},{9,10},{10,1... | collective-permute-start | bytes 294920 | tf_op jit(solution)/shard_map/ppermute | solution.py:458

commit v3 on v2

--- a/solution.py
+++ b/solution.py
@@ -43,10 +43,11 @@
     return split_table(np.block([[cosine, -sine], [sine, cosine]]))
 
 
-def row_twiddle():
+def row_table():
     k1 = np.repeat(np.arange(8), 8)
     angles = (k1[:, None] * np.arange(128)[None, :]) * (2.0 * math.pi / 1024)
-    return np.stack([np.cos(angles), -np.sin(angles)]).astype(np.float32)
+    twiddle = split_table(np.concatenate([np.cos(angles), -np.sin(angles)]))
+    return np.concatenate([*dft_table(-1.0), np.concatenate([*twiddle], axis=1)])
 
 
 def column_twiddle():
@@ -97,6 +98,10 @@
     return high, (value - high.astype(F32)).astype(BF16)
 
 
+def coded(value):
+    return value * lax.rsqrt(jnp.maximum(jnp.abs(value), 1e-30))
+
+
 def cadd(left, right):
     return (left[0] + right[0], left[1] + right[1])
 
@@ -148,12 +153,17 @@
     four_ref[...] = own_ref[:, 15 * PIL : 16 * PIL]
 
 
+def twiddles(table_ref):
+    return table_ref[512:640, 0:128].astype(F32) + table_ref[512:640, 128:256].astype(F32)
+
+
 def rows_kernel(
-    x_ref, w_ref, cell_ref, dft_ref, tw_ref, out_ref, pack_ref, xb_ref, xt_ref, hot_ref, g_ref, b_ref
+    x_ref, w_ref, cell_ref, table_ref, out_ref, pack_ref, xb_ref, xt_ref, hot_ref, g_ref, b_ref, tw_ref
 ):
     for slab in range(12):
         pack_ref[slab * 4 : slab * 4 + 4, :] = x_ref[slab].astype(F32)
     xb_ref[...] = pack_ref[...].astype(BF16)
+    tw_ref[...] = twiddles(table_ref)
     cells = cell_ref[...]
     upper = cells >> 8
     weight = w_ref[...]
@@ -172,7 +182,7 @@
         piece = xt_ref[rows, :]
         g_ref[rows, :] = dot(piece, hot_ref[0], 1, 1) + dot(piece, hot_ref[1], 1, 1)
 
-    def one_row(row, carry):
+    def one_row(row):
         for t in range(3):
             values = []
             for n1 in range(8):
@@ -190,21 +200,24 @@
                 value = values[k1]
                 if k1 > 0:
                     twiddle = (
-                        tw_ref[0, k1 * 8 : k1 * 8 + 8, :],
-                        tw_ref[1, k1 * 8 : k1 * 8 + 8, :],
+                        tw_ref[0 + k1 * 8 : 8 + k1 * 8, :],
+                        tw_ref[64 + k1 * 8 : 72 + k1 * 8, :],
                     )
                     value = cmul(value, twiddle)
                 rows = pl.ds(pl.multiple_of(base + k1 * 8, 8), 8)
                 b_ref[rows, 0:128] = value[0]
                 b_ref[rows, 128:256] = value[1]
-        return carry
-
-    lax.fori_loop(0, 8, one_row, 0)
+
+    for row in range(8):
+        one_row(row)
     for pair in range(6):
         b_high, b_low = halves(b_ref[pair * 256 : (pair + 1) * 256, :])
         result = (
-            dot(dft_ref[0], b_high, 1, 1) + dot(dft_ref[0], b_low, 1, 1) + dot(dft_ref[1], b_high, 1, 1)
+            dot(table_ref[0:256, :], b_high, 1, 1)
+            + dot(table_ref[0:256, :], b_low, 1, 1)
+            + dot(table_ref[256:512, :], b_high, 1, 1)
         )
+        result = coded(result)
         for part in range(2):
             for side in range(2):
                 out_ref[pl.ds(part * 12 + pair * 2 + side, 128, 24), :] = result[
@@ -212,65 +225,75 @@
                 ]
 
 
-def columns_kernel(r_ref, kern_ref, fwd_ref, inv_ref, tw_ref, lane_ref, out_ref, v_ref, u_ref):
-    for part in range(2):
-        for group in range(12):
-            v_ref[part * 128 : (part + 1) * 128, group * 128 : (group + 1) * 128] = r_ref[
-                pl.ds(part * 12 + group, 128, 24), :
-            ]
-    for chunk in range(6):
-        lanes = slice(chunk * 256, (chunk + 1) * 256)
-        v_high, v_low = halves(v_ref[:, lanes])
-        u_ref[:, lanes] = dot(fwd_ref[0], v_high) + dot(fwd_ref[0], v_low) + dot(fwd_ref[1], v_high)
+def columns_kernel(r_ref, kern_ref, fwd_ref, inv_ref, tw_ref, lane_ref, out_ref, v_ref, u_ref, y_ref):
     sign = lane_ref[8:9, :]
 
     def swap(value):
         return tuple(part * sign + pltpu.roll(part, 64, 1) for part in value)
 
-    def one_block(block, carry):
-        start = pl.multiple_of(block * 8, 8)
-        re_rows = pl.ds(start, 8)
-        im_rows = pl.ds(pl.multiple_of(start + 128, 8), 8)
-        twiddles, kernels = [], []
-        for m in range(4):
-            rows = pl.ds(pl.multiple_of(start + m * 128, 8), 8)
-            twiddles.append((tw_ref[0, rows, :], tw_ref[1, rows, :]))
-            kernels.append((kern_ref[0, rows, :], kern_ref[1, rows, :]))
-        for t in range(3):
-            values = []
+    def lanes_of(t, m):
+        return slice((t * 4 + m) * 128, (t * 4 + m + 1) * 128)
+
+    def spread(t):
+        for part in range(2):
             for m in range(4):
-                lanes = slice((m * 3 + t) * 128, (m * 3 + t + 1) * 128)
+                v_ref[part * 128 : (part + 1) * 128, lanes_of(t, m)] = r_ref[
+                    pl.ds(part * 12 + m * 3 + t, 128, 24), :
+                ]
+        for chunk in range(2):
+            lanes = slice((t * 2 + chunk) * 256, (t * 2 + chunk + 1) * 256)
+            v_high, v_low = halves(v_ref[:, lanes])
+            u_ref[:, lanes] = dot(fwd_ref[0], v_high) + dot(fwd_ref[0], v_low) + dot(fwd_ref[1], v_high)
+
+    def multiply(t):
+        for block in range(16):
+            re_rows = slice(block * 8, block * 8 + 8)
+            im_rows = slice(block * 8 + 128, block * 8 + 136)
+            values, twiddles = [], []
+            for m in range(4):
+                rows = slice(m * 128 + block * 8, m * 128 + block * 8 + 8)
+                twiddles.append((tw_ref[0, rows, :], tw_ref[1, rows, :]))
+                lanes = lanes_of(t, m)
                 values.append(cmul((u_ref[re_rows, lanes], u_ref[im_rows, lanes]), twiddles[m]))
             values = dft4(values, -1.0)
             for a in range(4):
+                rows = slice(a * 128 + block * 8, a * 128 + block * 8 + 8)
                 side = (lane_ref[a : a + 1, :], lane_ref[4 + a : 5 + a, :])
                 value = values[a] if a == 0 else cmul(values[a], side)
-                value = swap(cmul(swap(value), kernels[a]))
+                value = swap(cmul(swap(value), (kern_ref[0, rows, :], kern_ref[1, rows, :])))
                 values[a] = value if a == 0 else cmul_conj(value, side)
             values = dft4(values, 1.0)
             for m in range(4):
-                lanes = slice((m * 3 + t) * 128, (m * 3 + t + 1) * 128)
                 value = cmul_conj(values[m], twiddles[m])
-                v_ref[re_rows, lanes] = value[0]
-                v_ref[im_rows, lanes] = value[1]
-        return carry
-
-    lax.fori_loop(0, 16, one_block, 0)
-    for chunk in range(6):
-        lanes = slice(chunk * 256, (chunk + 1) * 256)
-        v_high, v_low = halves(v_ref[:, lanes])
-        result = dot(inv_ref[0], v_high) + dot(inv_ref[0], v_low) + dot(inv_ref[1], v_high)
-        for part in range(2):
-            for side in range(2):
-                out_ref[pl.ds(part * 12 + chunk * 2 + side, 128, 24), :] = result[
-                    part * 128 : (part + 1) * 128, side * 128 : (side + 1) * 128
-                ]
+                y_ref[re_rows, lanes_of(t, m)] = value[0]
+                y_ref[im_rows, lanes_of(t, m)] = value[1]
+
+    def gather(t):
+        for chunk in range(2):
+            lanes = slice((t * 2 + chunk) * 256, (t * 2 + chunk + 1) * 256)
+            y_high, y_low = halves(y_ref[:, lanes])
+            result = coded(dot(inv_ref[0], y_high) + dot(inv_ref[0], y_low) + dot(inv_ref[1], y_high))
+            for part in range(2):
+                for side in range(2):
+                    out_ref[pl.ds(part * 12 + (chunk * 2 + side) * 3 + t, 128, 24), :] = result[
+                        part * 128 : (part + 1) * 128, side * 128 : (side + 1) * 128
+                    ]
+
+    spread(0)
+    spread(1)
+    multiply(0)
+    spread(2)
+    gather(0)
+    multiply(1)
+    gather(1)
+    multiply(2)
+    gather(2)
 
 
 def sample_kernel(
-    r_ref, w_ref, cell_ref, near_ref, both_ref, side_ref, four_ref, dft_ref, tw_ref,
-    out_ref, v_ref, g_ref, f_ref, sum_ref,
+    r_ref, w_ref, cell_ref, table_ref, sum_ref, v_ref, g_ref, f_ref, tw_ref
 ):
+    tw_ref[...] = twiddles(table_ref)
     for part in range(2):
         for group in range(12):
             piece = r_ref[pl.ds(part * 12 + group, 128, 24), :]
@@ -279,10 +302,12 @@
         rows = slice(chunk * 768, (chunk + 1) * 768)
         v_high, v_low = halves(v_ref[rows, :])
         g_ref[rows, :] = (
-            dot(v_high, dft_ref[0], 1, 1) + dot(v_low, dft_ref[0], 1, 1) + dot(v_high, dft_ref[1], 1, 1)
+            dot(v_high, table_ref[0:256, :])
+            + dot(v_low, table_ref[0:256, :])
+            + dot(v_high, table_ref[256:512, :])
         )
 
-    def one_row(row, carry):
+    def one_row(row):
         for t in range(3):
             base = (((row // 2) * 3 + t) * 2 + row % 2) * 64
             values = []
@@ -291,8 +316,8 @@
                 value = (g_ref[rows, 0:128], g_ref[rows, 128:256])
                 if k1 > 0:
                     twiddle = (
-                        tw_ref[0, k1 * 8 : k1 * 8 + 8, :],
-                        tw_ref[1, k1 * 8 : k1 * 8 + 8, :],
+                        tw_ref[0 + k1 * 8 : 8 + k1 * 8, :],
+                        tw_ref[64 + k1 * 8 : 72 + k1 * 8, :],
                     )
                     value = cmul_conj(value, twiddle)
                 values.append(value)
@@ -302,9 +327,9 @@
                 lanes = slice((n1 % 2) * 128, (n1 % 2) * 128 + 128)
                 v_ref[pl.ds(pl.multiple_of(start, 8), 8), lanes] = values[n1][0]
                 v_ref[pl.ds(pl.multiple_of(start + HALF, 8), 8), lanes] = values[n1][1]
-        return carry
-
-    lax.fori_loop(0, 8, one_row, 0)
+
+    for row in range(8):
+        one_row(row)
     f_high, f_low = halves(v_ref[...])
     f_ref[0] = f_high
     f_ref[1] = f_low
@@ -321,7 +346,10 @@
             for part in range(8):
                 hit = jnp.broadcast_to(upper == quarter * 8 + part, (CHAN, 256))
                 total = total + jnp.where(hit, picked[part * CHAN : (part + 1) * CHAN, :], 0.0)
-        sum_ref[:, lanes] = total * w_ref[:, lanes] + near_ref[:, lanes]
+        sum_ref[:, lanes] = total * w_ref[:, lanes]
+
+def finish_kernel(far_ref, near_ref, both_ref, side_ref, four_ref, out_ref, sum_ref):
+    sum_ref[...] = far_ref[...] + near_ref[...]
     for cluster in range(4):
         lanes = slice(cluster * 4 * PIL, (cluster * 4 + 1) * PIL)
         sum_ref[:, lanes] += both_ref[:, cluster * PIL : (cluster + 1) * PIL].astype(F32)
@@ -480,7 +508,7 @@
     )(x, jitter)
 
 
-def rows_call(x, w, cell, forward, row_table):
+def rows_call(x, w, cell, table):
     return pl.pallas_call(
         rows_kernel,
         out_shape=shape((DEVICES * HALF, 128)),
@@ -491,10 +519,11 @@
             pltpu.VMEM((2, 256, WIDTH), BF16),
             pltpu.VMEM((1536, 256), F32),
             pltpu.VMEM((1536, 256), F32),
+            pltpu.VMEM((128, 128), F32),
         ],
         compiler_params=PARAMS,
         cost_estimate=cost(3_800_000_000, 4 * MIB),
-    )(x, w, cell, forward, row_table)
+    )(x, w, cell, table)
 
 
 def near_call(spots, own, both, side, four, mixing):
@@ -521,30 +550,39 @@
     return pl.pallas_call(
         columns_kernel,
         out_shape=shape((DEVICES * HALF, 128)),
-        scratch_shapes=[pltpu.VMEM((256, 1536), F32), pltpu.VMEM((256, 1536), F32)],
+        scratch_shapes=[pltpu.VMEM((256, 1536), F32)] * 3,
         compiler_params=PARAMS,
         cost_estimate=cost(2_000_000_000, 6 * MIB),
     )(columns, transfer, forward, backward, column_table, lane_table)
 
 
-def sample_call(rows, w, cell, near, both, side, four, backward, row_table):
+def sample_call(rows, w, cell, table):
     return pl.pallas_call(
         sample_kernel,
-        out_shape=shape((12, 4, WIDTH)),
+        out_shape=shape((CHAN, WIDTH)),
         scratch_shapes=[
             pltpu.VMEM((1536, 256), F32),
             pltpu.VMEM((1536, 256), F32),
             pltpu.VMEM((2, 1536, 256), BF16),
-            pltpu.VMEM((CHAN, WIDTH), F32),
+            pltpu.VMEM((128, 128), F32),
         ],
         compiler_params=PARAMS,
         cost_estimate=cost(3_800_000_000, 4 * MIB),
-    )(rows, w, cell, near, both, side, four, backward, row_table)
+    )(rows, w, cell, table)
+
+
+def finish_call(far, near, both, side, four):
+    return pl.pallas_call(
+        finish_kernel,
+        out_shape=shape((12, 4, WIDTH)),
+        scratch_shapes=[pltpu.VMEM((CHAN, WIDTH), F32)],
+        compiler_params=PARAMS,
+        cost_estimate=cost(1_000_000, 2 * MIB),
+    )(far, near, both, side, four)
 
 
 def exchange(message):
-    code = message * lax.rsqrt(jnp.maximum(jnp.abs(message), 1e-30))
-    code = code.reshape(DEVICES, HALF, 128).astype(jnp.float16)
+    code = message.reshape(DEVICES, HALF, 128).astype(jnp.float16)
     code = lax.all_to_all(code, AXES, split_axis=0, concat_axis=0, tiled=True)
     code = code.astype(F32)
     return (code * jnp.abs(code)).reshape(DEVICES * HALF, 128)
@@ -555,9 +593,9 @@
     w = weights.reshape(1, WIDTH)
     cell = cells.reshape(1, WIDTH)
     forward = jnp.asarray(dft_table(-1.0))
-    row_table = jnp.asarray(row_twiddle())
-
-    message = rows_call(x, w, cell, forward, row_table)
+    table = jnp.asarray(row_table())
+
+    message = rows_call(x, w, cell, table)
     columns = exchange(message)
     own, one, two, four = pack_call(x, jitter)
     side = shift(two, -1, 1)
@@ -588,7 +626,8 @@
     side = shift(side, 1, -1)
     four = shift(four, -1, -1)
     both = shift(jnp.concatenate([one, side[:, 0 : 4 * PIL]], axis=1), 0, 1)
-    coupled = sample_call(rows, w, cell, near, both, side, four, jnp.asarray(dft_table(1.0)), row_table)
+    far = sample_call(rows, w, cell, table)
+    coupled = finish_call(far, near, both, side, four)
     return coupled.reshape(2, 6, ANG, WIDTH).transpose(0, 2, 1, 3)
 
 

time: 75.6 us -> 68.2 us (0.902)
  the two profiles are of different devices: /device:TPU:4 before, /device:TPU:1 now
where the time goes in v3:
time: 68.2 us; the launch traced here: 67.7 us
  starting transfers between devices  32.6 us (48%)
  Pallas kernels  16.7 us (24%)
  waiting for transfers between devices  10.8 us (16%)
  local copies, waits for them, and re-layouts  4.03 us (6%)
  other arithmetic  2.43 us (4%)
  between operations  1.1 us (2%)
    ppermute x6, starting transfers between devices, shift(): return lax.ppermute(value, AXES, pairs)  16.4 us
    all_to_all x2, starting transfers between devices, exchange(): code = lax.all_to_all(code, AXES, split_axis=0, concat_axis=0, tiled=True)  16.3 us
    all_to_all x2, waiting for transfers between devices, exchange(): code = lax.all_to_all(code, AXES, split_axis=0, concat_axis=0, tiled=True)  6.82 us
    pallas_call x1, Pallas kernels, sample_call(): pl.pallas_call(sample_kernel, out_shape=shape((CHAN, WIDTH)), scratch_sha...  4.53 us
    pallas_call x1, Pallas kernels, rows_call(): pl.pallas_call(rows_kernel, out_shape=shape((DEVICES * HALF, 128)), scrat...  4.45 us
    ppermute x6, waiting for transfers between devices, shift(): return lax.ppermute(value, AXES, pairs)  4.02 us
    pallas_call x1, Pallas kernels, near_call(): pl.pallas_call(near_kernel, in_specs=[pl.BlockSpec(memory_space=pltpu.SME...  3.91 us
    unnamed x33, local copies, waits for them, and re-layouts  3.45 us
  transfers between devices with their start and end apart: 8, of which 4 were waited for; matrix products, arithmetic and copies ran while one was open for 3% of the time, Pallas kernels for 17%

profile of v3, /device:TPU:1, one launch (start us, length us, event | category | flops | bytes accessed | tf_op | source)
XLA Modules:
  0.0 67.7 jit_solution(8951751788479989229)
XLA Ops:
  0.0 0.9 %copy-done = bf16[2,4,6,2048]{3,1,2,0:T(4,128)(2,1)S(1)} copy-done((bf16[2,4,6,2048]{3,1,2,0:T(4,128)(2,1)S(1)}, bf16[2,4,6,2048]{3,1,2,0:T(4,128)(2,1)}, u32[]{:S(2)}) %copy-start) | copy-done | bytes 196632
  0.9 0.7 %copy-done.3 = f32[2048]{0:T(1024)S(1)} copy-done((f32[2048]{0:T(1024)S(1)}, f32[2048]{0:T(1024)}, u32[]{:S(2)}) %copy-start.3) | copy-done | bytes 8216
  1.6 0.7 %copy-done.5 = s32[2048]{0:T(1024)S(1)} copy-done((s32[2048]{0:T(1024)S(1)}, s32[2048]{0:T(1024)}, u32[]{:S(2)}) %copy-start.5) | copy-done | bytes 8216
  2.3 1.0 %copy-done.8 = bf16[640,256]{1,0:T(8,128)(2,1)S(1)} copy-done((bf16[640,256]{1,0:T(8,128)(2,1)S(1)}, bf16[640,256]{1,0:T(8,128)(2,1)}, u32[]{:S(2)}) %copy-start.8) | copy-done | bytes 327704
  3.3 4.5 %shard_map.127 = f32[3072,128]{1,0:T(8,128)S(1)} custom-call(bf16[12,4,2048]{2,1,0:T(4,128)(2,1)S(1)} %bitcast.21, f32[1,2048]{1,0:T(1,128)S(1)} %bitcast.23, s32[1,2048]{1,0:T(1,128)S(1)} %bitcast.25, bf16[640,256]{1,0:T(8,128)(2,1)S(1)} %copy-done.8), custom_call_target="tpu_custom_call" | custom-call | flops 3800000000 | bytes 4194304 | tf_op jit(solution)/shard_map/pallas_call | solution.py:512
  7.8 0.0 copy-start.1
  7.8 0.0 copy-start.2
  7.8 0.0 copy-start.14
  7.8 1.0 %convert_element_type.18 = f16[3072,128]{1,0:T(8,128)(2,1)} convert(f32[3072,128]{1,0:T(8,128)S(1)} %shard_map.127) | non-fusion elementwise | flops 393216 | bytes 2359296 | tf_op jit(solution)/shard_map/convert_element_type | solution.py:585
  8.8 11.5 %all-to-all-start = ((f16[128,24,128]{2,1,0:T(8,128)(2,1)}), f16[128,24,128]{2,1,0:T(8,128)(2,1)S(1)}, u32[]{:S(2)}, u32[]{:S(2)}) async-start(f16[128,24,128]{2,1,0:T(8,128)(2,1)} %bitcast.4), calls=%async_computation | async-start | bytes 1572864 | tf_op jit(solution)/shard_map/all_to_all | solution.py:586
  20.3 0.0 copy-start.15
  20.3 0.1 shard_map.130
  20.4 1.3 %collective-permute-start = (bf16[64,512]{1,0:T(8,128)(2,1)S(1)}, bf16[64,512]{1,0:T(8,128)(2,1)S(1)}, u32[]{:S(2)}, u32[]{:S(2)}) collective-permute-start(bf16[64,512]{1,0:T(8,128)(2,1)S(1)} %get-tuple-element.15), channel_id=1, source_target_pairs={{8,1},{9,2},{10,3},{11,4},{12,5},{13,6},{14,7},{15,0},{16,9},{17,1... | collective-permute-start | bytes 196616 | tf_op jit(solution)/shard_map/ppermute | solution.py:486
  21.7 5.5 %collective-permute-start.2 = (bf16[64,128]{1,0:T(8,128)(2,1)S(1)}, bf16[64,128]{1,0:T(8,128)(2,1)S(1)}, u32[]{:S(2)}, u32[]{:S(2)}) collective-permute-start(bf16[64,128]{1,0:T(8,128)(2,1)S(1)} %get-tuple-element.16), channel_id=1, source_target_pairs={{0,9},{1,10},{2,11},{3,12},{4,13},{5,14},{6,15},{7,8},{8,17},{9,18... | collective-permute-start | bytes 49160 | tf_op jit(solution)/shard_map/ppermute | solution.py:486
  27.3 0.1 broadcast_in_dim.2
  27.3 0.2 reshape.43
  27.6 0.2 copy.17.kern_ref
  27.8 0.0 copy-start.7
  27.8 0.0 copy-start.10
  27.8 0.0 copy-start.11
  27.8 0.0 copy-start.13
  28.5 0.1 copy.18
  28.6 0.1 reshape.45
  28.7 0.1 pad_add_fusion.list_ref
  28.8 2.3 %collective-permute-done.side_ref = bf16[64,512]{1,0:T(8,128)(2,1)S(1)} collective-permute-done((bf16[64,512]{1,0:T(8,128)(2,1)S(1)}, bf16[64,512]{1,0:T(8,128)(2,1)S(1)}, u32[]{:S(2)}, u32[]{:S(2)}) %collective-permute-start) | collective-permute-done | bytes 65568 | tf_op jit(solution)/shard_map/ppermute | solution.py:486
  31.1 2.9 %collective-permute-start.1 = (bf16[64,1024]{1,0:T(8,128)(2,1)S(1)}, bf16[64,1024]{1,0:T(8,128)(2,1)S(1)}, u32[]{:S(2)}, u32[]{:S(2)}) collective-permute-start(bf16[64,1024]{1,0:T(8,128)(2,1)S(1)} %pad_maximum_fusion), channel_id=1, source_target_pairs={{0,7},{1,0},{2,1},{3,2},{4,3},{5,4},{6,5},{7,6},{8,15},{9,8},{10,9... | collective-permute-start | bytes 393224 | tf_op jit(solution)/shard_map/ppermute | solution.py:486
  34.1 2.7 %all-to-all-done = f16[128,24,128]{2,1,0:T(8,128)(2,1)S(1)} async-done(((f16[128,24,128]{2,1,0:T(8,128)(2,1)}), f16[128,24,128]{2,1,0:T(8,128)(2,1)S(1)}, u32[]{:S(2)}, u32[]{:S(2)}) %all-to-all-start) | async-done | bytes 786464 | tf_op jit(solution)/shard_map/all_to_all | solution.py:586
  36.8 0.2 abs_multiply_fusion.1
  37.0 2.9 %shard_map.128 = f32[3072,128]{1,0:T(8,128)S(1)} custom-call(f32[3072,128]{1,0:T(8,128)S(1)} %bitcast.19, f32[2,512,128]{2,1,0:T(8,128)S(1)} %copy.17.kern_ref, bf16[2,256,256]{2,1,0:T(8,128)(2,1)S(1)} %copy-done.10, bf16[2,256,256]{2,1,0:T(8,128)(2,1)S(1)} %copy-done.11, f32[2,512,128]{2,1,0:T(8,128)S(1)} %copy-done.7, f32[16,128]{1,0:T(8,128)S(1)} %copy-done.13), custom_call_target="tpu_custom_call" | custom-call | flops 2000000000 | bytes 6291456 | tf_op jit(solution)/shard_map/pallas_call | solution.py:550
  39.9 0.0 copy-start.12
  39.9 1.0 %convert_element_type.21 = f16[3072,128]{1,0:T(8,128)(2,1)} convert(f32[3072,128]{1,0:T(8,128)S(1)} %shard_map.128) | non-fusion elementwise | flops 393216 | bytes 2359296 | tf_op jit(solution)/shard_map/convert_element_type | solution.py:585
  40.9 4.8 %all-to-all-start.1 = ((f16[128,24,128]{2,1,0:T(8,128)(2,1)}), f16[128,24,128]{2,1,0:T(8,128)(2,1)S(1)}, u32[]{:S(2)}, u32[]{:S(2)}) async-start(f16[128,24,128]{2,1,0:T(8,128)(2,1)} %bitcast.8), calls=%async_computation.1 | async-start | bytes 1572864 | tf_op jit(solution)/shard_map/all_to_all | solution.py:586
  45.6 0.0 collective-permute-done.2.four_ref
  45.7 0.0 collective-permute-done.1.both_ref
  45.7 3.9 %shard_map.131 = (f32[48,2048]{1,0:T(8,128)S(1)}, bf16[48,512]{1,0:T(8,128)(2,1)S(1)}, bf16[48,640]{1,0:T(8,128)(2,1)S(1)}, bf16[48,128]{1,0:T(8,128)(2,1)S(1)}) custom-call(s32[27]{0:T(128)S(1)} %pad_add_fusion.list_ref, bf16[64,2048]{1,0:T(8,128)(2,1)S(1)} %get-tuple-element.13.own_ref, bf16[64,1024]{1,0:T(8,128)(2,1)S(1)} %collective-permute-done.1.both_ref, ...), custom_call_target="tpu_custom_call" | custom-call | flops 8000000000 | bytes 4194304 | tf_op jit(solution)/shard_map/pallas_call | solution.py:530
  49.6 0.0 copy-start.4
  49.6 0.0 copy-start.6
  49.6 0.0 copy-start.9
  49.6 3.7 %collective-permute-start.3 = (bf16[48,640]{1,0:T(8,128)(2,1)S(1)}, bf16[48,640]{1,0:T(8,128)(2,1)S(1)}, u32[]{:S(2)}, u32[]{:S(2)}) collective-permute-start(bf16[48,640]{1,0:T(8,128)(2,1)S(1)} %get-tuple-element.19), channel_id=1, source_target_pairs={{0,15},{1,8},{2,9},{3,10},{4,11},{5,12},{6,13},{7,14},{8,23},{9,16... | collective-permute-start | bytes 184328 | tf_op jit(solution)/shard_map/ppermute | solution.py:486
  53.3 1.5 %collective-permute-start.5 = (bf16[48,128]{1,0:T(8,128)(2,1)S(1)}, bf16[48,128]{1,0:T(8,128)(2,1)S(1)}, u32[]{:S(2)}, u32[]{:S(2)}) collective-permute-start(bf16[48,128]{1,0:T(8,128)(2,1)S(1)} %get-tuple-element.20), channel_id=1, source_target_pairs={{8,7},{9,0},{10,1},{11,2},{12,3},{13,4},{14,5},{15,6},{16,15},{17,... | collective-permute-start | bytes 36872 | tf_op jit(solution)/shard_map/ppermute | solution.py:486
  54.8 1.7 %collective-permute-done.3.side_ref = bf16[48,640]{1,0:T(8,128)(2,1)S(1)} collective-permute-done((bf16[48,640]{1,0:T(8,128)(2,1)S(1)}, bf16[48,640]{1,0:T(8,128)(2,1)S(1)}, u32[]{:S(2)}, u32[]{:S(2)}) %collective-permute-start.3) | collective-permute-done | bytes 61472 | tf_op jit(solution)/shard_map/ppermute | solution.py:486
  56.5 1.5 %collective-permute-start.4 = (bf16[48,1024]{1,0:T(8,128)(2,1)S(1)}, bf16[48,1024]{1,0:T(8,128)(2,1)S(1)}, u32[]{:S(2)}, u32[]{:S(2)}) collective-permute-start(bf16[48,1024]{1,0:T(8,128)(2,1)S(1)} %pad_maximum_fusion.1), channel_id=1, source_target_pairs={{0,1},{1,2},{2,3},{3,4},{4,5},{5,6},{6,7},{7,0},{8,9},{9,10},{10,1... | collective-permute-start | bytes 294920 | tf_op jit(solution)/shard_map/ppermute | solution.py:486
  58.0 4.1 %all-to-all-done.1 = f16[128,24,128]{2,1,0:T(8,128)(2,1)S(1)} async-done(((f16[128,24,128]{2,1,0:T(8,128)(2,1)}), f16[128,24,128]{2,1,0:T(8,128)(2,1)S(1)}, u32[]{:S(2)}, u32[]{:S(2)}) %all-to-all-start.1) | async-done | bytes 786464 | tf_op jit(solution)/shard_map/all_to_all | solution.py:586
  62.1 0.2 abs_multiply_fusion
  62.3 4.5 %shard_map.129.far_ref = f32[48,2048]{1,0:T(8,128)S(1)} custom-call(f32[3072,128]{1,0:T(8,128)S(1)} %bitcast.20, f32[1,2048]{1,0:T(1,128)S(1)} %bitcast.24, s32[1,2048]{1,0:T(1,128)S(1)} %bitcast.26, bf16[640,256]{1,0:T(8,128)(2,1)S(1)} %copy-done.9), custom_call_target="tpu_custom_call" | custom-call | flops 3800000000 | bytes 4194304 | tf_op jit(solution)/shard_map/pallas_call | solution.py:560
  66.9 0.0 collective-permute-done.5.four_ref
  66.9 0.0 collective-permute-done.4.both_ref
  66.9 0.8 %shard_map.132 = f32[12,4,2048]{2,1,0:T(4,128)} custom-call(f32[48,2048]{1,0:T(8,128)S(1)} %shard_map.129.far_ref, f32[48,2048]{1,0:T(8,128)S(1)} %get-tuple-element.17.near_ref, bf16[48,1024]{1,0:T(8,128)(2,1)S(1)} %collective-permute-done.4.both_ref, bf16[48,640]{1,0:T(8,128)(2,1)S(1)} %collective-permute-done.3.side_ref, ...), custom_call_target="tpu_custom_call" | custom-call | flops 1000000 | bytes 2097152 | tf_op jit(solution)/shard_map/pallas_call | solution.py:575
  (20 shorter events, 0.1 us)
Async XLA Ops:
  0.0 0.9 %copy-start = (bf16[2,4,6,2048]{3,1,2,0:T(4,128)(2,1)S(1)}, bf16[2,4,6,2048]{3,1,2,0:T(4,128)(2,1)}, u32[]{:S(2)}) copy-start(bf16[2,4,6,2048]{3,1,2,0:T(4,128)(2,1)} %param.13) | copy-start | bytes 589828
  0.9 0.7 %copy-start.3 = (f32[2048]{0:T(1024)S(1)}, f32[2048]{0:T(1024)}, u32[]{:S(2)}) copy-start(f32[2048]{0:T(1024)} %param.15) | copy-start | bytes 24580
  1.6 0.7 %copy-start.5 = (s32[2048]{0:T(1024)S(1)}, s32[2048]{0:T(1024)}, u32[]{:S(2)}) copy-start(s32[2048]{0:T(1024)} %param.16) | copy-start | bytes 24580
  2.3 1.0 %copy-start.8 = (bf16[640,256]{1,0:T(8,128)(2,1)S(1)}, bf16[640,256]{1,0:T(8,128)(2,1)}, u32[]{:S(2)}) copy-start(bf16[640,256]{1,0:T(8,128)(2,1)} %constant.22.clone.table_ref) | copy-start | bytes 983044
  7.8 12.5 %copy-start.1 = (bf16[2,4,6,2048]{3,1,2,0:T(4,128)(2,1)S(1)}, bf16[2,4,6,2048]{3,1,2,0:T(4,128)(2,1)}, u32[]{:S(2)}) copy-start(bf16[2,4,6,2048]{3,1,2,0:T(4,128)(2,1)} %param.13) | copy-start | bytes 589828
  7.8 12.5 %copy-start.2 = (bf16[2,2048]{1,0:T(2,128)(2,1)S(1)}, bf16[2,2048]{1,0:T(2,128)(2,1)}, u32[]{:S(2)}) copy-start(bf16[2,2048]{1,0:T(2,128)(2,1)} %jitter_ref.1) | copy-start | bytes 24580
  7.8 19.4 %copy-start.14 = (f32[2,1024,8]{1,2,0:T(8,128)S(1)}, f32[2,1024,8]{1,2,0:T(8,128)}, u32[]{:S(2)}) copy-start(f32[2,1024,8]{1,2,0:T(8,128)} %param.19) | copy-start | bytes 196612
  8.8 28.0 %all-to-all-start = ((f16[128,24,128]{2,1,0:T(8,128)(2,1)}), f16[128,24,128]{2,1,0:T(8,128)(2,1)S(1)}, u32[]{:S(2)}, u32[]{:S(2)}) async-start(f16[128,24,128]{2,1,0:T(8,128)(2,1)} %bitcast.4), calls=%async_computation | async-start | bytes 1572864 | tf_op jit(solution)/shard_map/all_to_all | solution.py:586
  20.3 8.2 %copy-start.15 = (s32[1,8,3]{1,0,2:T(1,128)S(1)}, s32[1,8,3]{1,0,2:T(1,128)}, u32[]{:S(2)}) copy-start(s32[1,8,3]{1,0,2:T(1,128)} %param.17) | copy-start | bytes 292
  20.4 10.7 %collective-permute-start = (bf16[64,512]{1,0:T(8,128)(2,1)S(1)}, bf16[64,512]{1,0:T(8,128)(2,1)S(1)}, u32[]{:S(2)}, u32[]{:S(2)}) collective-permute-start(bf16[64,512]{1,0:T(8,128)(2,1)S(1)} %get-tuple-element.15), channel_id=1, source_target_pairs={{8,1},{9,2},{10,3},{11,4},{12,5},{13,6},{14,7},{15,0},{16,9},{17,1... | collective-permute-start | bytes 196616 | tf_op jit(solution)/shard_map/ppermute | solution.py:486
  21.7 23.9 %collective-permute-start.2 = (bf16[64,128]{1,0:T(8,128)(2,1)S(1)}, bf16[64,128]{1,0:T(8,128)(2,1)S(1)}, u32[]{:S(2)}, u32[]{:S(2)}) collective-permute-start(bf16[64,128]{1,0:T(8,128)(2,1)S(1)} %get-tuple-element.16), channel_id=1, source_target_pairs={{0,9},{1,10},{2,11},{3,12},{4,13},{5,14},{6,15},{7,8},{8,17},{9,18... | collective-permute-start | bytes 49160 | tf_op jit(solution)/shard_map/ppermute | solution.py:486
  27.8 9.2 %copy-start.7 = (f32[2,512,128]{2,1,0:T(8,128)S(1)}, f32[2,512,128]{2,1,0:T(8,128)}, u32[]{:S(2)}) copy-start(f32[2,512,128]{2,1,0:T(8,128)} %constant.24.clone.tw_ref) | copy-start | bytes 1572868
  27.8 9.2 %copy-start.10 = (bf16[2,256,256]{2,1,0:T(8,128)(2,1)S(1)}, bf16[2,256,256]{2,1,0:T(8,128)(2,1)}, u32[]{:S(2)}) copy-start(bf16[2,256,256]{2,1,0:T(8,128)(2,1)} %constant.21.clone.fwd_ref) | copy-start | bytes 786436
  27.8 9.2 %copy-start.11 = (bf16[2,256,256]{2,1,0:T(8,128)(2,1)S(1)}, bf16[2,256,256]{2,1,0:T(8,128)(2,1)}, u32[]{:S(2)}) copy-start(bf16[2,256,256]{2,1,0:T(8,128)(2,1)} %constant.23.clone.inv_ref) | copy-start | bytes 786436
  27.8 9.2 %copy-start.13 = (f32[16,128]{1,0:T(8,128)S(1)}, f32[16,128]{1,0:T(8,128)}, u32[]{:S(2)}) copy-start(f32[16,128]{1,0:T(8,128)} %constant.25.clone.lane_ref) | copy-start | bytes 24580
  31.1 14.6 %collective-permute-start.1 = (bf16[64,1024]{1,0:T(8,128)(2,1)S(1)}, bf16[64,1024]{1,0:T(8,128)(2,1)S(1)}, u32[]{:S(2)}, u32[]{:S(2)}) collective-permute-start(bf16[64,1024]{1,0:T(8,128)(2,1)S(1)} %pad_maximum_fusion), channel_id=1, source_target_pairs={{0,7},{1,0},{2,1},{3,2},{4,3},{5,4},{6,5},{7,6},{8,15},{9,8},{10,9... | collective-permute-start | bytes 393224 | tf_op jit(solution)/shard_map/ppermute | solution.py:486
  39.9 5.8 %copy-start.12 = (bf16[576,48]{1,0:T(8,128)(2,1)S(1)}, bf16[576,48]{1,0:T(8,128)(2,1)}, u32[]{:S(2)}) copy-start(bf16[576,48]{1,0:T(8,128)(2,1)} %constant.26.clone.mix_ref) | copy-start | bytes 165892
  40.9 21.3 %all-to-all-start.1 = ((f16[128,24,128]{2,1,0:T(8,128)(2,1)}), f16[128,24,128]{2,1,0:T(8,128)(2,1)S(1)}, u32[]{:S(2)}, u32[]{:S(2)}) async-start(f16[128,24,128]{2,1,0:T(8,128)(2,1)} %bitcast.8), calls=%async_computation.1 | async-start | bytes 1572864 | tf_op jit(solution)/shard_map/all_to_all | solution.py:586
  49.6 12.7 %copy-start.4 = (f32[2048]{0:T(1024)S(1)}, f32[2048]{0:T(1024)}, u32[]{:S(2)}) copy-start(f32[2048]{0:T(1024)} %param.15) | copy-start | bytes 24580
  49.6 12.7 %copy-start.6 = (s32[2048]{0:T(1024)S(1)}, s32[2048]{0:T(1024)}, u32[]{:S(2)}) copy-start(s32[2048]{0:T(1024)} %param.16) | copy-start | bytes 24580
  49.6 12.7 %copy-start.9 = (bf16[640,256]{1,0:T(8,128)(2,1)S(1)}, bf16[640,256]{1,0:T(8,128)(2,1)}, u32[]{:S(2)}) copy-start(bf16[640,256]{1,0:T(8,128)(2,1)} %constant.22.clone.table_ref) | copy-start | bytes 983044
  49.6 6.9 %collective-permute-start.3 = (bf16[48,640]{1,0:T(8,128)(2,1)S(1)}, bf16[48,640]{1,0:T(8,128)(2,1)S(1)}, u32[]{:S(2)}, u32[]{:S(2)}) collective-permute-start(bf16[48,640]{1,0:T(8,128)(2,1)S(1)} %get-tuple-element.19), channel_id=1, source_target_pairs={{0,15},{1,8},{2,9},{3,10},{4,11},{5,12},{6,13},{7,14},{8,23},{9,16... | collective-permute-start | bytes 184328 | tf_op jit(solution)/shard_map/ppermute | solution.py:486
  53.3 13.6 %collective-permute-start.5 = (bf16[48,128]{1,0:T(8,128)(2,1)S(1)}, bf16[48,128]{1,0:T(8,128)(2,1)S(1)}, u32[]{:S(2)}, u32[]{:S(2)}) collective-permute-start(bf16[48,128]{1,0:T(8,128)(2,1)S(1)} %get-tuple-element.20), channel_id=1, source_target_pairs={{8,7},{9,0},{10,1},{11,2},{12,3},{13,4},{14,5},{15,6},{16,15},{17,... | collective-permute-start | bytes 36872 | tf_op jit(solution)/shard_map/ppermute | solution.py:486
  56.5 10.4 %collective-permute-start.4 = (bf16[48,1024]{1,0:T(8,128)(2,1)S(1)}, bf16[48,1024]{1,0:T(8,128)(2,1)S(1)}, u32[]{:S(2)}, u32[]{:S(2)}) collective-permute-start(bf16[48,1024]{1,0:T(8,128)(2,1)S(1)} %pad_maximum_fusion.1), channel_id=1, source_target_pairs={{0,1},{1,2},{2,3},{3,4},{4,5},{5,6},{6,7},{7,0},{8,9},{9,10},{10,1... | collective-permute-start | bytes 294920 | tf_op jit(solution)/shard_map/ppermute | solution.py:486

commit v4 on v3

--- a/solution.py
+++ b/solution.py
@@ -98,7 +98,22 @@
     return high, (value - high.astype(F32)).astype(BF16)
 
 
+STEP = 585.0
+FLOOR = 36.0
+
+
 def coded(value):
+    size = jnp.log(jnp.maximum(jnp.abs(value), 2.0**-FLOOR))
+    code = size * (STEP / math.log(2.0)) + (FLOOR * STEP + 0.5)
+    return (code * jnp.clip(value * 2.0**60, -1.0, 1.0)).astype(jnp.int32)
+
+
+def decoded(code):
+    code = code.astype(F32)
+    return jnp.exp2(jnp.abs(code) * (1.0 / STEP) - FLOOR) * jnp.clip(code, -1.0, 1.0)
+
+
+def rooted(value):
     return value * lax.rsqrt(jnp.maximum(jnp.abs(value), 1e-30))
 
 
@@ -158,12 +173,18 @@
 
 
 def rows_kernel(
-    x_ref, w_ref, cell_ref, table_ref, out_ref, pack_ref, xb_ref, xt_ref, hot_ref, g_ref, b_ref, tw_ref
+    x_hbm, w_hbm, cell_hbm, table_hbm, out_ref,
+    x_ref, w_ref, cell_ref, table_ref, pack_ref, xb_ref, xt_ref, hot_ref, g_ref, b_ref, tw_ref, code_ref, sems,
 ):
-    for slab in range(12):
-        pack_ref[slab * 4 : slab * 4 + 4, :] = x_ref[slab].astype(F32)
-    xb_ref[...] = pack_ref[...].astype(BF16)
-    tw_ref[...] = twiddles(table_ref)
+    pairs = ((cell_hbm, cell_ref), (w_hbm, w_ref), (x_hbm, x_ref), (table_hbm, table_ref))
+    copies = [
+        pltpu.make_async_copy(source, target, sems.at[place])
+        for place, (source, target) in enumerate(pairs)
+    ]
+    for copy in copies:
+        copy.start()
+    copies[0].wait()
+    copies[1].wait()
     cells = cell_ref[...]
     upper = cells >> 8
     weight = w_ref[...]
@@ -174,6 +195,10 @@
         hit = place == (cells & 255)
         hot_ref[0, block * 16 : block * 16 + 16, :] = jnp.where(hit, high, 0.0).astype(BF16)
         hot_ref[1, block * 16 : block * 16 + 16, :] = jnp.where(hit, low, 0.0).astype(BF16)
+    copies[2].wait()
+    for slab in range(12):
+        pack_ref[slab * 4 : slab * 4 + 4, :] = x_ref[slab].astype(F32)
+    xb_ref[...] = pack_ref[...].astype(BF16)
     for part in range(32):
         mask = jnp.where(upper == part, 1.0, 0.0).astype(BF16)
         xt_ref[part * CHAN : (part + 1) * CHAN, :] = xb_ref[...] * mask
@@ -181,6 +206,9 @@
         rows = slice(chunk * 768, (chunk + 1) * 768)
         piece = xt_ref[rows, :]
         g_ref[rows, :] = dot(piece, hot_ref[0], 1, 1) + dot(piece, hot_ref[1], 1, 1)
+
+    copies[3].wait()
+    tw_ref[...] = twiddles(table_ref)
 
     def one_row(row):
         for t in range(3):
@@ -220,12 +248,16 @@
         result = coded(result)
         for part in range(2):
             for side in range(2):
-                out_ref[pl.ds(part * 12 + pair * 2 + side, 128, 24), :] = result[
+                code_ref[pl.ds(part * 12 + pair * 2 + side, 128, 24), :] = result[
                     part * 128 : (part + 1) * 128, side * 128 : (side + 1) * 128
                 ]
-
-
-def columns_kernel(r_ref, kern_ref, fwd_ref, inv_ref, tw_ref, lane_ref, out_ref, v_ref, u_ref, y_ref):
+    out_ref[...] = code_ref[...].astype(jnp.int16)
+
+
+def columns_kernel(
+    r_ref, kern_ref, fwd_ref, inv_ref, tw_ref, lane_ref, out_ref, v_ref, u_ref, y_ref, code_ref
+):
+    code_ref[...] = r_ref[...].astype(jnp.int32)
     sign = lane_ref[8:9, :]
 
     def swap(value):
@@ -237,9 +269,9 @@
     def spread(t):
         for part in range(2):
             for m in range(4):
-                v_ref[part * 128 : (part + 1) * 128, lanes_of(t, m)] = r_ref[
-                    pl.ds(part * 12 + m * 3 + t, 128, 24), :
-                ]
+                v_ref[part * 128 : (part + 1) * 128, lanes_of(t, m)] = decoded(
+                    code_ref[pl.ds(part * 12 + m * 3 + t, 128, 24), :]
+                )
         for chunk in range(2):
             lanes = slice((t * 2 + chunk) * 256, (t * 2 + chunk + 1) * 256)
             v_high, v_low = halves(v_ref[:, lanes])
@@ -272,7 +304,7 @@
         for chunk in range(2):
             lanes = slice((t * 2 + chunk) * 256, (t * 2 + chunk + 1) * 256)
             y_high, y_low = halves(y_ref[:, lanes])
-            result = coded(dot(inv_ref[0], y_high) + dot(inv_ref[0], y_low) + dot(inv_ref[1], y_high))
+            result = rooted(dot(inv_ref[0], y_high) + dot(inv_ref[0], y_low) + dot(inv_ref[1], y_high))
             for part in range(2):
                 for side in range(2):
                     out_ref[pl.ds(part * 12 + (chunk * 2 + side) * 3 + t, 128, 24), :] = result[
@@ -511,8 +543,13 @@
 def rows_call(x, w, cell, table):
     return pl.pallas_call(
         rows_kernel,
-        out_shape=shape((DEVICES * HALF, 128)),
+        in_specs=[pl.BlockSpec(memory_space=pltpu.HBM)] * 4,
+        out_shape=shape((DEVICES * HALF, 128), jnp.int16),
         scratch_shapes=[
+            pltpu.VMEM((12, 4, WIDTH), BF16),
+            pltpu.VMEM((1, WIDTH), F32),
+            pltpu.VMEM((1, WIDTH), jnp.int32),
+            pltpu.VMEM((640, 256), BF16),
             pltpu.VMEM((CHAN, WIDTH), F32),
             pltpu.VMEM((CHAN, WIDTH), BF16),
             pltpu.VMEM((1536, WIDTH), BF16),
@@ -520,8 +557,10 @@
             pltpu.VMEM((1536, 256), F32),
             pltpu.VMEM((1536, 256), F32),
             pltpu.VMEM((128, 128), F32),
+            pltpu.VMEM((DEVICES * HALF, 128), jnp.int32),
+            pltpu.SemaphoreType.DMA((4,)),
         ],
-        compiler_params=PARAMS,
+        compiler_params=pltpu.CompilerParams(vmem_limit_bytes=63 * MIB),
         cost_estimate=cost(3_800_000_000, 4 * MIB),
     )(x, w, cell, table)
 
@@ -550,7 +589,7 @@
     return pl.pallas_call(
         columns_kernel,
         out_shape=shape((DEVICES * HALF, 128)),
-        scratch_shapes=[pltpu.VMEM((256, 1536), F32)] * 3,
+        scratch_shapes=[pltpu.VMEM((256, 1536), F32)] * 3 + [pltpu.VMEM((DEVICES * HALF, 128), jnp.int32)],
         compiler_params=PARAMS,
         cost_estimate=cost(2_000_000_000, 6 * MIB),
     )(columns, transfer, forward, backward, column_table, lane_table)
@@ -582,10 +621,9 @@
 
 
 def exchange(message):
-    code = message.reshape(DEVICES, HALF, 128).astype(jnp.float16)
-    code = lax.all_to_all(code, AXES, split_axis=0, concat_axis=0, tiled=True)
-    code = code.astype(F32)
-    return (code * jnp.abs(code)).reshape(DEVICES * HALF, 128)
+    message = message.reshape(DEVICES, HALF, 128)
+    message = lax.all_to_all(message, AXES, split_axis=0, concat_axis=0, tiled=True)
+    return message.reshape(DEVICES * HALF, 128)
 
 
 def local(incident, jitter, weights, cells, pair_list, pair_count, kernel):
@@ -612,7 +650,8 @@
         jnp.asarray(column_twiddle()),
         jnp.asarray(lane_twiddle()),
     )
-    rows = exchange(message)
+    code = exchange(message.astype(jnp.float16)).astype(F32)
+    rows = code * jnp.abs(code)
 
     spots = jnp.concatenate(
         [

time: 68.2 us -> 66.4 us (0.974)
  local copies, waits for them, and re-layouts: 4.03 us -> 0.74 us
  waiting for transfers between devices: 10.8 us -> 12 us
  other arithmetic: 2.43 us -> 1.32 us
  Pallas kernels: 16.7 us -> 17.8 us
    unnamed x33 -> x25, local copies, waits for them, and re-layouts: 3.45 us -> 0.16 us
    pallas_call x1, Pallas kernels: 4.45 us -> 6.89 us  [rows_call(): pl.pallas_call(rows_kernel, in_specs=[pl.BlockSpec(memory_space=pltpu.HBM...]
    pallas_call x1, Pallas kernels: 3.91 us -> 2.28 us  [near_call(): pl.pallas_call(near_kernel, in_specs=[pl.BlockSpec(memory_space=pltpu.SME...]
    ppermute x6, waiting for transfers between devices: 4.02 us -> 5.2 us  [shift(): return lax.ppermute(value, AXES, pairs)]
    convert_element_type x2 -> x1, other arithmetic: 1.98 us -> 0.99 us  [local(): code = exchange(message.astype(jnp.float16)).astype(F32)]
  transfers between devices with their start and end apart: 8 -> 8, of which waited for: 4 -> 4; matrix products, arithmetic and copies ran while one was open for 3% -> 3% of each run, Pallas kernels for 17% -> 15%
where the time goes in v4:
time: 66.4 us; the launch traced here: 66 us
  starting transfers between devices  33.2 us (50%)
  Pallas kernels  17.8 us (27%)
  waiting for transfers between devices  12 us (18%)
  other arithmetic  1.32 us (2%)
  between operations  1 us (2%)
  local copies, waits for them, and re-layouts  0.74 us (1%)
    ppermute x6, starting transfers between devices, shift(): return lax.ppermute(value, AXES, pairs)  16.9 us
    all_to_all x2, starting transfers between devices, exchange(): lax.all_to_all(message, AXES, split_axis=0, concat_axis=0, tiled=True)  16.3 us
    pallas_call x1, Pallas kernels, rows_call(): pl.pallas_call(rows_kernel, in_specs=[pl.BlockSpec(memory_space=pltpu.HBM...  6.89 us
    all_to_all x2, waiting for transfers between devices, exchange(): lax.all_to_all(message, AXES, split_axis=0, concat_axis=0, tiled=True)  6.81 us
    ppermute x6, waiting for transfers between devices, shift(): return lax.ppermute(value, AXES, pairs)  5.2 us
    pallas_call x1, Pallas kernels, sample_call(): pl.pallas_call(sample_kernel, out_shape=shape((CHAN, WIDTH)), scratch_sha...  4.53 us
    pallas_call x1, Pallas kernels, columns_call(): pl.pallas_call(columns_kernel, out_shape=shape((DEVICES * HALF, 128)), sc...  3.14 us
    pallas_call x1, Pallas kernels, near_call(): pl.pallas_call(near_kernel, in_specs=[pl.BlockSpec(memory_space=pltpu.SME...  2.28 us
  transfers between devices with their start and end apart: 8, of which 4 were waited for; matrix products, arithmetic and copies ran while one was open for 3% of the time, Pallas kernels for 15%

profile of v4, /device:TPU:1, one launch (start us, length us, event | category | flops | bytes accessed | tf_op | source)
XLA Modules:
  0.0 66.0 jit_solution(433783119804376193)
XLA Ops:
  0.0 6.9 %shard_map.127 = s16[3072,128]{1,0:T(8,128)(2,1)} custom-call(bf16[12,4,2048]{2,1,0:T(4,128)(2,1)} %bitcast.22, f32[1,2048]{1,0:T(1,128)} %bitcast.24, s32[1,2048]{1,0:T(1,128)} %bitcast.26, bf16[640,256]{1,0:T(8,128)(2,1)} %constant.22.clone.table_hbm.table_ref), custom_call_target="tpu_custom_call" | custom-call | flops 3800000000 | bytes 4194304 | tf_op jit(solution)/shard_map/pallas_call | solution.py:544
  6.9 0.0 copy-start
  6.9 0.0 copy-start.1
  6.9 0.0 copy-start.10
  6.9 11.5 %all-to-all-start = ((s16[128,24,128]{2,1,0:T(8,128)(2,1)}), s16[128,24,128]{2,1,0:T(8,128)(2,1)S(1)}, u32[]{:S(2)}, u32[]{:S(2)}) async-start(s16[128,24,128]{2,1,0:T(8,128)(2,1)} %bitcast.28), calls=%async_computation | async-start | bytes 1572864 | tf_op jit(solution)/shard_map/all_to_all | solution.py:625
  18.5 0.0 copy-done
  18.5 0.0 copy-done.1
  18.5 0.0 copy-start.11
  18.5 0.1 shard_map.130
  18.6 0.0 copy-start.4
  18.6 0.0 copy-start.6
  18.6 0.0 copy-start.7
  18.6 0.0 copy-start.9
  18.6 1.4 %collective-permute-start = (bf16[64,512]{1,0:T(8,128)(2,1)S(1)}, bf16[64,512]{1,0:T(8,128)(2,1)S(1)}, u32[]{:S(2)}, u32[]{:S(2)}) collective-permute-start(bf16[64,512]{1,0:T(8,128)(2,1)S(1)} %get-tuple-element.15), channel_id=1, source_target_pairs={{8,1},{9,2},{10,3},{11,4},{12,5},{13,6},{14,7},{15,0},{16,9},{17,1... | collective-permute-start | bytes 196616 | tf_op jit(solution)/shard_map/ppermute | solution.py:518
  20.1 5.5 %collective-permute-start.2 = (bf16[64,128]{1,0:T(8,128)(2,1)S(1)}, bf16[64,128]{1,0:T(8,128)(2,1)S(1)}, u32[]{:S(2)}, u32[]{:S(2)}) collective-permute-start(bf16[64,128]{1,0:T(8,128)(2,1)S(1)} %get-tuple-element.16), channel_id=1, source_target_pairs={{0,9},{1,10},{2,11},{3,12},{4,13},{5,14},{6,15},{7,8},{8,17},{9,18... | collective-permute-start | bytes 49160 | tf_op jit(solution)/shard_map/ppermute | solution.py:518
  25.6 0.0 copy-done.10
  25.6 0.1 broadcast_in_dim.2
  25.7 0.2 reshape.46
  25.9 0.2 copy.17.kern_ref
  26.8 0.0 copy-done.11
  26.8 0.1 copy.18
  26.9 0.1 reshape.48
  26.9 0.1 pad_add_fusion.list_ref
  27.0 2.8 %collective-permute-done.side_ref = bf16[64,512]{1,0:T(8,128)(2,1)S(1)} collective-permute-done((bf16[64,512]{1,0:T(8,128)(2,1)S(1)}, bf16[64,512]{1,0:T(8,128)(2,1)S(1)}, u32[]{:S(2)}, u32[]{:S(2)}) %collective-permute-start) | collective-permute-done | bytes 65568 | tf_op jit(solution)/shard_map/ppermute | solution.py:518
  29.8 2.4 %collective-permute-start.1 = (bf16[64,1024]{1,0:T(8,128)(2,1)S(1)}, bf16[64,1024]{1,0:T(8,128)(2,1)S(1)}, u32[]{:S(2)}, u32[]{:S(2)}) collective-permute-start(bf16[64,1024]{1,0:T(8,128)(2,1)S(1)} %pad_maximum_fusion), channel_id=1, source_target_pairs={{0,7},{1,0},{2,1},{3,2},{4,3},{5,4},{6,5},{7,6},{8,15},{9,8},{10,9... | collective-permute-start | bytes 393224 | tf_op jit(solution)/shard_map/ppermute | solution.py:518
  32.2 2.7 %all-to-all-done = s16[128,24,128]{2,1,0:T(8,128)(2,1)S(1)} async-done(((s16[128,24,128]{2,1,0:T(8,128)(2,1)}), s16[128,24,128]{2,1,0:T(8,128)(2,1)S(1)}, u32[]{:S(2)}, u32[]{:S(2)}) %all-to-all-start) | async-done | bytes 786464 | tf_op jit(solution)/shard_map/all_to_all | solution.py:625
  34.9 0.0 copy-done.4
  34.9 0.0 copy-done.6
  34.9 3.1 %shard_map.128 = f32[3072,128]{1,0:T(8,128)S(1)} custom-call(s16[3072,128]{1,0:T(8,128)(2,1)S(1)} %bitcast.21, f32[2,512,128]{2,1,0:T(8,128)S(1)} %copy.17.kern_ref, bf16[2,256,256]{2,1,0:T(8,128)(2,1)S(1)} %copy-done.6, bf16[2,256,256]{2,1,0:T(8,128)(2,1)S(1)} %copy-done.7, f32[2,512,128]{2,1,0:T(8,128)S(1)} %copy-done.4, f32[16,128]{1,0:T(8,128)S(1)} %copy-done.9), custom_call_target="tpu_custom_call" | custom-call | flops 2000000000 | bytes 6291456 | tf_op jit(solution)/shard_map/pallas_call | solution.py:589
  38.1 0.0 copy-start.8
  38.1 1.0 %convert_element_type.9 = f16[3072,128]{1,0:T(8,128)(2,1)} convert(f32[3072,128]{1,0:T(8,128)S(1)} %shard_map.128) | non-fusion elementwise | flops 393216 | bytes 2359296 | tf_op jit(solution)/shard_map/convert_element_type | solution.py:653
  39.1 4.8 %all-to-all-start.1 = ((f16[128,24,128]{2,1,0:T(8,128)(2,1)}), f16[128,24,128]{2,1,0:T(8,128)(2,1)S(1)}, u32[]{:S(2)}, u32[]{:S(2)}) async-start(f16[128,24,128]{2,1,0:T(8,128)(2,1)} %bitcast.8), calls=%async_computation.1 | async-start | bytes 1572864 | tf_op jit(solution)/shard_map/all_to_all | solution.py:625
  43.9 0.0 collective-permute-done.2.four_ref
  43.9 0.0 collective-permute-done.1.both_ref
  43.9 2.3 %shard_map.131 = (f32[48,2048]{1,0:T(8,128)S(1)}, bf16[48,512]{1,0:T(8,128)(2,1)S(1)}, bf16[48,640]{1,0:T(8,128)(2,1)S(1)}, bf16[48,128]{1,0:T(8,128)(2,1)S(1)}) custom-call(s32[27]{0:T(128)S(1)} %pad_add_fusion.list_ref, bf16[64,2048]{1,0:T(8,128)(2,1)S(1)} %get-tuple-element.13.own_ref, bf16[64,1024]{1,0:T(8,128)(2,1)S(1)} %collective-permute-done.1.both_ref, ...), custom_call_target="tpu_custom_call" | custom-call | flops 8000000000 | bytes 4194304 | tf_op jit(solution)/shard_map/pallas_call | solution.py:569
  46.2 0.0 copy-start.2
  46.2 0.0 copy-start.3
  46.2 0.0 copy-start.5
  46.2 3.7 %collective-permute-start.3 = (bf16[48,640]{1,0:T(8,128)(2,1)S(1)}, bf16[48,640]{1,0:T(8,128)(2,1)S(1)}, u32[]{:S(2)}, u32[]{:S(2)}) collective-permute-start(bf16[48,640]{1,0:T(8,128)(2,1)S(1)} %get-tuple-element.19), channel_id=1, source_target_pairs={{0,15},{1,8},{2,9},{3,10},{4,11},{5,12},{6,13},{7,14},{8,23},{9,16... | collective-permute-start | bytes 184328 | tf_op jit(solution)/shard_map/ppermute | solution.py:518
  49.9 1.5 %collective-permute-start.5 = (bf16[48,128]{1,0:T(8,128)(2,1)S(1)}, bf16[48,128]{1,0:T(8,128)(2,1)S(1)}, u32[]{:S(2)}, u32[]{:S(2)}) collective-permute-start(bf16[48,128]{1,0:T(8,128)(2,1)S(1)} %get-tuple-element.20), channel_id=1, source_target_pairs={{8,7},{9,0},{10,1},{11,2},{12,3},{13,4},{14,5},{15,6},{16,15},{17,... | collective-permute-start | bytes 36872 | tf_op jit(solution)/shard_map/ppermute | solution.py:518
  51.4 2.4 %collective-permute-done.3.side_ref = bf16[48,640]{1,0:T(8,128)(2,1)S(1)} collective-permute-done((bf16[48,640]{1,0:T(8,128)(2,1)S(1)}, bf16[48,640]{1,0:T(8,128)(2,1)S(1)}, u32[]{:S(2)}, u32[]{:S(2)}) %collective-permute-start.3) | collective-permute-done | bytes 61472 | tf_op jit(solution)/shard_map/ppermute | solution.py:518
  53.8 2.4 %collective-permute-start.4 = (bf16[48,1024]{1,0:T(8,128)(2,1)S(1)}, bf16[48,1024]{1,0:T(8,128)(2,1)S(1)}, u32[]{:S(2)}, u32[]{:S(2)}) collective-permute-start(bf16[48,1024]{1,0:T(8,128)(2,1)S(1)} %pad_maximum_fusion.1), channel_id=1, source_target_pairs={{0,1},{1,2},{2,3},{3,4},{4,5},{5,6},{6,7},{7,0},{8,9},{9,10},{10,1... | collective-permute-start | bytes 294920 | tf_op jit(solution)/shard_map/ppermute | solution.py:518
  56.2 4.1 %all-to-all-done.1 = f16[128,24,128]{2,1,0:T(8,128)(2,1)S(1)} async-done(((f16[128,24,128]{2,1,0:T(8,128)(2,1)}), f16[128,24,128]{2,1,0:T(8,128)(2,1)S(1)}, u32[]{:S(2)}, u32[]{:S(2)}) %all-to-all-start.1) | async-done | bytes 786464 | tf_op jit(solution)/shard_map/all_to_all | solution.py:625
  60.4 0.2 abs_multiply_fusion.r_ref
  60.6 4.5 %shard_map.129.far_ref = f32[48,2048]{1,0:T(8,128)S(1)} custom-call(f32[3072,128]{1,0:T(8,128)S(1)} %abs_multiply_fusion.r_ref, f32[1,2048]{1,0:T(1,128)S(1)} %bitcast.25, s32[1,2048]{1,0:T(1,128)S(1)} %bitcast.27, bf16[640,256]{1,0:T(8,128)(2,1)S(1)} %copy-done.5), custom_call_target="tpu_custom_call" | custom-call | flops 3800000000 | bytes 4194304 | tf_op jit(solution)/shard_map/pallas_call | solution.py:599
  65.2 0.0 collective-permute-done.5.four_ref
  65.2 0.0 collective-permute-done.4.both_ref
  65.2 0.8 %shard_map.132 = f32[12,4,2048]{2,1,0:T(4,128)} custom-call(f32[48,2048]{1,0:T(8,128)S(1)} %shard_map.129.far_ref, f32[48,2048]{1,0:T(8,128)S(1)} %get-tuple-element.17.near_ref, bf16[48,1024]{1,0:T(8,128)(2,1)S(1)} %collective-permute-done.4.both_ref, bf16[48,640]{1,0:T(8,128)(2,1)S(1)} %collective-permute-done.3.side_ref, ...), custom_call_target="tpu_custom_call" | custom-call | flops 1000000 | bytes 2097152 | tf_op jit(solution)/shard_map/pallas_call | solution.py:614
  (10 shorter events, 0.1 us)
Async XLA Ops:
  6.9 11.6 %copy-start = (bf16[2,4,6,2048]{3,1,2,0:T(4,128)(2,1)S(1)}, bf16[2,4,6,2048]{3,1,2,0:T(4,128)(2,1)}, u32[]{:S(2)}) copy-start(bf16[2,4,6,2048]{3,1,2,0:T(4,128)(2,1)} %param.13) | copy-start | bytes 589828
  6.9 11.6 %copy-start.1 = (bf16[2,2048]{1,0:T(2,128)(2,1)S(1)}, bf16[2,2048]{1,0:T(2,128)(2,1)}, u32[]{:S(2)}) copy-start(bf16[2,2048]{1,0:T(2,128)(2,1)} %jitter_ref.1) | copy-start | bytes 24580
  6.9 18.7 %copy-start.10 = (f32[2,1024,8]{1,2,0:T(8,128)S(1)}, f32[2,1024,8]{1,2,0:T(8,128)}, u32[]{:S(2)}) copy-start(f32[2,1024,8]{1,2,0:T(8,128)} %param.19) | copy-start | bytes 196612
  6.9 28.0 %all-to-all-start = ((s16[128,24,128]{2,1,0:T(8,128)(2,1)}), s16[128,24,128]{2,1,0:T(8,128)(2,1)S(1)}, u32[]{:S(2)}, u32[]{:S(2)}) async-start(s16[128,24,128]{2,1,0:T(8,128)(2,1)} %bitcast.28), calls=%async_computation | async-start | bytes 1572864 | tf_op jit(solution)/shard_map/all_to_all | solution.py:625
  18.5 8.3 %copy-start.11 = (s32[1,8,3]{1,0,2:T(1,128)S(1)}, s32[1,8,3]{1,0,2:T(1,128)}, u32[]{:S(2)}) copy-start(s32[1,8,3]{1,0,2:T(1,128)} %param.17) | copy-start | bytes 292
  18.6 16.3 %copy-start.4 = (f32[2,512,128]{2,1,0:T(8,128)S(1)}, f32[2,512,128]{2,1,0:T(8,128)}, u32[]{:S(2)}) copy-start(f32[2,512,128]{2,1,0:T(8,128)} %constant.24.clone.tw_ref) | copy-start | bytes 1572868
  18.6 16.3 %copy-start.6 = (bf16[2,256,256]{2,1,0:T(8,128)(2,1)S(1)}, bf16[2,256,256]{2,1,0:T(8,128)(2,1)}, u32[]{:S(2)}) copy-start(bf16[2,256,256]{2,1,0:T(8,128)(2,1)} %constant.21.clone.fwd_ref) | copy-start | bytes 786436
  18.6 16.3 %copy-start.7 = (bf16[2,256,256]{2,1,0:T(8,128)(2,1)S(1)}, bf16[2,256,256]{2,1,0:T(8,128)(2,1)}, u32[]{:S(2)}) copy-start(bf16[2,256,256]{2,1,0:T(8,128)(2,1)} %constant.23.clone.inv_ref) | copy-start | bytes 786436
  18.6 16.3 %copy-start.9 = (f32[16,128]{1,0:T(8,128)S(1)}, f32[16,128]{1,0:T(8,128)}, u32[]{:S(2)}) copy-start(f32[16,128]{1,0:T(8,128)} %constant.25.clone.lane_ref) | copy-start | bytes 24580
  18.6 11.2 %collective-permute-start = (bf16[64,512]{1,0:T(8,128)(2,1)S(1)}, bf16[64,512]{1,0:T(8,128)(2,1)S(1)}, u32[]{:S(2)}, u32[]{:S(2)}) collective-permute-start(bf16[64,512]{1,0:T(8,128)(2,1)S(1)} %get-tuple-element.15), channel_id=1, source_target_pairs={{8,1},{9,2},{10,3},{11,4},{12,5},{13,6},{14,7},{15,0},{16,9},{17,1... | collective-permute-start | bytes 196616 | tf_op jit(solution)/shard_map/ppermute | solution.py:518
  20.1 23.8 %collective-permute-start.2 = (bf16[64,128]{1,0:T(8,128)(2,1)S(1)}, bf16[64,128]{1,0:T(8,128)(2,1)S(1)}, u32[]{:S(2)}, u32[]{:S(2)}) collective-permute-start(bf16[64,128]{1,0:T(8,128)(2,1)S(1)} %get-tuple-element.16), channel_id=1, source_target_pairs={{0,9},{1,10},{2,11},{3,12},{4,13},{5,14},{6,15},{7,8},{8,17},{9,18... | collective-permute-start | bytes 49160 | tf_op jit(solution)/shard_map/ppermute | solution.py:518
  29.8 14.1 %collective-permute-start.1 = (bf16[64,1024]{1,0:T(8,128)(2,1)S(1)}, bf16[64,1024]{1,0:T(8,128)(2,1)S(1)}, u32[]{:S(2)}, u32[]{:S(2)}) collective-permute-start(bf16[64,1024]{1,0:T(8,128)(2,1)S(1)} %pad_maximum_fusion), channel_id=1, source_target_pairs={{0,7},{1,0},{2,1},{3,2},{4,3},{5,4},{6,5},{7,6},{8,15},{9,8},{10,9... | collective-permute-start | bytes 393224 | tf_op jit(solution)/shard_map/ppermute | solution.py:518
  38.1 5.8 %copy-start.8 = (bf16[576,48]{1,0:T(8,128)(2,1)S(1)}, bf16[576,48]{1,0:T(8,128)(2,1)}, u32[]{:S(2)}) copy-start(bf16[576,48]{1,0:T(8,128)(2,1)} %constant.26.clone.mix_ref) | copy-start | bytes 165892
  39.1 21.3 %all-to-all-start.1 = ((f16[128,24,128]{2,1,0:T(8,128)(2,1)}), f16[128,24,128]{2,1,0:T(8,128)(2,1)S(1)}, u32[]{:S(2)}, u32[]{:S(2)}) async-start(f16[128,24,128]{2,1,0:T(8,128)(2,1)} %bitcast.8), calls=%async_computation.1 | async-start | bytes 1572864 | tf_op jit(solution)/shard_map/all_to_all | solution.py:625
  46.2 14.4 %copy-start.2 = (f32[2048]{0:T(1024)S(1)}, f32[2048]{0:T(1024)}, u32[]{:S(2)}) copy-start(f32[2048]{0:T(1024)} %param.15) | copy-start | bytes 24580
  46.2 14.4 %copy-start.3 = (s32[2048]{0:T(1024)S(1)}, s32[2048]{0:T(1024)}, u32[]{:S(2)}) copy-start(s32[2048]{0:T(1024)} %param.16) | copy-start | bytes 24580
  46.2 14.4 %copy-start.5 = (bf16[640,256]{1,0:T(8,128)(2,1)S(1)}, bf16[640,256]{1,0:T(8,128)(2,1)}, u32[]{:S(2)}) copy-start(bf16[640,256]{1,0:T(8,128)(2,1)} %constant.22.clone.table_hbm.table_ref) | copy-start | bytes 983044
  46.2 7.6 %collective-permute-start.3 = (bf16[48,640]{1,0:T(8,128)(2,1)S(1)}, bf16[48,640]{1,0:T(8,128)(2,1)S(1)}, u32[]{:S(2)}, u32[]{:S(2)}) collective-permute-start(bf16[48,640]{1,0:T(8,128)(2,1)S(1)} %get-tuple-element.19), channel_id=1, source_target_pairs={{0,15},{1,8},{2,9},{3,10},{4,11},{5,12},{6,13},{7,14},{8,23},{9,16... | collective-permute-start | bytes 184328 | tf_op jit(solution)/shard_map/ppermute | solution.py:518
  49.9 15.2 %collective-permute-start.5 = (bf16[48,128]{1,0:T(8,128)(2,1)S(1)}, bf16[48,128]{1,0:T(8,128)(2,1)S(1)}, u32[]{:S(2)}, u32[]{:S(2)}) collective-permute-start(bf16[48,128]{1,0:T(8,128)(2,1)S(1)} %get-tuple-element.20), channel_id=1, source_target_pairs={{8,7},{9,0},{10,1},{11,2},{12,3},{13,4},{14,5},{15,6},{16,15},{17,... | collective-permute-start | bytes 36872 | tf_op jit(solution)/shard_map/ppermute | solution.py:518
  53.8 11.4 %collective-permute-start.4 = (bf16[48,1024]{1,0:T(8,128)(2,1)S(1)}, bf16[48,1024]{1,0:T(8,128)(2,1)S(1)}, u32[]{:S(2)}, u32[]{:S(2)}) collective-permute-start(bf16[48,1024]{1,0:T(8,128)(2,1)S(1)} %pad_maximum_fusion.1), channel_id=1, source_target_pairs={{0,1},{1,2},{2,3},{3,4},{4,5},{5,6},{6,7},{7,0},{8,9},{9,10},{10,1... | collective-permute-start | bytes 294920 | tf_op jit(solution)/shard_map/ppermute | solution.py:518

commit v5 on v4

--- a/solution.py
+++ b/solution.py
@@ -113,8 +113,12 @@
     return jnp.exp2(jnp.abs(code) * (1.0 / STEP) - FLOOR) * jnp.clip(code, -1.0, 1.0)
 
 
-def rooted(value):
-    return value * lax.rsqrt(jnp.maximum(jnp.abs(value), 1e-30))
+def packed(real, imag):
+    return (coded(real) << 16) | (coded(imag) & 0xFFFF)
+
+
+def unpacked(word):
+    return decoded(word >> 16), decoded((word << 16) >> 16)
 
 
 def cadd(left, right):
@@ -174,7 +178,7 @@
 
 def rows_kernel(
     x_hbm, w_hbm, cell_hbm, table_hbm, out_ref,
-    x_ref, w_ref, cell_ref, table_ref, pack_ref, xb_ref, xt_ref, hot_ref, g_ref, b_ref, tw_ref, code_ref, sems,
+    x_ref, w_ref, cell_ref, table_ref, pack_ref, xb_ref, xt_ref, hot_ref, g_ref, b_ref, tw_ref, sems,
 ):
     pairs = ((cell_hbm, cell_ref), (w_hbm, w_ref), (x_hbm, x_ref), (table_hbm, table_ref))
     copies = [
@@ -245,19 +249,12 @@
             + dot(table_ref[0:256, :], b_low, 1, 1)
             + dot(table_ref[256:512, :], b_high, 1, 1)
         )
-        result = coded(result)
-        for part in range(2):
-            for side in range(2):
-                code_ref[pl.ds(part * 12 + pair * 2 + side, 128, 24), :] = result[
-                    part * 128 : (part + 1) * 128, side * 128 : (side + 1) * 128
-                ]
-    out_ref[...] = code_ref[...].astype(jnp.int16)
-
-
-def columns_kernel(
-    r_ref, kern_ref, fwd_ref, inv_ref, tw_ref, lane_ref, out_ref, v_ref, u_ref, y_ref, code_ref
-):
-    code_ref[...] = r_ref[...].astype(jnp.int32)
+        for side in range(2):
+            lanes = slice(side * 128, (side + 1) * 128)
+            out_ref[pl.ds(pair * 2 + side, 128, 12), :] = packed(result[0:128, lanes], result[128:256, lanes])
+
+
+def columns_kernel(r_ref, kern_ref, fwd_ref, inv_ref, tw_ref, lane_ref, out_ref, v_ref, u_ref, y_ref):
     sign = lane_ref[8:9, :]
 
     def swap(value):
@@ -267,11 +264,10 @@
         return slice((t * 4 + m) * 128, (t * 4 + m + 1) * 128)
 
     def spread(t):
-        for part in range(2):
-            for m in range(4):
-                v_ref[part * 128 : (part + 1) * 128, lanes_of(t, m)] = decoded(
-                    code_ref[pl.ds(part * 12 + m * 3 + t, 128, 24), :]
-                )
+        for m in range(4):
+            real, imag = unpacked(r_ref[pl.ds(m * 3 + t, 128, 12), :])
+            v_ref[0:128, lanes_of(t, m)] = real
+            v_ref[128:256, lanes_of(t, m)] = imag
         for chunk in range(2):
             lanes = slice((t * 2 + chunk) * 256, (t * 2 + chunk + 1) * 256)
             v_high, v_low = halves(v_ref[:, lanes])
@@ -304,12 +300,12 @@
         for chunk in range(2):
             lanes = slice((t * 2 + chunk) * 256, (t * 2 + chunk + 1) * 256)
             y_high, y_low = halves(y_ref[:, lanes])
-            result = rooted(dot(inv_ref[0], y_high) + dot(inv_ref[0], y_low) + dot(inv_ref[1], y_high))
-            for part in range(2):
-                for side in range(2):
-                    out_ref[pl.ds(part * 12 + (chunk * 2 + side) * 3 + t, 128, 24), :] = result[
-                        part * 128 : (part + 1) * 128, side * 128 : (side + 1) * 128
-                    ]
+            result = dot(inv_ref[0], y_high) + dot(inv_ref[0], y_low) + dot(inv_ref[1], y_high)
+            for side in range(2):
+                lanes = slice(side * 128, (side + 1) * 128)
+                out_ref[pl.ds((chunk * 2 + side) * 3 + t, 128, 12), :] = packed(
+                    result[0:128, lanes], result[128:256, lanes]
+                )
 
     spread(0)
     spread(1)
@@ -323,21 +319,29 @@
 
 
 def sample_kernel(
-    r_ref, w_ref, cell_ref, table_ref, sum_ref, v_ref, g_ref, f_ref, tw_ref
+    r_ref, w_ref, cell_ref, table_ref, sum_ref, v_ref, g_ref, grid_ref, hot_ref, tw_ref
 ):
     tw_ref[...] = twiddles(table_ref)
-    for part in range(2):
-        for group in range(12):
-            piece = r_ref[pl.ds(part * 12 + group, 128, 24), :]
-            v_ref[group * 128 : (group + 1) * 128, part * 128 : (part + 1) * 128] = piece.T
-    for chunk in range(2):
-        rows = slice(chunk * 768, (chunk + 1) * 768)
+    upper = cell_ref[...] >> 8
+    for block in range(16):
+        place = lax.broadcasted_iota(jnp.int32, (16, WIDTH), 0) + block * 16
+        hit = place == (cell_ref[...] & 255)
+        hot_ref[block * 16 : block * 16 + 16, :] = jnp.where(hit, 1.0, 0.0).astype(BF16)
+
+    def spread(m):
+        for group in range(m * 3, m * 3 + 3):
+            real, imag = unpacked(r_ref[pl.ds(group, 128, 12), :])
+            v_ref[group * 128 : (group + 1) * 128, 0:128] = real.T
+            v_ref[group * 128 : (group + 1) * 128, 128:256] = imag.T
+        rows = slice(m * 384, (m + 1) * 384)
         v_high, v_low = halves(v_ref[rows, :])
         g_ref[rows, :] = (
             dot(v_high, table_ref[0:256, :])
             + dot(v_low, table_ref[0:256, :])
             + dot(v_high, table_ref[256:512, :])
         )
+        one_row(2 * m)
+        one_row(2 * m + 1)
 
     def one_row(row):
         for t in range(3):
@@ -357,28 +361,27 @@
             for n1 in range(8):
                 start = (row * 4 + n1 // 2) * CHAN + t * 8
                 lanes = slice((n1 % 2) * 128, (n1 % 2) * 128 + 128)
-                v_ref[pl.ds(pl.multiple_of(start, 8), 8), lanes] = values[n1][0]
-                v_ref[pl.ds(pl.multiple_of(start + HALF, 8), 8), lanes] = values[n1][1]
-
-    for row in range(8):
-        one_row(row)
-    f_high, f_low = halves(v_ref[...])
-    f_ref[0] = f_high
-    f_ref[1] = f_low
-    place = lax.broadcasted_iota(jnp.int32, (256, 256), 0)
-    for chunk in range(8):
-        lanes = slice(chunk * 256, (chunk + 1) * 256)
-        cells = cell_ref[:, lanes]
-        hot = jnp.where(place == (cells & 255), 1.0, 0.0).astype(BF16)
-        upper = cells >> 8
-        total = jnp.zeros((CHAN, 256), F32)
-        for quarter in range(4):
-            rows = slice(quarter * 384, (quarter + 1) * 384)
-            picked = dot(f_ref[0, rows, :], hot) + dot(f_ref[1, rows, :], hot)
+                grid_ref[pl.ds(pl.multiple_of(start, 8), 8), lanes] = values[n1][0]
+                grid_ref[pl.ds(pl.multiple_of(start + HALF, 8), 8), lanes] = values[n1][1]
+
+    def sample(m):
+        rows = slice(m * 384, (m + 1) * 384)
+        high, low = halves(grid_ref[rows, :])
+        for chunk in range(8):
+            lanes = slice(chunk * 256, (chunk + 1) * 256)
+            picked = dot(high, hot_ref[:, lanes]) + dot(low, hot_ref[:, lanes])
+            total = jnp.zeros((CHAN, 256), F32) if m == 0 else sum_ref[:, lanes]
             for part in range(8):
-                hit = jnp.broadcast_to(upper == quarter * 8 + part, (CHAN, 256))
+                hit = jnp.broadcast_to(upper[:, lanes] == m * 8 + part, (CHAN, 256))
                 total = total + jnp.where(hit, picked[part * CHAN : (part + 1) * CHAN, :], 0.0)
-        sum_ref[:, lanes] = total * w_ref[:, lanes]
+            sum_ref[:, lanes] = total * w_ref[:, lanes] if m == 3 else total
+
+    spread(0)
+    for m in range(4):
+        if m < 3:
+            spread(m + 1)
+        sample(m)
+
 
 def finish_kernel(far_ref, near_ref, both_ref, side_ref, four_ref, out_ref, sum_ref):
     sum_ref[...] = far_ref[...] + near_ref[...]
@@ -544,7 +547,7 @@
     return pl.pallas_call(
         rows_kernel,
         in_specs=[pl.BlockSpec(memory_space=pltpu.HBM)] * 4,
-        out_shape=shape((DEVICES * HALF, 128), jnp.int16),
+        out_shape=shape((DEVICES * 12, 128), jnp.int32),
         scratch_shapes=[
             pltpu.VMEM((12, 4, WIDTH), BF16),
             pltpu.VMEM((1, WIDTH), F32),
@@ -557,7 +560,6 @@
             pltpu.VMEM((1536, 256), F32),
             pltpu.VMEM((1536, 256), F32),
             pltpu.VMEM((128, 128), F32),
-            pltpu.VMEM((DEVICES * HALF, 128), jnp.int32),
             pltpu.SemaphoreType.DMA((4,)),
         ],
         compiler_params=pltpu.CompilerParams(vmem_limit_bytes=63 * MIB),
@@ -588,8 +590,8 @@
 def columns_call(columns, transfer, forward, backward, column_table, lane_table):
     return pl.pallas_call(
         columns_kernel,
-        out_shape=shape((DEVICES * HALF, 128)),
-        scratch_shapes=[pltpu.VMEM((256, 1536), F32)] * 3 + [pltpu.VMEM((DEVICES * HALF, 128), jnp.int32)],
+        out_shape=shape((DEVICES * 12, 128), jnp.int32),
+        scratch_shapes=[pltpu.VMEM((256, 1536), F32)] * 3,
         compiler_params=PARAMS,
         cost_estimate=cost(2_000_000_000, 6 * MIB),
     )(columns, transfer, forward, backward, column_table, lane_table)
@@ -602,7 +604,8 @@
         scratch_shapes=[
             pltpu.VMEM((1536, 256), F32),
             pltpu.VMEM((1536, 256), F32),
-            pltpu.VMEM((2, 1536, 256), BF16),
+            pltpu.VMEM((1536, 256), F32),
+            pltpu.VMEM((256, WIDTH), BF16),
             pltpu.VMEM((128, 128), F32),
         ],
         compiler_params=PARAMS,
@@ -621,9 +624,9 @@
 
 
 def exchange(message):
-    message = message.reshape(DEVICES, HALF, 128)
+    message = message.reshape(DEVICES * 3, 4, 128)
     message = lax.all_to_all(message, AXES, split_axis=0, concat_axis=0, tiled=True)
-    return message.reshape(DEVICES * HALF, 128)
+    return message.reshape(DEVICES * 12, 128)
 
 
 def local(incident, jitter, weights, cells, pair_list, pair_count, kernel):
@@ -650,8 +653,7 @@
         jnp.asarray(column_twiddle()),
         jnp.asarray(lane_twiddle()),
     )
-    code = exchange(message.astype(jnp.float16)).astype(F32)
-    rows = code * jnp.abs(code)
+    rows = exchange(message)
 
     spots = jnp.concatenate(
         [

time: 66.4 us -> 66.1 us (level)
  other arithmetic: 1.32 us -> 0.1 us
    convert_element_type x1 -> x0, other arithmetic: 0.99 us -> none  [local(): code = exchange(message.astype(jnp.float16)).astype(F32)]
    ppermute x6, waiting for transfers between devices: 5.2 us -> 4.3 us  [shift(): return lax.ppermute(value, AXES, pairs)]
    pallas_call x1, Pallas kernels: 3.14 us -> 4.03 us  [columns_call(): pl.pallas_call(columns_kernel, out_shape=shape((DEVICES * 12, 128), jnp.i...]
    all_to_all x2, waiting for transfers between devices: 6.81 us -> 7.64 us  [exchange(): lax.all_to_all(message, AXES, split_axis=0, concat_axis=0, tiled=True)]
  transfers between devices with their start and end apart: 8 -> 8, of which waited for: 4 -> 4; matrix products, arithmetic and copies ran while one was open for 3% -> 1% of each run, Pallas kernels for 15% -> 16%
where the time goes in v5:
time: 66.1 us; the launch traced here: 65.6 us
  starting transfers between devices  33.6 us (51%)
  Pallas kernels  18.3 us (28%)
  waiting for transfers between devices  11.9 us (18%)
  between operations  0.98 us (1%)
  local copies, waits for them, and re-layouts  0.72 us (1%)
    ppermute x6, starting transfers between devices, shift(): return lax.ppermute(value, AXES, pairs)  16.9 us
    all_to_all x2, starting transfers between devices, exchange(): lax.all_to_all(message, AXES, split_axis=0, concat_axis=0, tiled=True)  16.7 us
    all_to_all x2, waiting for transfers between devices, exchange(): lax.all_to_all(message, AXES, split_axis=0, concat_axis=0, tiled=True)  7.64 us
    pallas_call x1, Pallas kernels, rows_call(): pl.pallas_call(rows_kernel, in_specs=[pl.BlockSpec(memory_space=pltpu.HBM...  6.68 us
    pallas_call x1, Pallas kernels, sample_call(): pl.pallas_call(sample_kernel, out_shape=shape((CHAN, WIDTH)), scratch_sha...  4.36 us
    ppermute x6, waiting for transfers between devices, shift(): return lax.ppermute(value, AXES, pairs)  4.3 us
    pallas_call x1, Pallas kernels, columns_call(): pl.pallas_call(columns_kernel, out_shape=shape((DEVICES * 12, 128), jnp.i...  4.03 us
    pallas_call x1, Pallas kernels, near_call(): pl.pallas_call(near_kernel, in_specs=[pl.BlockSpec(memory_space=pltpu.SME...  2.28 us
  transfers between devices with their start and end apart: 8, of which 4 were waited for; matrix products, arithmetic and copies ran while one was open for 1% of the time, Pallas kernels for 16%

profile of v5, /device:TPU:1, one launch (start us, length us, event | category | flops | bytes accessed | tf_op | source)
XLA Modules:
  0.0 65.6 jit_solution(15556367360444784024)
XLA Ops:
  0.0 6.7 %shard_map.127 = s32[1536,128]{1,0:T(8,128)} custom-call(bf16[12,4,2048]{2,1,0:T(4,128)(2,1)} %bitcast.21, f32[1,2048]{1,0:T(1,128)} %bitcast.23, s32[1,2048]{1,0:T(1,128)} %bitcast.25, bf16[640,256]{1,0:T(8,128)(2,1)} %constant.22.clone.table_hbm.table_ref), custom_call_target="tpu_custom_call" | custom-call | flops 3800000000 | bytes 4194304 | tf_op jit(solution)/shard_map/pallas_call | solution.py:547
  6.7 0.0 copy-start
  6.7 0.0 copy-start.1
  6.7 11.5 %all-to-all-start = ((s32[384,4,128]{2,1,0:T(4,128)}), s32[384,4,128]{2,1,0:T(4,128)S(1)}, u32[]{:S(2)}, u32[]{:S(2)}) async-start(s32[384,4,128]{2,1,0:T(4,128)} %bitcast.27), calls=%async_computation | async-start | bytes 1572864 | tf_op jit(solution)/shard_map/all_to_all | solution.py:628
  18.2 0.0 copy-done
  18.3 0.0 copy-done.1
  18.3 0.0 copy-start.10
  18.3 0.1 shard_map.130
  18.4 1.3 %collective-permute-start = (bf16[64,512]{1,0:T(8,128)(2,1)S(1)}, bf16[64,512]{1,0:T(8,128)(2,1)S(1)}, u32[]{:S(2)}, u32[]{:S(2)}) collective-permute-start(bf16[64,512]{1,0:T(8,128)(2,1)S(1)} %get-tuple-element.15), channel_id=1, source_target_pairs={{8,1},{9,2},{10,3},{11,4},{12,5},{13,6},{14,7},{15,0},{16,9},{17,1... | collective-permute-start | bytes 196616 | tf_op jit(solution)/shard_map/ppermute | solution.py:521
  19.7 5.5 %collective-permute-start.2 = (bf16[64,128]{1,0:T(8,128)(2,1)S(1)}, bf16[64,128]{1,0:T(8,128)(2,1)S(1)}, u32[]{:S(2)}, u32[]{:S(2)}) collective-permute-start(bf16[64,128]{1,0:T(8,128)(2,1)S(1)} %get-tuple-element.16), channel_id=1, source_target_pairs={{0,9},{1,10},{2,11},{3,12},{4,13},{5,14},{6,15},{7,8},{8,17},{9,18... | collective-permute-start | bytes 49160 | tf_op jit(solution)/shard_map/ppermute | solution.py:521
  25.2 0.0 copy-done.10
  25.2 0.1 broadcast_in_dim.2
  25.3 0.2 reshape.46
  25.5 0.0 copy-start.11
  25.5 0.0 copy-start.4
  25.5 0.0 copy-start.7
  25.5 0.2 copy.17.kern_ref
  25.7 0.0 copy-start.6
  26.5 0.0 copy-done.11
  26.5 0.1 copy.18
  26.5 0.1 reshape.49
  26.6 0.1 pad_add_fusion.list_ref
  26.7 2.3 %collective-permute-done.side_ref = bf16[64,512]{1,0:T(8,128)(2,1)S(1)} collective-permute-done((bf16[64,512]{1,0:T(8,128)(2,1)S(1)}, bf16[64,512]{1,0:T(8,128)(2,1)S(1)}, u32[]{:S(2)}, u32[]{:S(2)}) %collective-permute-start) | collective-permute-done | bytes 65568 | tf_op jit(solution)/shard_map/ppermute | solution.py:521
  29.1 2.9 %collective-permute-start.1 = (bf16[64,1024]{1,0:T(8,128)(2,1)S(1)}, bf16[64,1024]{1,0:T(8,128)(2,1)S(1)}, u32[]{:S(2)}, u32[]{:S(2)}) collective-permute-start(bf16[64,1024]{1,0:T(8,128)(2,1)S(1)} %pad_maximum_fusion), channel_id=1, source_target_pairs={{0,7},{1,0},{2,1},{3,2},{4,3},{5,4},{6,5},{7,6},{8,15},{9,8},{10,9... | collective-permute-start | bytes 393224 | tf_op jit(solution)/shard_map/ppermute | solution.py:521
  32.0 2.7 %all-to-all-done = s32[384,4,128]{2,1,0:T(4,128)S(1)} async-done(((s32[384,4,128]{2,1,0:T(4,128)}), s32[384,4,128]{2,1,0:T(4,128)S(1)}, u32[]{:S(2)}, u32[]{:S(2)}) %all-to-all-start) | async-done | bytes 786464 | tf_op jit(solution)/shard_map/all_to_all | solution.py:628
  34.7 0.0 copy-done.4
  34.7 0.0 copy-done.7
  34.7 0.0 copy-done.6
  34.7 0.0 copy-done.9
  34.7 4.0 %shard_map.128 = s32[1536,128]{1,0:T(8,128)} custom-call(s32[1536,128]{1,0:T(8,128)S(1)} %bitcast.19, f32[2,512,128]{2,1,0:T(8,128)S(1)} %copy.17.kern_ref, bf16[2,256,256]{2,1,0:T(8,128)(2,1)S(1)} %copy-done.6, bf16[2,256,256]{2,1,0:T(8,128)(2,1)S(1)} %copy-done.7, f32[2,512,128]{2,1,0:T(8,128)S(1)} %copy-done.4, f32[16,128]{1,0:T(8,128)S(1)} %copy-done.9), custom_call_target="tpu_custom_call" | custom-call | flops 2000000000 | bytes 6291456 | tf_op jit(solution)/shard_map/pallas_call | solution.py:591
  38.8 5.1 %all-to-all-start.1 = ((s32[384,4,128]{2,1,0:T(4,128)}), s32[384,4,128]{2,1,0:T(4,128)S(1)}, u32[]{:S(2)}, u32[]{:S(2)}) async-start(s32[384,4,128]{2,1,0:T(4,128)} %bitcast.8), calls=%async_computation.1 | async-start | bytes 1572864 | tf_op jit(solution)/shard_map/all_to_all | solution.py:628
  43.9 0.0 collective-permute-done.2.four_ref
  43.9 0.0 collective-permute-done.1.both_ref
  43.9 0.0 copy-done.8
  43.9 0.0 copy-start.5
  44.0 2.3 %shard_map.131 = (f32[48,2048]{1,0:T(8,128)S(1)}, bf16[48,512]{1,0:T(8,128)(2,1)S(1)}, bf16[48,640]{1,0:T(8,128)(2,1)S(1)}, bf16[48,128]{1,0:T(8,128)(2,1)S(1)}) custom-call(s32[27]{0:T(128)S(1)} %pad_add_fusion.list_ref, bf16[64,2048]{1,0:T(8,128)(2,1)S(1)} %get-tuple-element.13.own_ref, bf16[64,1024]{1,0:T(8,128)(2,1)S(1)} %collective-permute-done.1.both_ref, ...), custom_call_target="tpu_custom_call" | custom-call | flops 8000000000 | bytes 4194304 | tf_op jit(solution)/shard_map/pallas_call | solution.py:571
  46.2 3.5 %collective-permute-start.3 = (bf16[48,640]{1,0:T(8,128)(2,1)S(1)}, bf16[48,640]{1,0:T(8,128)(2,1)S(1)}, u32[]{:S(2)}, u32[]{:S(2)}) collective-permute-start(bf16[48,640]{1,0:T(8,128)(2,1)S(1)} %get-tuple-element.19), channel_id=1, source_target_pairs={{0,15},{1,8},{2,9},{3,10},{4,11},{5,12},{6,13},{7,14},{8,23},{9,16... | collective-permute-start | bytes 184328 | tf_op jit(solution)/shard_map/ppermute | solution.py:521
  49.8 1.5 %collective-permute-start.5 = (bf16[48,128]{1,0:T(8,128)(2,1)S(1)}, bf16[48,128]{1,0:T(8,128)(2,1)S(1)}, u32[]{:S(2)}, u32[]{:S(2)}) collective-permute-start(bf16[48,128]{1,0:T(8,128)(2,1)S(1)} %get-tuple-element.20), channel_id=1, source_target_pairs={{8,7},{9,0},{10,1},{11,2},{12,3},{13,4},{14,5},{15,6},{16,15},{17,... | collective-permute-start | bytes 36872 | tf_op jit(solution)/shard_map/ppermute | solution.py:521
  51.3 1.9 %collective-permute-done.3.side_ref = bf16[48,640]{1,0:T(8,128)(2,1)S(1)} collective-permute-done((bf16[48,640]{1,0:T(8,128)(2,1)S(1)}, bf16[48,640]{1,0:T(8,128)(2,1)S(1)}, u32[]{:S(2)}, u32[]{:S(2)}) %collective-permute-start.3) | collective-permute-done | bytes 61472 | tf_op jit(solution)/shard_map/ppermute | solution.py:521
  53.3 2.2 %collective-permute-start.4 = (bf16[48,1024]{1,0:T(8,128)(2,1)S(1)}, bf16[48,1024]{1,0:T(8,128)(2,1)S(1)}, u32[]{:S(2)}, u32[]{:S(2)}) collective-permute-start(bf16[48,1024]{1,0:T(8,128)(2,1)S(1)} %pad_maximum_fusion.1), channel_id=1, source_target_pairs={{0,1},{1,2},{2,3},{3,4},{4,5},{5,6},{6,7},{7,0},{8,9},{9,10},{10,1... | collective-permute-start | bytes 294920 | tf_op jit(solution)/shard_map/ppermute | solution.py:521
  55.4 5.0 %all-to-all-done.1 = s32[384,4,128]{2,1,0:T(4,128)S(1)} async-done(((s32[384,4,128]{2,1,0:T(4,128)}), s32[384,4,128]{2,1,0:T(4,128)S(1)}, u32[]{:S(2)}, u32[]{:S(2)}) %all-to-all-start.1) | async-done | bytes 786464 | tf_op jit(solution)/shard_map/all_to_all | solution.py:628
  60.4 0.0 copy-done.5
  60.4 0.0 copy-done.2
  60.4 0.0 copy-done.3
  60.4 4.4 %shard_map.129.far_ref = f32[48,2048]{1,0:T(8,128)S(1)} custom-call(s32[1536,128]{1,0:T(8,128)S(1)} %bitcast.20, f32[1,2048]{1,0:T(1,128)S(1)} %bitcast.24, s32[1,2048]{1,0:T(1,128)S(1)} %bitcast.26, bf16[640,256]{1,0:T(8,128)(2,1)S(1)} %copy-done.5), custom_call_target="tpu_custom_call" | custom-call | flops 3800000000 | bytes 4194304 | tf_op jit(solution)/shard_map/pallas_call | solution.py:601
  64.8 0.0 collective-permute-done.5.four_ref
  64.8 0.0 collective-permute-done.4.both_ref
  64.8 0.8 %shard_map.132 = f32[12,4,2048]{2,1,0:T(4,128)} custom-call(f32[48,2048]{1,0:T(8,128)S(1)} %shard_map.129.far_ref, f32[48,2048]{1,0:T(8,128)S(1)} %get-tuple-element.17.near_ref, bf16[48,1024]{1,0:T(8,128)(2,1)S(1)} %collective-permute-done.4.both_ref, bf16[48,640]{1,0:T(8,128)(2,1)S(1)} %collective-permute-done.3.side_ref, ...), custom_call_target="tpu_custom_call" | custom-call | flops 1000000 | bytes 2097152 | tf_op jit(solution)/shard_map/pallas_call | solution.py:617
  (8 shorter events, 0.0 us)
Async XLA Ops:
  6.7 11.6 %copy-start = (bf16[2,4,6,2048]{3,1,2,0:T(4,128)(2,1)S(1)}, bf16[2,4,6,2048]{3,1,2,0:T(4,128)(2,1)}, u32[]{:S(2)}) copy-start(bf16[2,4,6,2048]{3,1,2,0:T(4,128)(2,1)} %param.13) | copy-start | bytes 589828
  6.7 11.6 %copy-start.1 = (bf16[2,2048]{1,0:T(2,128)(2,1)S(1)}, bf16[2,2048]{1,0:T(2,128)(2,1)}, u32[]{:S(2)}) copy-start(bf16[2,2048]{1,0:T(2,128)(2,1)} %jitter_ref.1) | copy-start | bytes 24580
  6.7 28.0 %all-to-all-start = ((s32[384,4,128]{2,1,0:T(4,128)}), s32[384,4,128]{2,1,0:T(4,128)S(1)}, u32[]{:S(2)}, u32[]{:S(2)}) async-start(s32[384,4,128]{2,1,0:T(4,128)} %bitcast.27), calls=%async_computation | async-start | bytes 1572864 | tf_op jit(solution)/shard_map/all_to_all | solution.py:628
  18.3 6.9 %copy-start.10 = (f32[2,1024,8]{1,2,0:T(8,128)S(1)}, f32[2,1024,8]{1,2,0:T(8,128)}, u32[]{:S(2)}) copy-start(f32[2,1024,8]{1,2,0:T(8,128)} %param.19) | copy-start | bytes 196612
  18.4 10.7 %collective-permute-start = (bf16[64,512]{1,0:T(8,128)(2,1)S(1)}, bf16[64,512]{1,0:T(8,128)(2,1)S(1)}, u32[]{:S(2)}, u32[]{:S(2)}) collective-permute-start(bf16[64,512]{1,0:T(8,128)(2,1)S(1)} %get-tuple-element.15), channel_id=1, source_target_pairs={{8,1},{9,2},{10,3},{11,4},{12,5},{13,6},{14,7},{15,0},{16,9},{17,1... | collective-permute-start | bytes 196616 | tf_op jit(solution)/shard_map/ppermute | solution.py:521
  19.7 24.2 %collective-permute-start.2 = (bf16[64,128]{1,0:T(8,128)(2,1)S(1)}, bf16[64,128]{1,0:T(8,128)(2,1)S(1)}, u32[]{:S(2)}, u32[]{:S(2)}) collective-permute-start(bf16[64,128]{1,0:T(8,128)(2,1)S(1)} %get-tuple-element.16), channel_id=1, source_target_pairs={{0,9},{1,10},{2,11},{3,12},{4,13},{5,14},{6,15},{7,8},{8,17},{9,18... | collective-permute-start | bytes 49160 | tf_op jit(solution)/shard_map/ppermute | solution.py:521
  25.5 0.9 %copy-start.11 = (s32[1,8,3]{1,0,2:T(1,128)S(1)}, s32[1,8,3]{1,0,2:T(1,128)}, u32[]{:S(2)}) copy-start(s32[1,8,3]{1,0,2:T(1,128)} %param.17) | copy-start | bytes 292
  25.5 9.2 %copy-start.4 = (f32[2,512,128]{2,1,0:T(8,128)S(1)}, f32[2,512,128]{2,1,0:T(8,128)}, u32[]{:S(2)}) copy-start(f32[2,512,128]{2,1,0:T(8,128)} %constant.24.clone.tw_ref) | copy-start | bytes 1572868
  25.5 9.2 %copy-start.7 = (bf16[2,256,256]{2,1,0:T(8,128)(2,1)S(1)}, bf16[2,256,256]{2,1,0:T(8,128)(2,1)}, u32[]{:S(2)}) copy-start(bf16[2,256,256]{2,1,0:T(8,128)(2,1)} %constant.23.clone.inv_ref) | copy-start | bytes 786436
  25.7 9.0 %copy-start.6 = (bf16[2,256,256]{2,1,0:T(8,128)(2,1)S(1)}, bf16[2,256,256]{2,1,0:T(8,128)(2,1)}, u32[]{:S(2)}) copy-start(bf16[2,256,256]{2,1,0:T(8,128)(2,1)} %constant.21.clone.fwd_ref) | copy-start | bytes 786436
  29.1 5.7 %copy-start.9 = (f32[16,128]{1,0:T(8,128)S(1)}, f32[16,128]{1,0:T(8,128)}, u32[]{:S(2)}) copy-start(f32[16,128]{1,0:T(8,128)} %constant.25.clone.lane_ref) | copy-start | bytes 24580
  29.1 14.9 %collective-permute-start.1 = (bf16[64,1024]{1,0:T(8,128)(2,1)S(1)}, bf16[64,1024]{1,0:T(8,128)(2,1)S(1)}, u32[]{:S(2)}, u32[]{:S(2)}) collective-permute-start(bf16[64,1024]{1,0:T(8,128)(2,1)S(1)} %pad_maximum_fusion), channel_id=1, source_target_pairs={{0,7},{1,0},{2,1},{3,2},{4,3},{5,4},{6,5},{7,6},{8,15},{9,8},{10,9... | collective-permute-start | bytes 393224 | tf_op jit(solution)/shard_map/ppermute | solution.py:521
  38.8 5.2 %copy-start.8 = (bf16[576,48]{1,0:T(8,128)(2,1)S(1)}, bf16[576,48]{1,0:T(8,128)(2,1)}, u32[]{:S(2)}) copy-start(bf16[576,48]{1,0:T(8,128)(2,1)} %constant.26.clone.mix_ref) | copy-start | bytes 165892
  38.8 21.6 %all-to-all-start.1 = ((s32[384,4,128]{2,1,0:T(4,128)}), s32[384,4,128]{2,1,0:T(4,128)S(1)}, u32[]{:S(2)}, u32[]{:S(2)}) async-start(s32[384,4,128]{2,1,0:T(4,128)} %bitcast.8), calls=%async_computation.1 | async-start | bytes 1572864 | tf_op jit(solution)/shard_map/all_to_all | solution.py:628
  43.9 16.4 %copy-start.5 = (bf16[640,256]{1,0:T(8,128)(2,1)S(1)}, bf16[640,256]{1,0:T(8,128)(2,1)}, u32[]{:S(2)}) copy-start(bf16[640,256]{1,0:T(8,128)(2,1)} %constant.22.clone.table_hbm.table_ref) | copy-start | bytes 983044
  46.2 7.0 %collective-permute-start.3 = (bf16[48,640]{1,0:T(8,128)(2,1)S(1)}, bf16[48,640]{1,0:T(8,128)(2,1)S(1)}, u32[]{:S(2)}, u32[]{:S(2)}) collective-permute-start(bf16[48,640]{1,0:T(8,128)(2,1)S(1)} %get-tuple-element.19), channel_id=1, source_target_pairs={{0,15},{1,8},{2,9},{3,10},{4,11},{5,12},{6,13},{7,14},{8,23},{9,16... | collective-permute-start | bytes 184328 | tf_op jit(solution)/shard_map/ppermute | solution.py:521
  49.8 15.0 %collective-permute-start.5 = (bf16[48,128]{1,0:T(8,128)(2,1)S(1)}, bf16[48,128]{1,0:T(8,128)(2,1)S(1)}, u32[]{:S(2)}, u32[]{:S(2)}) collective-permute-start(bf16[48,128]{1,0:T(8,128)(2,1)S(1)} %get-tuple-element.20), channel_id=1, source_target_pairs={{8,7},{9,0},{10,1},{11,2},{12,3},{13,4},{14,5},{15,6},{16,15},{17,... | collective-permute-start | bytes 36872 | tf_op jit(solution)/shard_map/ppermute | solution.py:521
  53.2 7.2 %copy-start.2 = (f32[2048]{0:T(1024)S(1)}, f32[2048]{0:T(1024)}, u32[]{:S(2)}) copy-start(f32[2048]{0:T(1024)} %param.15) | copy-start | bytes 24580
  53.2 7.2 %copy-start.3 = (s32[2048]{0:T(1024)S(1)}, s32[2048]{0:T(1024)}, u32[]{:S(2)}) copy-start(s32[2048]{0:T(1024)} %param.16) | copy-start | bytes 24580
  53.3 11.5 %collective-permute-start.4 = (bf16[48,1024]{1,0:T(8,128)(2,1)S(1)}, bf16[48,1024]{1,0:T(8,128)(2,1)S(1)}, u32[]{:S(2)}, u32[]{:S(2)}) collective-permute-start(bf16[48,1024]{1,0:T(8,128)(2,1)S(1)} %pad_maximum_fusion.1), channel_id=1, source_target_pairs={{0,1},{1,2},{2,3},{3,4},{4,5},{5,6},{6,7},{7,0},{8,9},{9,10},{10,1... | collective-permute-start | bytes 294920 | tf_op jit(solution)/shard_map/ppermute | solution.py:521

commit v6 on v5

--- a/solution.py
+++ b/solution.py
@@ -318,16 +318,18 @@
     gather(2)
 
 
-def sample_kernel(
-    r_ref, w_ref, cell_ref, table_ref, sum_ref, v_ref, g_ref, grid_ref, hot_ref, tw_ref
-):
-    tw_ref[...] = twiddles(table_ref)
-    upper = cell_ref[...] >> 8
+def place_kernel(cell_ref, hot_ref):
     for block in range(16):
         place = lax.broadcasted_iota(jnp.int32, (16, WIDTH), 0) + block * 16
         hit = place == (cell_ref[...] & 255)
         hot_ref[block * 16 : block * 16 + 16, :] = jnp.where(hit, 1.0, 0.0).astype(BF16)
 
+
+def sample_kernel(
+    r_ref, w_ref, cell_ref, table_ref, hot_ref, sum_ref, v_ref, g_ref, grid_ref, tw_ref
+):
+    tw_ref[...] = twiddles(table_ref)
+    upper = cell_ref[...] >> 8
     def spread(m):
         for group in range(m * 3, m * 3 + 3):
             real, imag = unpacked(r_ref[pl.ds(group, 128, 12), :])
@@ -597,7 +599,16 @@
     )(columns, transfer, forward, backward, column_table, lane_table)
 
 
-def sample_call(rows, w, cell, table):
+def place_call(cell):
+    return pl.pallas_call(
+        place_kernel,
+        out_shape=shape((256, WIDTH), BF16),
+        compiler_params=PARAMS,
+        cost_estimate=cost(500_000_000, MIB),
+    )(cell)
+
+
+def sample_call(rows, w, cell, table, hot):
     return pl.pallas_call(
         sample_kernel,
         out_shape=shape((CHAN, WIDTH)),
@@ -605,12 +616,11 @@
             pltpu.VMEM((1536, 256), F32),
             pltpu.VMEM((1536, 256), F32),
             pltpu.VMEM((1536, 256), F32),
-            pltpu.VMEM((256, WIDTH), BF16),
             pltpu.VMEM((128, 128), F32),
         ],
         compiler_params=PARAMS,
         cost_estimate=cost(3_800_000_000, 4 * MIB),
-    )(rows, w, cell, table)
+    )(rows, w, cell, table, hot)
 
 
 def finish_call(far, near, both, side, four):
@@ -667,7 +677,7 @@
     side = shift(side, 1, -1)
     four = shift(four, -1, -1)
     both = shift(jnp.concatenate([one, side[:, 0 : 4 * PIL]], axis=1), 0, 1)
-    far = sample_call(rows, w, cell, table)
+    far = sample_call(rows, w, cell, table, place_call(cell))
     coupled = finish_call(far, near, both, side, four)
     return coupled.reshape(2, 6, ANG, WIDTH).transpose(0, 2, 1, 3)
 

time: 66.1 us -> 66.1 us (level)
    all_to_all x2, waiting for transfers between devices: 7.64 us -> 6.8 us  [exchange(): lax.all_to_all(message, AXES, split_axis=0, concat_axis=0, tiled=True)]
  transfers between devices with their start and end apart: 8 -> 8, of which waited for: 4 -> 4; matrix products, arithmetic and copies ran while one was open for 1% -> 1% of each run, Pallas kernels for 16% -> 17%
where the time goes in v6:
time: 66.1 us; the launch traced here: 65.7 us
  starting transfers between devices  34 us (51%)
  Pallas kernels  18.5 us (28%)
  waiting for transfers between devices  11.3 us (17%)
  between operations  0.99 us (1%)
  local copies, waits for them, and re-layouts  0.73 us (1%)
    ppermute x6, starting transfers between devices, shift(): return lax.ppermute(value, AXES, pairs)  17.3 us
    all_to_all x2, starting transfers between devices, exchange(): lax.all_to_all(message, AXES, split_axis=0, concat_axis=0, tiled=True)  16.7 us
    all_to_all x2, waiting for transfers between devices, exchange(): lax.all_to_all(message, AXES, split_axis=0, concat_axis=0, tiled=True)  6.8 us
    pallas_call x1, Pallas kernels, rows_call(): pl.pallas_call(rows_kernel, in_specs=[pl.BlockSpec(memory_space=pltpu.HBM...  6.68 us
    ppermute x6, waiting for transfers between devices, shift(): return lax.ppermute(value, AXES, pairs)  4.52 us
    pallas_call x1, Pallas kernels, sample_call(): pl.pallas_call(sample_kernel, out_shape=shape((CHAN, WIDTH)), scratch_sha...  4.41 us
    pallas_call x1, Pallas kernels, columns_call(): pl.pallas_call(columns_kernel, out_shape=shape((DEVICES * 12, 128), jnp.i...  4.03 us
    pallas_call x1, Pallas kernels, near_call(): pl.pallas_call(near_kernel, in_specs=[pl.BlockSpec(memory_space=pltpu.SME...  2.27 us
  transfers between devices with their start and end apart: 8, of which 4 were waited for; matrix products, arithmetic and copies ran while one was open for 1% of the time, Pallas kernels for 17%

profile of v6, /device:TPU:1, one launch (start us, length us, event | category | flops | bytes accessed | tf_op | source)
XLA Modules:
  0.0 65.7 jit_solution(10576946870439550174)
XLA Ops:
  0.0 6.7 %shard_map.127 = s32[1536,128]{1,0:T(8,128)} custom-call(bf16[12,4,2048]{2,1,0:T(4,128)(2,1)} %bitcast.21, f32[1,2048]{1,0:T(1,128)} %bitcast.23, s32[1,2048]{1,0:T(1,128)} %bitcast.25, bf16[640,256]{1,0:T(8,128)(2,1)} %constant.22.clone.table_hbm.table_ref), custom_call_target="tpu_custom_call" | custom-call | flops 3800000000 | bytes 4194304 | tf_op jit(solution)/shard_map/pallas_call | solution.py:549
  6.7 0.0 copy-start
  6.7 0.0 copy-start.1
  6.7 11.5 %all-to-all-start = ((s32[384,4,128]{2,1,0:T(4,128)}), s32[384,4,128]{2,1,0:T(4,128)S(1)}, u32[]{:S(2)}, u32[]{:S(2)}) async-start(s32[384,4,128]{2,1,0:T(4,128)} %bitcast.28), calls=%async_computation | async-start | bytes 1572864 | tf_op jit(solution)/shard_map/all_to_all | solution.py:638
  18.2 0.0 copy-done
  18.3 0.0 copy-done.1
  18.3 0.0 copy-start.10
  18.3 0.1 shard_map.131
  18.4 1.3 %collective-permute-start = (bf16[64,512]{1,0:T(8,128)(2,1)S(1)}, bf16[64,512]{1,0:T(8,128)(2,1)S(1)}, u32[]{:S(2)}, u32[]{:S(2)}) collective-permute-start(bf16[64,512]{1,0:T(8,128)(2,1)S(1)} %get-tuple-element.15), channel_id=1, source_target_pairs={{8,1},{9,2},{10,3},{11,4},{12,5},{13,6},{14,7},{15,0},{16,9},{17,1... | collective-permute-start | bytes 196616 | tf_op jit(solution)/shard_map/ppermute | solution.py:523
  19.7 5.5 %collective-permute-start.2 = (bf16[64,128]{1,0:T(8,128)(2,1)S(1)}, bf16[64,128]{1,0:T(8,128)(2,1)S(1)}, u32[]{:S(2)}, u32[]{:S(2)}) collective-permute-start(bf16[64,128]{1,0:T(8,128)(2,1)S(1)} %get-tuple-element.16), channel_id=1, source_target_pairs={{0,9},{1,10},{2,11},{3,12},{4,13},{5,14},{6,15},{7,8},{8,17},{9,18... | collective-permute-start | bytes 49160 | tf_op jit(solution)/shard_map/ppermute | solution.py:523
  25.2 0.0 copy-done.10
  25.2 0.1 broadcast_in_dim.2
  25.3 0.2 reshape.46
  25.5 0.0 copy-start.11
  25.5 0.0 copy-start.4
  25.5 0.0 copy-start.7
  25.5 0.2 copy.17.kern_ref
  25.7 0.0 copy-start.6
  26.5 0.0 copy-done.11
  26.5 0.1 copy.18
  26.5 0.1 reshape.49
  26.6 0.1 pad_add_fusion.list_ref
  26.7 2.3 %collective-permute-done.side_ref = bf16[64,512]{1,0:T(8,128)(2,1)S(1)} collective-permute-done((bf16[64,512]{1,0:T(8,128)(2,1)S(1)}, bf16[64,512]{1,0:T(8,128)(2,1)S(1)}, u32[]{:S(2)}, u32[]{:S(2)}) %collective-permute-start) | collective-permute-done | bytes 65568 | tf_op jit(solution)/shard_map/ppermute | solution.py:523
  29.1 2.9 %collective-permute-start.1 = (bf16[64,1024]{1,0:T(8,128)(2,1)S(1)}, bf16[64,1024]{1,0:T(8,128)(2,1)S(1)}, u32[]{:S(2)}, u32[]{:S(2)}) collective-permute-start(bf16[64,1024]{1,0:T(8,128)(2,1)S(1)} %pad_maximum_fusion), channel_id=1, source_target_pairs={{0,7},{1,0},{2,1},{3,2},{4,3},{5,4},{6,5},{7,6},{8,15},{9,8},{10,9... | collective-permute-start | bytes 393224 | tf_op jit(solution)/shard_map/ppermute | solution.py:523
  32.0 2.7 %all-to-all-done = s32[384,4,128]{2,1,0:T(4,128)S(1)} async-done(((s32[384,4,128]{2,1,0:T(4,128)}), s32[384,4,128]{2,1,0:T(4,128)S(1)}, u32[]{:S(2)}, u32[]{:S(2)}) %all-to-all-start) | async-done | bytes 786464 | tf_op jit(solution)/shard_map/all_to_all | solution.py:638
  34.7 0.0 copy-done.4
  34.7 0.0 copy-done.7
  34.7 0.0 copy-done.6
  34.7 0.0 copy-done.9
  34.7 4.0 %shard_map.128 = s32[1536,128]{1,0:T(8,128)} custom-call(s32[1536,128]{1,0:T(8,128)S(1)} %bitcast.19, f32[2,512,128]{2,1,0:T(8,128)S(1)} %copy.17.kern_ref, bf16[2,256,256]{2,1,0:T(8,128)(2,1)S(1)} %copy-done.6, bf16[2,256,256]{2,1,0:T(8,128)(2,1)S(1)} %copy-done.7, f32[2,512,128]{2,1,0:T(8,128)S(1)} %copy-done.4, f32[16,128]{1,0:T(8,128)S(1)} %copy-done.9), custom_call_target="tpu_custom_call" | custom-call | flops 2000000000 | bytes 6291456 | tf_op jit(solution)/shard_map/pallas_call | solution.py:593
  38.8 5.1 %all-to-all-start.1 = ((s32[384,4,128]{2,1,0:T(4,128)}), s32[384,4,128]{2,1,0:T(4,128)S(1)}, u32[]{:S(2)}, u32[]{:S(2)}) async-start(s32[384,4,128]{2,1,0:T(4,128)} %bitcast.8), calls=%async_computation.1 | async-start | bytes 1572864 | tf_op jit(solution)/shard_map/all_to_all | solution.py:638
  43.9 0.0 collective-permute-done.2.four_ref
  43.9 0.0 collective-permute-done.1.both_ref
  43.9 0.0 copy-start.3
  44.0 2.3 %shard_map.132 = (f32[48,2048]{1,0:T(8,128)S(1)}, bf16[48,512]{1,0:T(8,128)(2,1)S(1)}, bf16[48,640]{1,0:T(8,128)(2,1)S(1)}, bf16[48,128]{1,0:T(8,128)(2,1)S(1)}) custom-call(s32[27]{0:T(128)S(1)} %pad_add_fusion.list_ref, bf16[64,2048]{1,0:T(8,128)(2,1)S(1)} %get-tuple-element.13.own_ref, bf16[64,1024]{1,0:T(8,128)(2,1)S(1)} %collective-permute-done.1.both_ref, ...), custom_call_target="tpu_custom_call" | custom-call | flops 8000000000 | bytes 4194304 | tf_op jit(solution)/shard_map/pallas_call | solution.py:573
  46.2 0.0 copy-start.5
  46.2 3.7 %collective-permute-start.3 = (bf16[48,640]{1,0:T(8,128)(2,1)S(1)}, bf16[48,640]{1,0:T(8,128)(2,1)S(1)}, u32[]{:S(2)}, u32[]{:S(2)}) collective-permute-start(bf16[48,640]{1,0:T(8,128)(2,1)S(1)} %get-tuple-element.19), channel_id=1, source_target_pairs={{0,15},{1,8},{2,9},{3,10},{4,11},{5,12},{6,13},{7,14},{8,23},{9,16... | collective-permute-start | bytes 184328 | tf_op jit(solution)/shard_map/ppermute | solution.py:523
  49.9 0.0 copy-done.3
  49.9 0.2 shard_map.129.hot_ref
  50.1 1.5 %collective-permute-start.5 = (bf16[48,128]{1,0:T(8,128)(2,1)S(1)}, bf16[48,128]{1,0:T(8,128)(2,1)S(1)}, u32[]{:S(2)}, u32[]{:S(2)}) collective-permute-start(bf16[48,128]{1,0:T(8,128)(2,1)S(1)} %get-tuple-element.20), channel_id=1, source_target_pairs={{8,7},{9,0},{10,1},{11,2},{12,3},{13,4},{14,5},{15,6},{16,15},{17,... | collective-permute-start | bytes 36872 | tf_op jit(solution)/shard_map/ppermute | solution.py:523
  51.6 2.2 %collective-permute-done.3.side_ref = bf16[48,640]{1,0:T(8,128)(2,1)S(1)} collective-permute-done((bf16[48,640]{1,0:T(8,128)(2,1)S(1)}, bf16[48,640]{1,0:T(8,128)(2,1)S(1)}, u32[]{:S(2)}, u32[]{:S(2)}) %collective-permute-start.3) | collective-permute-done | bytes 61472 | tf_op jit(solution)/shard_map/ppermute | solution.py:523
  53.8 2.5 %collective-permute-start.4 = (bf16[48,1024]{1,0:T(8,128)(2,1)S(1)}, bf16[48,1024]{1,0:T(8,128)(2,1)S(1)}, u32[]{:S(2)}, u32[]{:S(2)}) collective-permute-start(bf16[48,1024]{1,0:T(8,128)(2,1)S(1)} %pad_maximum_fusion.1), channel_id=1, source_target_pairs={{0,1},{1,2},{2,3},{3,4},{4,5},{5,6},{6,7},{7,0},{8,9},{9,10},{10,1... | collective-permute-start | bytes 294920 | tf_op jit(solution)/shard_map/ppermute | solution.py:523
  56.3 4.1 %all-to-all-done.1 = s32[384,4,128]{2,1,0:T(4,128)S(1)} async-done(((s32[384,4,128]{2,1,0:T(4,128)}), s32[384,4,128]{2,1,0:T(4,128)S(1)}, u32[]{:S(2)}, u32[]{:S(2)}) %all-to-all-start.1) | async-done | bytes 786464 | tf_op jit(solution)/shard_map/all_to_all | solution.py:638
  60.4 0.0 copy-done.5
  60.4 4.4 %shard_map.130.far_ref = f32[48,2048]{1,0:T(8,128)S(1)} custom-call(s32[1536,128]{1,0:T(8,128)S(1)} %bitcast.20, f32[1,2048]{1,0:T(1,128)S(1)} %bitcast.24, s32[1,2048]{1,0:T(1,128)S(1)} %bitcast.27, bf16[640,256]{1,0:T(8,128)(2,1)S(1)} %copy-done.5, bf16[256,2048]{1,0:T(8,128)(2,1)S(1)} %shard_map.129.hot_ref), custom_call_target="tpu_custom_call" | custom-call | flops 3800000000 | bytes 4194304 | tf_op jit(solution)/shard_map/pallas_call | solution.py:612
  64.8 0.0 collective-permute-done.5.four_ref
  64.8 0.0 collective-permute-done.4.both_ref
  64.8 0.8 %shard_map.133 = f32[12,4,2048]{2,1,0:T(4,128)} custom-call(f32[48,2048]{1,0:T(8,128)S(1)} %shard_map.130.far_ref, f32[48,2048]{1,0:T(8,128)S(1)} %get-tuple-element.17.near_ref, bf16[48,1024]{1,0:T(8,128)(2,1)S(1)} %collective-permute-done.4.both_ref, bf16[48,640]{1,0:T(8,128)(2,1)S(1)} %collective-permute-done.3.side_ref, ...), custom_call_target="tpu_custom_call" | custom-call | flops 1000000 | bytes 2097152 | tf_op jit(solution)/shard_map/pallas_call | solution.py:627
  (9 shorter events, 0.0 us)
Async XLA Ops:
  6.7 11.6 %copy-start = (bf16[2,4,6,2048]{3,1,2,0:T(4,128)(2,1)S(1)}, bf16[2,4,6,2048]{3,1,2,0:T(4,128)(2,1)}, u32[]{:S(2)}) copy-start(bf16[2,4,6,2048]{3,1,2,0:T(4,128)(2,1)} %param.13) | copy-start | bytes 589828
  6.7 11.6 %copy-start.1 = (bf16[2,2048]{1,0:T(2,128)(2,1)S(1)}, bf16[2,2048]{1,0:T(2,128)(2,1)}, u32[]{:S(2)}) copy-start(bf16[2,2048]{1,0:T(2,128)(2,1)} %jitter_ref.1) | copy-start | bytes 24580
  6.7 28.0 %all-to-all-start = ((s32[384,4,128]{2,1,0:T(4,128)}), s32[384,4,128]{2,1,0:T(4,128)S(1)}, u32[]{:S(2)}, u32[]{:S(2)}) async-start(s32[384,4,128]{2,1,0:T(4,128)} %bitcast.28), calls=%async_computation | async-start | bytes 1572864 | tf_op jit(solution)/shard_map/all_to_all | solution.py:638
  18.3 6.9 %copy-start.10 = (f32[2,1024,8]{1,2,0:T(8,128)S(1)}, f32[2,1024,8]{1,2,0:T(8,128)}, u32[]{:S(2)}) copy-start(f32[2,1024,8]{1,2,0:T(8,128)} %param.19) | copy-start | bytes 196612
  18.4 10.7 %collective-permute-start = (bf16[64,512]{1,0:T(8,128)(2,1)S(1)}, bf16[64,512]{1,0:T(8,128)(2,1)S(1)}, u32[]{:S(2)}, u32[]{:S(2)}) collective-permute-start(bf16[64,512]{1,0:T(8,128)(2,1)S(1)} %get-tuple-element.15), channel_id=1, source_target_pairs={{8,1},{9,2},{10,3},{11,4},{12,5},{13,6},{14,7},{15,0},{16,9},{17,1... | collective-permute-start | bytes 196616 | tf_op jit(solution)/shard_map/ppermute | solution.py:523
  19.7 24.2 %collective-permute-start.2 = (bf16[64,128]{1,0:T(8,128)(2,1)S(1)}, bf16[64,128]{1,0:T(8,128)(2,1)S(1)}, u32[]{:S(2)}, u32[]{:S(2)}) collective-permute-start(bf16[64,128]{1,0:T(8,128)(2,1)S(1)} %get-tuple-element.16), channel_id=1, source_target_pairs={{0,9},{1,10},{2,11},{3,12},{4,13},{5,14},{6,15},{7,8},{8,17},{9,18... | collective-permute-start | bytes 49160 | tf_op jit(solution)/shard_map/ppermute | solution.py:523
  25.5 0.9 %copy-start.11 = (s32[1,8,3]{1,0,2:T(1,128)S(1)}, s32[1,8,3]{1,0,2:T(1,128)}, u32[]{:S(2)}) copy-start(s32[1,8,3]{1,0,2:T(1,128)} %param.17) | copy-start | bytes 292
  25.5 9.2 %copy-start.4 = (f32[2,512,128]{2,1,0:T(8,128)S(1)}, f32[2,512,128]{2,1,0:T(8,128)}, u32[]{:S(2)}) copy-start(f32[2,512,128]{2,1,0:T(8,128)} %constant.24.clone.tw_ref) | copy-start | bytes 1572868
  25.5 9.2 %copy-start.7 = (bf16[2,256,256]{2,1,0:T(8,128)(2,1)S(1)}, bf16[2,256,256]{2,1,0:T(8,128)(2,1)}, u32[]{:S(2)}) copy-start(bf16[2,256,256]{2,1,0:T(8,128)(2,1)} %constant.23.clone.inv_ref) | copy-start | bytes 786436
  25.7 9.0 %copy-start.6 = (bf16[2,256,256]{2,1,0:T(8,128)(2,1)S(1)}, bf16[2,256,256]{2,1,0:T(8,128)(2,1)}, u32[]{:S(2)}) copy-start(bf16[2,256,256]{2,1,0:T(8,128)(2,1)} %constant.21.clone.fwd_ref) | copy-start | bytes 786436
  29.1 5.7 %copy-start.9 = (f32[16,128]{1,0:T(8,128)S(1)}, f32[16,128]{1,0:T(8,128)}, u32[]{:S(2)}) copy-start(f32[16,128]{1,0:T(8,128)} %constant.25.clone.lane_ref) | copy-start | bytes 24580
  29.1 14.9 %collective-permute-start.1 = (bf16[64,1024]{1,0:T(8,128)(2,1)S(1)}, bf16[64,1024]{1,0:T(8,128)(2,1)S(1)}, u32[]{:S(2)}, u32[]{:S(2)}) collective-permute-start(bf16[64,1024]{1,0:T(8,128)(2,1)S(1)} %pad_maximum_fusion), channel_id=1, source_target_pairs={{0,7},{1,0},{2,1},{3,2},{4,3},{5,4},{6,5},{7,6},{8,15},{9,8},{10,9... | collective-permute-start | bytes 393224 | tf_op jit(solution)/shard_map/ppermute | solution.py:523
  38.8 5.2 %copy-start.8 = (bf16[576,48]{1,0:T(8,128)(2,1)S(1)}, bf16[576,48]{1,0:T(8,128)(2,1)}, u32[]{:S(2)}) copy-start(bf16[576,48]{1,0:T(8,128)(2,1)} %constant.26.clone.mix_ref) | copy-start | bytes 165892
  38.8 21.6 %all-to-all-start.1 = ((s32[384,4,128]{2,1,0:T(4,128)}), s32[384,4,128]{2,1,0:T(4,128)S(1)}, u32[]{:S(2)}, u32[]{:S(2)}) async-start(s32[384,4,128]{2,1,0:T(4,128)} %bitcast.8), calls=%async_computation.1 | async-start | bytes 1572864 | tf_op jit(solution)/shard_map/all_to_all | solution.py:638
  43.9 6.0 %copy-start.3 = (s32[2048]{0:T(1024)S(1)}, s32[2048]{0:T(1024)}, u32[]{:S(2)}) copy-start(s32[2048]{0:T(1024)} %param.16) | copy-start | bytes 24580
  46.2 14.1 %copy-start.5 = (bf16[640,256]{1,0:T(8,128)(2,1)S(1)}, bf16[640,256]{1,0:T(8,128)(2,1)}, u32[]{:S(2)}) copy-start(bf16[640,256]{1,0:T(8,128)(2,1)} %constant.22.clone.table_hbm.table_ref) | copy-start | bytes 983044
  46.2 7.5 %collective-permute-start.3 = (bf16[48,640]{1,0:T(8,128)(2,1)S(1)}, bf16[48,640]{1,0:T(8,128)(2,1)S(1)}, u32[]{:S(2)}, u32[]{:S(2)}) collective-permute-start(bf16[48,640]{1,0:T(8,128)(2,1)S(1)} %get-tuple-element.19), channel_id=1, source_target_pairs={{0,15},{1,8},{2,9},{3,10},{4,11},{5,12},{6,13},{7,14},{8,23},{9,16... | collective-permute-start | bytes 184328 | tf_op jit(solution)/shard_map/ppermute | solution.py:523
  50.1 14.7 %collective-permute-start.5 = (bf16[48,128]{1,0:T(8,128)(2,1)S(1)}, bf16[48,128]{1,0:T(8,128)(2,1)S(1)}, u32[]{:S(2)}, u32[]{:S(2)}) collective-permute-start(bf16[48,128]{1,0:T(8,128)(2,1)S(1)} %get-tuple-element.20), channel_id=1, source_target_pairs={{8,7},{9,0},{10,1},{11,2},{12,3},{13,4},{14,5},{15,6},{16,15},{17,... | collective-permute-start | bytes 36872 | tf_op jit(solution)/shard_map/ppermute | solution.py:523
  53.8 6.6 %copy-start.2 = (f32[2048]{0:T(1024)S(1)}, f32[2048]{0:T(1024)}, u32[]{:S(2)}) copy-start(f32[2048]{0:T(1024)} %param.15) | copy-start | bytes 24580
  53.8 11.0 %collective-permute-start.4 = (bf16[48,1024]{1,0:T(8,128)(2,1)S(1)}, bf16[48,1024]{1,0:T(8,128)(2,1)S(1)}, u32[]{:S(2)}, u32[]{:S(2)}) collective-permute-start(bf16[48,1024]{1,0:T(8,128)(2,1)S(1)} %pad_maximum_fusion.1), channel_id=1, source_target_pairs={{0,1},{1,2},{2,3},{3,4},{4,5},{5,6},{6,7},{7,0},{8,9},{9,10},{10,1... | collective-permute-start | bytes 294920 | tf_op jit(solution)/shard_map/ppermute | solution.py:523
